TPU v7x, 128 devices: a whole 4x4x4 slice. The times are simulated.
128 devices in a mesh: replica: 2 (over z_hi), fsdp: 64 (over x, z_lo, y, core).
Axes of the slice: x: 4, y: 4, z: 4 (z_hi: 2, z_lo: 2; z = z_hi * 2 + z_lo), core: 2. Of those that a mesh axis runs over, the one named last changes fastest.
Arguments:
- inputs: bfloat16 [2, 4096, 2048], P('replica', 'fsdp'), may hold values from -6 to 6
- cotangent: bfloat16 [2, 4096, 2048], P('replica', 'fsdp'), may hold values from -0.0014648438 to 0.0014648438
- params_in: float32 [2, 2, 2048, 8192], P('replica', None, None, 'fsdp'), may hold values from -0.125 to 0.125
- params_down: float32 [2, 8192, 2048], P('replica', 'fsdp'), may hold values from -0.0625 to 0.0625
- first_in: bfloat16 [2, 2, 2048, 8192], P('replica', None, None, 'fsdp'), may hold values from -0.017944336 to 0.017944336
- first_down: bfloat16 [2, 8192, 2048], P('replica', 'fsdp'), may hold values from -0.017944336 to 0.017944336
- second_in: bfloat16 [2, 2, 2048, 8192], P('replica', None, None, 'fsdp'), may hold values from 9.983778e-07 to 9.9658966e-05
- second_down: bfloat16 [2, 8192, 2048], P('replica', 'fsdp'), may hold values from 9.983778e-07 to 9.9658966e-05
- base_in: float32 [2, 2048, 8192], P(None, None, 'fsdp'), may hold values from -0.125 to 0.125
- base_down: float32 [8192, 2048], P('fsdp'), may hold values from -0.0625 to 0.0625
- outer_in: float32 [2, 2048, 8192], P(None, None, 'fsdp'), may hold values from -0.06 to 0.06
- outer_down: float32 [8192, 2048], P('fsdp'), may hold values from -0.06 to 0.06
Outputs:
- new_base_in: float32 [2, 2048, 8192], P(None, None, 'fsdp')
- new_base_down: float32 [8192, 2048], P('fsdp')
- new_outer_in: float32 [2, 2048, 8192], P(None, None, 'fsdp')
- new_outer_down: float32 [8192, 2048], P('fsdp')
- new_first_in: bfloat16 [2, 2, 2048, 8192], P('replica', None, None, 'fsdp')
- new_first_down: bfloat16 [2, 8192, 2048], P('replica', 'fsdp')
- new_second_in: bfloat16 [2, 2, 2048, 8192], P('replica', None, None, 'fsdp')
- new_second_down: bfloat16 [2, 8192, 2048], P('replica', 'fsdp')
All inputs are finite; a program needn't handle non-finite values.
Results may differ from a plain program's by a relative error of at most 0.0055.
Values may be sent and summed in bfloat16 or wider, within the bound.
No kernel may reach another device: no remote copies, remote signals or barrier semaphores. Data moves between devices by JAX's collectives and lax.ppermute only.
A program may use at most 128 MiB of HBM per device.

v0:
```python
import jax
import jax.numpy as jnp
from jax import lax
from jax.sharding import PartitionSpec as P

beta_one = 0.9
beta_two = 0.95
bias_one = 1.0 - 0.9**64
bias_two = 1.0 - 0.95**64
inner_rate = 0.004
decay_rate = 0.1
epsilon_adam = 1e-08
momentum_keep = 0.9
outer_rate = 0.7


def contract_rows(left, right):
    return lax.dot_general(
        left, right, (((0,), (0,)), ((), ())), preferred_element_type=jnp.float32
    )


def forward(rows_in, weights_in, weights_down):
    gate_w = weights_in[0].astype(jnp.bfloat16)
    up_w = weights_in[1].astype(jnp.bfloat16)
    down_w = weights_down.astype(jnp.bfloat16)
    gate_pre = jnp.dot(rows_in, gate_w, preferred_element_type=jnp.float32)
    up_proj = jnp.dot(rows_in, up_w, preferred_element_type=jnp.float32)
    sigmoid_gate = jax.nn.sigmoid(gate_pre)
    silu_gate = gate_pre * sigmoid_gate
    hidden = (silu_gate * up_proj).astype(jnp.bfloat16)
    return (gate_pre, up_proj, sigmoid_gate, silu_gate, hidden, down_w)


def backward(rows_in, rows_cot, saved):
    gate_pre, up_proj, sigmoid_gate, silu_gate, hidden, down_w = saved
    grad_down = contract_rows(hidden, rows_cot)
    dhidden = lax.dot_general(
        rows_cot, down_w, (((1,), (1,)), ((), ())), preferred_element_type=jnp.float32
    )
    dgate = (dhidden * up_proj * (sigmoid_gate * (1.0 + gate_pre * (1.0 - sigmoid_gate)))).astype(
        jnp.bfloat16
    )
    dup = (dhidden * silu_gate).astype(jnp.bfloat16)
    grad_in = jnp.stack([contract_rows(rows_in, dgate), contract_rows(rows_in, dup)])
    return (grad_in, grad_down)


def adamw(param, grad, first, second):
    first_new = beta_one * first.astype(jnp.float32) + (1.0 - beta_one) * grad
    second_new = beta_two * second.astype(jnp.float32) + (1.0 - beta_two) * grad * grad
    update = first_new / bias_one / (jnp.sqrt(second_new / bias_two) + epsilon_adam)
    param_new = param - inner_rate * (update + decay_rate * param)
    return (param_new, first_new.astype(jnp.bfloat16), second_new.astype(jnp.bfloat16))


def outer_step(total, count, base, outer):
    grad_outer = total / count
    new_outer = momentum_keep * outer + grad_outer
    new_base = base - outer_rate * (grad_outer + momentum_keep * new_outer)
    return (new_base, new_outer)


def local(
    inputs,
    cotangent,
    params_in,
    params_down,
    first_in,
    first_down,
    second_in,
    second_down,
    base_in,
    base_down,
    outer_in,
    outer_down,
):
    rows_in = lax.all_gather(inputs, "fsdp", axis=1, tiled=True)
    saved = forward(rows_in[0], params_in[0], params_down[0])
    rows_cot = lax.all_gather(cotangent, "fsdp", axis=1, tiled=True)
    grad_in, grad_down = backward(rows_in[0], rows_cot[0], saved)
    new_in, fin, sin = adamw(params_in[0], grad_in, first_in[0], second_in[0])
    new_down, fdown, sdown = adamw(params_down[0], grad_down, first_down[0], second_down[0])
    delta_in = base_in - new_in
    delta_down = base_down - new_down
    count = lax.axis_size("replica")
    total_in, total_down = lax.psum((delta_in, delta_down), "replica")
    new_base_in, new_outer_in = outer_step(total_in, count, base_in, outer_in)
    new_base_down, new_outer_down = outer_step(total_down, count, base_down, outer_down)
    return (
        new_base_in,
        new_base_down,
        new_outer_in,
        new_outer_down,
        fin[None],
        fdown[None],
        sin[None],
        sdown[None],
    )


def solution(mesh):
    in_specs = (
        P("replica", "fsdp", None),
        P("replica", "fsdp", None),
        P("replica", None, None, "fsdp"),
        P("replica", "fsdp", None),
        P("replica", None, None, "fsdp"),
        P("replica", "fsdp", None),
        P("replica", None, None, "fsdp"),
        P("replica", "fsdp", None),
        P(None, None, "fsdp"),
        P("fsdp", None),
        P(None, None, "fsdp"),
        P("fsdp", None),
    )
    out_specs = (
        P(None, None, "fsdp"),
        P("fsdp", None),
        P(None, None, "fsdp"),
        P("fsdp", None),
        P("replica", None, None, "fsdp"),
        P("replica", "fsdp", None),
        P("replica", None, None, "fsdp"),
        P("replica", "fsdp", None),
    )
    return jax.shard_map(local, mesh=mesh, in_specs=in_specs, out_specs=out_specs, check_vma=False)
```

profile of v0, /device:TPU:1, one launch (start us, length us, event | category | flops | bytes accessed | tf_op | source)
XLA Modules:
  0.0 410.9 jit_solution(13865541734734214414)
XLA Ops:
  7.2 0.0 copy-start.8
  7.2 0.0 all-gather.5.cloned.1.call-start
  7.2 0.7 all-gather.5.cloned.1.call-update
  7.9 0.0 all-gather.3.cloned.1.call-start
  8.0 0.7 all-gather.3.cloned.1.call-update
  8.7 0.0 all-reduce.3.cloned.1.call-start
  8.7 2.7 convert.4
  11.4 0.0 copy-done.8
  11.4 1.8 copy.20
  13.2 3.0 copy.25
  16.2 0.0 copy-done.17
  16.2 1.3 copy.21
  17.5 1.3 copy.22
  18.8 117.7 %all-gather.5.cloned.1.call-done = bf16[1,4096,2048]{2,1,0:T(8,128)(2,1)} async-done(((bf16[1,64,2048]{2,1,0:T(8,128)(2,1)}), bf16[1,4096,2048]{2,1,0:T(8,128)(2,1)}) %all-gather.5.cloned.1.call-update) | async-done | bytes 16777232 | tf_op jit(solution)/shard_map/all_gather | solution.py:78
  136.5 10.2 %fusion.4 = f32[4096,128]{1,0:T(8,128)S(1)} fusion(bf16[1,4096,2048]{2,1,0:T(8,128)(2,1)} %all-gather.5.cloned.1.call-done, bf16[1,2,2048,128]{3,2,1,0:T(8,128)(2,1)S(1)} %copy-done.15), kind=kOutput, calls=%fused_computation.4 | convolution fusion | flops 2147483648 | bytes 19398656 | tf_op jit(solution)/shard_map/dot_general | solution.py:27
  146.7 0.4 copy-done
  147.1 0.3 copy-done.16
  147.4 6.1 %fusion.6 = f32[4096,128]{1,0:T(8,128)} fusion(bf16[1,4096,2048]{2,1,0:T(8,128)(2,1)S(1)} %copy-done, bf16[1,2,2048,128]{3,2,1,0:T(8,128)(2,1)S(1)} %copy-done.16), kind=kOutput, calls=%fused_computation.6 | convolution fusion | flops 2147483648 | bytes 19398656 | tf_op jit(solution)/shard_map/dot_general | solution.py:28
  153.5 107.3 %all-gather.3.cloned.1.call-done = bf16[1,4096,2048]{2,1,0:T(8,128)(2,1)} async-done(((bf16[1,64,2048]{2,1,0:T(8,128)(2,1)}), bf16[1,4096,2048]{2,1,0:T(8,128)(2,1)}) %all-gather.3.cloned.1.call-update) | async-done | bytes 16777232 | tf_op jit(solution)/shard_map/all_gather | solution.py:80
  260.8 0.0 copy-done.11
  260.8 8.5 %fusion.10 = f32[4096,128]{1,0:T(8,128)S(1)} fusion(bf16[1,4096,2048]{2,1,0:T(8,128)(2,1)} %all-gather.3.cloned.1.call-done, f32[1,128,2048]{2,1,0:T(8,128)S(1)} %copy-done.11), kind=kOutput, calls=%fused_computation.10 | convolution fusion | flops 2147745792 | bytes 19922944 | tf_op jit(solution)/shard_map/dot_general | solution.py:38
  269.3 0.0 slice-start.2
  269.3 0.0 slice-start.3
  269.3 8.3 %fusion = f32[128,2048]{1,0:T(8,128)S(1)} fusion(bf16[1,4096,2048]{2,1,0:T(8,128)(2,1)} %all-gather.5.cloned.1.call-done, f32[4096,128]{1,0:T(8,128)S(1)} %fusion.10, f32[4096,128]{1,0:T(8,128)S(1)} %fusion.4), kind=kOutput, calls=%fused_computation | convolution fusion | flops 2150629376 | bytes 22020096 | tf_op jit(solution)/shard_map/dot_general | solution.py:18
  277.7 0.0 copy-start.1
  277.7 0.0 copy-start.5
  277.7 4.5 %fusion.2 = f32[128,2048]{1,0:T(8,128)S(1)} fusion(bf16[1,4096,2048]{2,1,0:T(8,128)(2,1)S(1)} %bitcast.88, f32[4096,128]{1,0:T(8,128)S(1)} %fusion.4, f32[4096,128]{1,0:T(8,128)S(1)} %fusion.10, f32[4096,128]{1,0:T(8,128)} %fusion.6), kind=kOutput, calls=%fused_computation.2 | convolution fusion | flops 2152726528 | bytes 24117248 | tf_op jit(solution)/shard_map/dot_general | solution.py:18
  282.1 0.0 copy-start.3
  282.2 0.0 copy-start.12
  282.2 0.0 copy-start.13
  282.2 0.0 copy-start.19
  282.2 0.0 copy-start.20
  282.2 5.4 %fusion.21 = f32[2,2048,128]{1,2,0:T(8,128)} fusion(f32[2,2048,128]{1,2,0:T(8,128)S(1)} %copy-done.1, f32[1,2,2048,128]{2,3,1,0:T(8,128)} %copy.20, bf16[1,2,2048,128]{2,3,1,0:T(8,128)(2,1)} %copy.22, f32[1,2048,128]{1,2,0:T(8,128)S(1)} %bitcast.89, f32[1,2048,128]{1,2,0:T(8,128)S(1)} %bitcast.91, bf16[1,2,2048,128]{2,3,1,0:T(8,128)(2,1)S(1)} %copy-done.5), kind=kLoop, calls=%fused_computation.28 | loop fusion | flops 9961472 | bytes 10485760 | tf_op jit(solution)/shard_map/sub | solution.py:84
  287.6 0.0 copy-done.13
  287.6 0.0 copy-done.19
  287.6 10.2 %fusion.30 = (bf16[1,128,2048]{2,1,0:T(8,128)(2,1)}, f32[128,2048]{1,0:T(8,128)}, bf16[1,128,2048]{2,1,0:T(8,128)(2,1)}) fusion(bf16[1,128,2048]{2,1,0:T(8,128)(2,1)S(1)} %copy-done.19, f32[128,2048]{1,0:T(8,128)S(1)} %copy-done.13, bf16[1,128,2048]{2,1,0:T(8,128)(2,1)S(1)} %copy-done.20, f32[1,128,2048]{2,1,0:T(8,128)S(1)} %copy-done.12, ...), kind=kOutput, calls=%fused_computation.52 | convolution fusion | flops 2155872256 | bytes 26214400 | tf_op jit(solution)/shard_map/dot_general | solution.py:18
  297.9 0.0 all-reduce.3.cloned.1.call-update
  297.9 0.0 copy-start.4
  297.9 0.0 copy-start.6
  297.9 3.0 copy.24
  301.0 3.3 fusion.19
  304.2 2.4 copy.28
  306.7 1.3 copy.29
  308.0 83.3 %all-reduce.3.cloned.1.call-done = (f32[2,2048,128]{1,2,0:T(8,128)}, f32[128,2048]{1,0:T(8,128)}) async-done(((f32[2,2048,128]{1,2,0:T(8,128)}, f32[128,2048]{1,0:T(8,128)}), (f32[2,2048,128]{1,2,0:T(8,128)}, f32[128,2048]{1,0:T(8,128)})) %all-reduce.3.cloned.1.call-update) | async-done | bytes 3145744 | tf_op jit(solution)/shard_map/psum | solution.py:87
  391.2 5.1 %multiply_add_fusion = (f32[2,2048,128]{1,2,0:T(8,128)}, f32[2,2048,128]{1,2,0:T(8,128)}) fusion(f32[2,2048,128]{1,2,0:T(8,128)} %copy.24, f32[2,2048,128]{1,2,0:T(8,128)} %get-tuple-element.16, f32[2,2048,128]{1,2,0:T(8,128)S(1)} %copy-done.2), kind=kLoop, calls=%fused_computation.32 | loop fusion | flops 3670016 | bytes 10485760 | tf_op jit(solution)/shard_map/add | solution.py:59
  396.4 3.0 copy.26
  399.4 1.8 copy.27
  401.2 3.2 multiply_subtract_fusion.1
  (32 shorter events, 0.1 us)
Async XLA Ops:
  7.2 4.2 %copy-start.8 = (f32[1,2,2048,128]{3,2,1,0:T(8,128)S(1)}, f32[1,2,2048,128]{3,2,1,0:T(8,128)}, u32[]{:S(2)}) copy-start(f32[1,2,2048,128]{3,2,1,0:T(8,128)} %param.14) | copy-start | bytes 6291460
  7.2 129.3 %all-gather.5.cloned.1.call-start = ((), (), s32[]{:S(2)}) async-start(), calls=%async_computation.1 | async-start | bytes 17039360 | tf_op jit(solution)/shard_map/all_gather | solution.py:78
  7.9 252.9 %all-gather.3.cloned.1.call-start = ((), (), s32[]{:S(2)}) async-start(), calls=%async_computation | async-start | bytes 17039360 | tf_op jit(solution)/shard_map/all_gather | solution.py:80
  8.7 382.6 %all-reduce.3.cloned.1.call-start = ((), (), s32[]{:S(2)}) async-start(), calls=%async_computation.2 | async-start | bytes 6291456 | tf_op jit(solution)/shard_map/psum | solution.py:87
  13.2 3.0 copy-start.17
  16.2 1.3 copy-start.18
  16.2 120.3 %copy-start.15 = (bf16[1,2,2048,128]{3,2,1,0:T(8,128)(2,1)S(1)}, bf16[1,2,2048,128]{3,2,1,0:T(8,128)(2,1)}, u32[]{:S(2)}) copy-start(bf16[1,2,2048,128]{3,2,1,0:T(8,128)(2,1)} %convert.4) | copy-start | bytes 3145732
  136.5 10.6 %copy-start = (bf16[1,4096,2048]{2,1,0:T(8,128)(2,1)S(1)}, bf16[1,4096,2048]{2,1,0:T(8,128)(2,1)}, u32[]{:S(2)}) copy-start(bf16[1,4096,2048]{2,1,0:T(8,128)(2,1)} %all-gather.5.cloned.1.call-done) | copy-start | bytes 50331652
  136.5 10.9 %copy-start.16 = (bf16[1,2,2048,128]{3,2,1,0:T(8,128)(2,1)S(1)}, bf16[1,2,2048,128]{3,2,1,0:T(8,128)(2,1)}, u32[]{:S(2)}) copy-start(bf16[1,2,2048,128]{3,2,1,0:T(8,128)(2,1)} %convert.4) | copy-start | bytes 3145732
  147.4 113.4 %copy-start.11 = (f32[1,128,2048]{2,1,0:T(8,128)S(1)}, f32[1,128,2048]{2,1,0:T(8,128)}, u32[]{:S(2)}) copy-start(f32[1,128,2048]{2,1,0:T(8,128)} %param.15) | copy-start | bytes 3145732
  260.8 16.8 %slice-start = ((s8[16777216]{0:T(1024)(128)(4,1)}), s8[4194304]{0:T(1024)(128)(4,1)S(1)}, s32[]{:S(2)}) async-start(s8[16777216]{0:T(1024)(128)(4,1)} %bitcast.87), calls=%async_computation.3 | async-start | bytes 8388608
  260.8 16.8 %slice-start.1 = ((s8[16777216]{0:T(1024)(128)(4,1)}), s8[4194304]{0:T(1024)(128)(4,1)S(1)}, s32[]{:S(2)}) async-start(s8[16777216]{0:T(1024)(128)(4,1)} %bitcast.87), calls=%async_computation.4 | async-start | bytes 8388608
  269.3 8.4 %slice-start.2 = ((s8[16777216]{0:T(1024)(128)(4,1)}), s8[4194304]{0:T(1024)(128)(4,1)S(1)}, s32[]{:S(2)}) async-start(s8[16777216]{0:T(1024)(128)(4,1)} %bitcast.87), calls=%async_computation.5 | async-start | bytes 8388608
  269.3 8.4 %slice-start.3 = ((s8[16777216]{0:T(1024)(128)(4,1)}), s8[4194304]{0:T(1024)(128)(4,1)S(1)}, s32[]{:S(2)}) async-start(s8[16777216]{0:T(1024)(128)(4,1)} %bitcast.87), calls=%async_computation.6 | async-start | bytes 8388608
  277.7 4.5 %copy-start.1 = (f32[2,2048,128]{1,2,0:T(8,128)S(1)}, f32[2,2048,128]{1,2,0:T(8,128)}, u32[]{:S(2)}) copy-start(f32[2,2048,128]{1,2,0:T(8,128)} %copy.25) | copy-start | bytes 6291460
  277.7 4.5 %copy-start.5 = (bf16[1,2,2048,128]{2,3,1,0:T(8,128)(2,1)S(1)}, bf16[1,2,2048,128]{2,3,1,0:T(8,128)(2,1)}, u32[]{:S(2)}) copy-start(bf16[1,2,2048,128]{2,3,1,0:T(8,128)(2,1)} %copy.21) | copy-start | bytes 3145732
  282.1 5.5 %copy-start.3 = (f32[128,2048]{1,0:T(8,128)}, f32[128,2048]{1,0:T(8,128)S(1)}, u32[]{:S(2)}) copy-start(f32[128,2048]{1,0:T(8,128)S(1)} %fusion.2) | copy-start | bytes 3145732
  282.2 5.4 %copy-start.9 = (f32[4096,128]{1,0:T(8,128)S(1)}, f32[4096,128]{1,0:T(8,128)}, u32[]{:S(2)}) copy-start(f32[4096,128]{1,0:T(8,128)} %fusion.6) | copy-start | bytes 6291460
  282.2 5.4 %copy-start.12 = (f32[1,128,2048]{2,1,0:T(8,128)S(1)}, f32[1,128,2048]{2,1,0:T(8,128)}, u32[]{:S(2)}) copy-start(f32[1,128,2048]{2,1,0:T(8,128)} %param.15) | copy-start | bytes 3145732
  282.2 5.4 %copy-start.13 = (f32[128,2048]{1,0:T(8,128)S(1)}, f32[128,2048]{1,0:T(8,128)}, u32[]{:S(2)}) copy-start(f32[128,2048]{1,0:T(8,128)} %param.21) | copy-start | bytes 3145732
  282.2 5.4 %copy-start.19 = (bf16[1,128,2048]{2,1,0:T(8,128)(2,1)S(1)}, bf16[1,128,2048]{2,1,0:T(8,128)(2,1)}, u32[]{:S(2)}) copy-start(bf16[1,128,2048]{2,1,0:T(8,128)(2,1)} %param.19) | copy-start | bytes 1572868
  282.2 5.4 %copy-start.20 = (bf16[1,128,2048]{2,1,0:T(8,128)(2,1)S(1)}, bf16[1,128,2048]{2,1,0:T(8,128)(2,1)}, u32[]{:S(2)}) copy-start(bf16[1,128,2048]{2,1,0:T(8,128)(2,1)} %param.17) | copy-start | bytes 1572868
  297.9 3.1 copy-start.4
  297.9 3.0 copy-start.6
  304.2 2.4 copy-start.10
  304.2 87.0 %copy-start.2 = (f32[2,2048,128]{1,2,0:T(8,128)S(1)}, f32[2,2048,128]{1,2,0:T(8,128)}, u32[]{:S(2)}) copy-start(f32[2,2048,128]{1,2,0:T(8,128)} %copy.25) | copy-start | bytes 6291460
  396.4 3.0 copy-start.7
  399.4 1.8 copy-start.14
Sparse Core Ops, SparseCore 0:
  9.7 126.7 all-gather.4
  138.2 122.5 all-gather.2
  298.0 93.1 all-reduce.2
where the time goes:
time: 411 us
  waiting for transfers between devices  310 us (75%)
  matrix products  47.7 us (12%)
  local copies, waits for them, and re-layouts  19.8 us (5%)
  other arithmetic  19.7 us (5%)
  between operations  14 us (3%)
    all_gather x1, waiting for transfers between devices, local(): rows_in = lax.all_gather(inputs, 'fsdp', axis=1, tiled=True)  118 us
    all_gather x1, waiting for transfers between devices, local(): rows_cot = lax.all_gather(cotangent, 'fsdp', axis=1, tiled=True)  107 us
    psum x1, waiting for transfers between devices, local(): total_in, total_down = lax.psum((delta_in, delta_down), 'replica')  83.3 us
    dot_general x3, matrix products, contract_rows(): lax.dot_general(left, right, (((0,), (0,)), ((), ())), preferred_element_...  23 us
    unnamed x59, local copies, waits for them, and re-layouts  19.8 us
    dot_general x1, matrix products, forward(): gate_pre = jnp.dot(rows_in, gate_w, preferred_element_type=jnp.float32)  10.2 us
    dot_general x1, matrix products, backward(): lax.dot_general(rows_cot, down_w, (((1,), (1,)), ((), ())), preferred_ele...  8.47 us
  transfers between devices with their start and end apart: 3, of which 3 were waited for; matrix products, arithmetic and copies ran while one was open for 9% of the time, Pallas kernels for 0%

commit v1 on v0

v1 whole, which is shorter than its diff:
```python
import functools

import jax
import jax.numpy as jnp
from jax import lax
from jax.experimental import pallas as pl
from jax.experimental.pallas import tpu as pltpu
from jax.sharding import PartitionSpec as P

beta_one = 0.9
beta_two = 0.95
bias_one = 1.0 - 0.9**64
bias_two = 1.0 - 0.95**64
inner_rate = 0.004
decay_rate = 0.1
epsilon_adam = 1e-08
momentum_keep = 0.9
outer_rate = 0.7

AXES = {"x": (4, 16), "z": (2, 8), "y": (4, 2), "core": (2, 1)}
FSDP = 64


def shift(value, axis, by):
    size, stride = AXES[axis]
    pairs = []
    for i in range(FSDP):
        place = (i // stride) % size
        pairs.append((i, i + ((place + by) % size - place) * stride))
    return lax.ppermute(value, "fsdp", pairs)


def after(values, *others):
    out = lax.optimization_barrier((values, others))
    return out[0]


def direct_ring(rows, axis):
    return [rows, shift(rows, axis, 1), shift(rows, axis, -1), shift(rows, axis, 2)]


def forward_kernel(count, *refs):
    gate_ref, up_ref, down_ref = refs[:3]
    pieces = refs[3 : 3 + 2 * count]
    outs = refs[3 + 2 * count :]
    for k in range(count):
        x_ref, c_ref = pieces[2 * k], pieces[2 * k + 1]
        rows_in, rows_cot = x_ref[0], c_ref[0]
        gate_pre = jnp.dot(rows_in, gate_ref[...], preferred_element_type=jnp.float32)
        up_proj = jnp.dot(rows_in, up_ref[...], preferred_element_type=jnp.float32)
        dhidden = lax.dot_general(
            rows_cot, down_ref[...], (((1,), (1,)), ((), ())), preferred_element_type=jnp.float32
        )
        sig = 1.0 / (1.0 + jnp.exp(-gate_pre))
        silu = gate_pre * sig
        outs[3 * k][...] = (silu * up_proj).astype(jnp.bfloat16)
        outs[3 * k + 1][...] = (dhidden * up_proj * (sig * (1.0 + gate_pre * (1.0 - sig)))).astype(
            jnp.bfloat16
        )
        outs[3 * k + 2][...] = (dhidden * silu).astype(jnp.bfloat16)


def plane(array, index):
    rows, width = array.shape[1:]
    return pl.BlockSpec((1, rows, width), lambda i, index=index: (index, 0, 0))


def forward(weights, pieces):
    gate_w, up_w, down_w = weights
    width = down_w.shape[0]
    operands, specs, shapes, out_specs = [], [], [], []
    for x, xi, c, ci in pieces:
        operands += [x, c]
        specs += [plane(x, xi), plane(c, ci)]
        rows = x.shape[1]
        shapes += [jax.ShapeDtypeStruct((rows, width), jnp.bfloat16)] * 3
        out_specs += [pl.BlockSpec((rows, width), lambda i: (0, 0))] * 3
    whole = [pl.BlockSpec(w.shape, lambda i: (0, 0)) for w in weights]
    total = sum(p[0].shape[1] for p in pieces)
    outs = pl.pallas_call(
        functools.partial(forward_kernel, len(pieces)),
        grid=(1,),
        in_specs=whole + specs,
        out_specs=out_specs,
        out_shape=shapes,
        cost_estimate=pl.CostEstimate(
            flops=2 * total * 2048 * 3 * width,
            bytes_accessed=total * 2048 * 4,
            transcendentals=total * width,
        ),
        compiler_params=pltpu.CompilerParams(vmem_limit_bytes=40 * 1024 * 1024),
        name="forward",
    )(gate_w, up_w, down_w, *operands)
    return [tuple(outs[3 * k : 3 * k + 3]) for k in range(len(pieces))]


def contract(left, right):
    return lax.dot_general(
        left, right, (((0,), (0,)), ((), ())), preferred_element_type=jnp.float32
    )


def grad_down_kernel(count, *refs):
    hidden, cot = refs[:count], refs[count : 2 * count]
    own_ref, send_ref = refs[2 * count :]
    half = own_ref.shape[0]
    total = contract(hidden[0][...], cot[0][0])
    for k in range(1, count):
        total += contract(hidden[k][...], cot[k][0])
    own_ref[...] = total[:half]
    send_ref[...] = total[half:].astype(jnp.bfloat16)


def grad_in_kernel(count, *refs):
    dgate, dup, rows = refs[:count], refs[count : 2 * count], refs[2 * count : 3 * count]
    own_ref, send_ref = refs[3 * count :]
    half = own_ref.shape[2]
    for which, grads in enumerate((dgate, dup)):
        total = contract(grads[0][...], rows[0][0])
        for k in range(1, count):
            total += contract(grads[k][...], rows[k][0])
        total = total.T
        own_ref[which] = total[:, :half]
        send_ref[which] = total[:, half:].astype(jnp.bfloat16)


TILE = 256


def column(array, index):
    return pl.BlockSpec((1, array.shape[1], TILE), lambda i, index=index: (index, 0, i))


def gradient_down(hidden, cots):
    width = hidden[0].shape[1]
    depth = cots[0][0].shape[2]
    half = width // 2
    return pl.pallas_call(
        functools.partial(grad_down_kernel, len(hidden)),
        grid=(depth // TILE,),
        in_specs=[pl.BlockSpec(h.shape, lambda i: (0, 0)) for h in hidden]
        + [column(c, k) for c, k in cots],
        out_specs=[pl.BlockSpec((half, TILE), lambda i: (0, i))] * 2,
        out_shape=[
            jax.ShapeDtypeStruct((half, depth), jnp.float32),
            jax.ShapeDtypeStruct((half, depth), jnp.bfloat16),
        ],
        compiler_params=pltpu.CompilerParams(vmem_limit_bytes=40 * 1024 * 1024),
        name="grad_down",
    )(*hidden, *[c for c, _ in cots])


def gradient_in(dgate, dup, rows):
    width = dgate[0].shape[1]
    depth = rows[0][0].shape[2]
    half = width // 2
    return pl.pallas_call(
        functools.partial(grad_in_kernel, len(dgate)),
        grid=(depth // TILE,),
        in_specs=[pl.BlockSpec(h.shape, lambda i: (0, 0)) for h in dgate + dup]
        + [column(c, k) for c, k in rows],
        out_specs=[pl.BlockSpec((2, TILE, half), lambda i: (0, i, 0))] * 2,
        out_shape=[
            jax.ShapeDtypeStruct((2, depth, half), jnp.float32),
            jax.ShapeDtypeStruct((2, depth, half), jnp.bfloat16),
        ],
        compiler_params=pltpu.CompilerParams(vmem_limit_bytes=40 * 1024 * 1024),
        name="grad_in",
    )(*dgate, *dup, *[c for c, _ in rows])


def adamw(param, grad, first, second):
    first_new = beta_one * first.astype(jnp.float32) + (1.0 - beta_one) * grad
    second_new = beta_two * second.astype(jnp.float32) + (1.0 - beta_two) * grad * grad
    update = first_new / bias_one / (jnp.sqrt(second_new / bias_two) + epsilon_adam)
    param_new = param - inner_rate * (update + decay_rate * param)
    return (param_new, first_new.astype(jnp.bfloat16), second_new.astype(jnp.bfloat16))


def outer_step(own, other, base, outer):
    grad_outer = (own.astype(jnp.float32) + other.astype(jnp.float32)) / 2.0
    new_outer = momentum_keep * outer + grad_outer
    new_base = base - outer_rate * (grad_outer + momentum_keep * new_outer)
    return (new_base, new_outer)


def local(
    inputs,
    cotangent,
    params_in,
    params_down,
    first_in,
    first_down,
    second_in,
    second_down,
    base_in,
    base_down,
    outer_in,
    outer_down,
):
    half = inputs.shape[1] // 2
    own = [
        jnp.concatenate([inputs[:, k * half : (k + 1) * half], cotangent[:, k * half : (k + 1) * half]])
        for k in range(2)
    ]
    routes = (("x", "y"), ("y", "x"))
    first_wave = [direct_ring(own[k], routes[k][0]) for k in range(2)]
    across = [shift(own[k], "z", 1) for k in range(2)]

    weights_own = [
        params_in[0, 0].astype(jnp.bfloat16),
        params_in[0, 1].astype(jnp.bfloat16),
        params_down[0].astype(jnp.bfloat16),
    ]
    gate_w, up_w, down_w = weights_own
    gate_o, up_o, down_o = [shift(w, "core", 1) for w in weights_own]
    weights = (
        jnp.concatenate([gate_w, gate_o], axis=1),
        jnp.concatenate([up_w, up_o], axis=1),
        jnp.concatenate([down_w, down_o], axis=0),
    )

    def gathered(ring):
        return jnp.concatenate(ring, axis=1)

    wave_one = [gathered(r) for r in first_wave]
    near_one = [
        (shift(wave_one[k], routes[k][1], 1), shift(wave_one[k], routes[k][1], -1)) for k in range(2)
    ]
    second_wave = [direct_ring(across[k], routes[k][0]) for k in range(2)]
    wave_two = [gathered(r) for r in second_wave]
    near_two = [
        (shift(wave_two[k], routes[k][1], 1), shift(wave_two[k], routes[k][1], -1)) for k in range(2)
    ]
    near_one = lax.optimization_barrier(near_one)

    def far(near):
        return [
            (shift(near[k][0][:1], routes[k][1], 1), shift(near[k][1][1:], routes[k][1], -1))
            for k in range(2)
        ]

    far_one = far(near_one)
    near_two = lax.optimization_barrier(near_two)
    far_two = far(near_two)

    groups = []
    for wave, near, distant in ((wave_one, near_one, far_one), (wave_two, near_two, far_two)):
        groups.append([(wave[k], 0, wave[k], 1) for k in range(2)])
        groups.append([(piece, 0, piece, 1) for k in range(2) for piece in near[k]])
        groups.append([(distant[k][0], 0, distant[k][1], 0) for k in range(2)])
    pieces = [piece for group in groups for piece in group]
    results = [r for group in groups for r in forward(weights, group)]

    own_down, send_down = gradient_down([r[0] for r in results], [(p[2], p[3]) for p in pieces])
    grad_down = own_down + shift(send_down, "core", 1).astype(jnp.float32)
    new_down, fdown, sdown = adamw(params_down[0], grad_down, first_down[0], second_down[0])
    delta_down = (base_down - new_down).astype(jnp.bfloat16)
    other_down = lax.ppermute(delta_down, "replica", [(0, 1), (1, 0)])

    own_in, send_in = gradient_in(
        [r[1] for r in results], [r[2] for r in results], [(p[0], p[1]) for p in pieces]
    )
    grad_in = own_in + shift(send_in, "core", 1).astype(jnp.float32)
    new_in, fin, sin = adamw(params_in[0], grad_in, first_in[0], second_in[0])
    delta_in = (base_in - new_in).astype(jnp.bfloat16)
    other_in = lax.ppermute(delta_in, "replica", [(0, 1), (1, 0)])

    new_base_down, new_outer_down = outer_step(delta_down, other_down, base_down, outer_down)
    new_base_in, new_outer_in = outer_step(delta_in, other_in, base_in, outer_in)
    return (
        new_base_in,
        new_base_down,
        new_outer_in,
        new_outer_down,
        fin[None],
        fdown[None],
        sin[None],
        sdown[None],
    )


def solution(mesh):
    in_specs = (
        P("replica", "fsdp", None),
        P("replica", "fsdp", None),
        P("replica", None, None, "fsdp"),
        P("replica", "fsdp", None),
        P("replica", None, None, "fsdp"),
        P("replica", "fsdp", None),
        P("replica", None, None, "fsdp"),
        P("replica", "fsdp", None),
        P(None, None, "fsdp"),
        P("fsdp", None),
        P(None, None, "fsdp"),
        P("fsdp", None),
    )
    out_specs = (
        P(None, None, "fsdp"),
        P("fsdp", None),
        P(None, None, "fsdp"),
        P("fsdp", None),
        P("replica", None, None, "fsdp"),
        P("replica", "fsdp", None),
        P("replica", None, None, "fsdp"),
        P("replica", "fsdp", None),
    )
    return jax.shard_map(local, mesh=mesh, in_specs=in_specs, out_specs=out_specs, check_vma=False)
```

time: 411 us -> 222 us (0.54)
  waiting for transfers between devices: 310 us -> 110 us
  starting transfers between devices: 0.11 us -> 60 us
  matrix products: 47.7 us -> 0 us
  Pallas kernels: 0 us -> 33.2 us
  local copies, waits for them, and re-layouts: 19.8 us -> 5.96 us
  between operations: 14 us -> 1.22 us
  other arithmetic: 19.7 us -> 10.6 us
    all_gather x2 -> x0, waiting for transfers between devices: 225 us -> none  [the longest x1 118 us: local(): rows_in = lax.all_gather(inputs, 'fsdp', axis=1, tiled=True)]
    ppermute x0 -> x37, waiting for transfers between devices: none -> 110 us  [the longest x35 82.4 us: shift(): return lax.ppermute(value, 'fsdp', pairs)]
    psum x1 -> x0, waiting for transfers between devices: 83.3 us -> none  [local(): total_in, total_down = lax.psum((delta_in, delta_down), 'replica')]
    ppermute x0 -> x37, starting transfers between devices: none -> 60 us  [the longest x35 55.6 us: shift(): return lax.ppermute(value, 'fsdp', pairs)]
    dot_general x6 -> x0, matrix products: 47.7 us -> none  [the longest x3 23 us: contract_rows(): lax.dot_general(left, right, (((0,), (0,)), ((), ())), preferred_element_...]
    pallas_call x0 -> x8, Pallas kernels: none -> 33.2 us  [the longest x1 14.4 us: gradient_in(): pl.pallas_call(functools.partial(grad_in_kernel, len(dgate)), grid=(depth...]
    unnamed x59 -> x60, local copies, waits for them, and re-layouts: 19.8 us -> 2.49 us
    broadcast_in_dim x0 -> x2, other arithmetic: none -> 5.45 us  [the longest x1 3.45 us: local(): sin[None]]
  transfers between devices with their start and end apart: 3 -> 37, of which waited for: 3 -> 17; matrix products, arithmetic and copies ran while one was open for 9% -> 5% of each run, Pallas kernels for 0% -> 11%
where the time goes in v1:
time: 222 us; the launch traced here: 221 us
  waiting for transfers between devices  110 us (50%)
  starting transfers between devices  60 us (27%)
  Pallas kernels  33.2 us (15%)
  other arithmetic  10.6 us (5%)
  local copies, waits for them, and re-layouts  5.96 us (3%)
    ppermute x35, waiting for transfers between devices, shift(): return lax.ppermute(value, 'fsdp', pairs)  82.4 us
    ppermute x35, starting transfers between devices, shift(): return lax.ppermute(value, 'fsdp', pairs)  55.6 us
    ppermute x1, waiting for transfers between devices, local(): other_in = lax.ppermute(delta_in, 'replica', [(0, 1), (1, 0)])  20.8 us
    pallas_call x1, Pallas kernels, gradient_in(): pl.pallas_call(functools.partial(grad_in_kernel, len(dgate)), grid=(depth...  14.4 us
    pallas_call x6, Pallas kernels, forward(): pl.pallas_call(functools.partial(forward_kernel, len(pieces)), grid=(1,),...  10.5 us
    pallas_call x1, Pallas kernels, gradient_down(): pl.pallas_call(functools.partial(grad_down_kernel, len(hidden)), grid=(de...  8.33 us
    ppermute x1, waiting for transfers between devices, local(): other_down = lax.ppermute(delta_down, 'replica', [(0, 1), (1, 0)])  7.21 us
  transfers between devices with their start and end apart: 37, of which 17 were waited for; matrix products, arithmetic and copies ran while one was open for 5% of the time, Pallas kernels for 11%

profile of v1, /device:TPU:1, one launch (start us, length us, event | category | flops | bytes accessed | tf_op | source)
XLA Modules:
  0.0 221.3 jit_solution(3597284350208704609)
XLA Ops:
  0.6 1.3 fusion.10
  2.0 2.5 %collective-permute-start.17 = (bf16[2,32,2048]{2,1,0:T(8,128)(2,1)S(1)}, bf16[2,32,2048]{2,1,0:T(8,128)(2,1)S(1)}, u32[]{:S(2)}, u32[]{:S(2)}) collective-permute-start(bf16[2,32,2048]{2,1,0:T(8,128)(2,1)S(1)} %pad_maximum_fusion.5), channel_id=1, source_target_pairs={{0,8},{1,9},{2,10},{3,11},{4,12},{5,13},{6,14},{7,15},{8,0},{9,1},... | collective-permute-start | bytes 786440 | tf_op jit(solution)/shard_map/ppermute | solution.py:30
  4.5 2.7 %collective-permute-start.5 = (bf16[2,32,2048]{2,1,0:T(8,128)(2,1)S(1)}, bf16[2,32,2048]{2,1,0:T(8,128)(2,1)S(1)}, u32[]{:S(2)}, u32[]{:S(2)}) collective-permute-start(bf16[2,32,2048]{2,1,0:T(8,128)(2,1)S(1)} %pad_maximum_fusion.5), channel_id=1, source_target_pairs={{0,32},{1,33},{2,34},{3,35},{4,36},{5,37},{6,38},{7,39},{8,40},{9,... | collective-permute-start | bytes 786440 | tf_op jit(solution)/shard_map/ppermute | solution.py:30
  7.3 3.0 %collective-permute-start.8 = (bf16[2,32,2048]{2,1,0:T(8,128)(2,1)S(1)}, bf16[2,32,2048]{2,1,0:T(8,128)(2,1)S(1)}, u32[]{:S(2)}, u32[]{:S(2)}) collective-permute-start(bf16[2,32,2048]{2,1,0:T(8,128)(2,1)S(1)} %pad_maximum_fusion.6), channel_id=1, source_target_pairs={{0,4},{1,5},{2,6},{3,7},{4,0},{5,1},{6,2},{7,3},{8,12},{9,13},{10,... | collective-permute-start | bytes 786440 | tf_op jit(solution)/shard_map/ppermute | solution.py:30
  12.0 3.5 %collective-permute-done.8 = bf16[2,32,2048]{2,1,0:T(8,128)(2,1)S(1)} collective-permute-done((bf16[2,32,2048]{2,1,0:T(8,128)(2,1)S(1)}, bf16[2,32,2048]{2,1,0:T(8,128)(2,1)S(1)}, u32[]{:S(2)}, u32[]{:S(2)}) %collective-permute-start.8) | collective-permute-done | bytes 262176 | tf_op jit(solution)/shard_map/ppermute | solution.py:30
  16.3 5.7 %collective-permute-done.7 = bf16[2,32,2048]{2,1,0:T(8,128)(2,1)S(1)} collective-permute-done((bf16[2,32,2048]{2,1,0:T(8,128)(2,1)S(1)}, bf16[2,32,2048]{2,1,0:T(8,128)(2,1)S(1)}, u32[]{:S(2)}, u32[]{:S(2)}) %collective-permute-start.7) | collective-permute-done | bytes 262176 | tf_op jit(solution)/shard_map/ppermute | solution.py:30
  22.7 2.4 %collective-permute-start.12 = (bf16[2,128,2048]{2,1,0:T(8,128)(2,1)S(1)}, bf16[2,128,2048]{2,1,0:T(8,128)(2,1)S(1)}, u32[]{:S(2)}, u32[]{:S(2)}) collective-permute-start(bf16[2,128,2048]{2,1,0:T(8,128)(2,1)S(1)} %pad_maximum_fusion.4.refs_5_.refs_6_.refs_33_.refs_17_), channel_id=1, source_target_pairs={{0,48},{1,49},{2,50},{3,51},{4,52},{5,53},{6,54},{7,55},{8,56},{9,... | collective-permute-start | bytes 3145736 | tf_op jit(solution)/shard_map/ppermute | solution.py:30
  25.1 1.5 collective-permute-start.19
  26.6 3.0 %collective-permute-done.3 = bf16[2,32,2048]{2,1,0:T(8,128)(2,1)S(1)} collective-permute-done((bf16[2,32,2048]{2,1,0:T(8,128)(2,1)S(1)}, bf16[2,32,2048]{2,1,0:T(8,128)(2,1)S(1)}, u32[]{:S(2)}, u32[]{:S(2)}) %collective-permute-start.3) | collective-permute-done | bytes 262176 | tf_op jit(solution)/shard_map/ppermute | solution.py:30
  29.6 3.4 %collective-permute-start.24 = (bf16[2,32,2048]{2,1,0:T(8,128)(2,1)S(1)}, bf16[2,32,2048]{2,1,0:T(8,128)(2,1)S(1)}, u32[]{:S(2)}, u32[]{:S(2)}) collective-permute-start(bf16[2,32,2048]{2,1,0:T(8,128)(2,1)S(1)} %collective-permute-done.21), channel_id=1, source_target_pairs={{0,4},{1,5},{2,6},{3,7},{4,0},{5,1},{6,2},{7,3},{8,12},{9,13},{10,... | collective-permute-start | bytes 786440 | tf_op jit(solution)/shard_map/ppermute | solution.py:30
  33.1 1.9 collective-permute-done.20
  35.0 4.8 %collective-permute-start.2 = (bf16[128,2048]{1,0:T(8,128)(2,1)S(1)}, bf16[128,2048]{1,0:T(8,128)(2,1)S(1)}, u32[]{:S(2)}, u32[]{:S(2)}) collective-permute-start(bf16[128,2048]{1,0:T(8,128)(2,1)S(1)} %bitcast_convert_fusion), channel_id=1, source_target_pairs={{0,1},{1,0},{2,3},{3,2},{4,5},{5,4},{6,7},{7,6},{8,9},{9,8},{10,11... | collective-permute-start | bytes 1572872 | tf_op jit(solution)/shard_map/ppermute | solution.py:30
  39.8 16.9 %collective-permute-done.19 = bf16[2,32,2048]{2,1,0:T(8,128)(2,1)S(1)} collective-permute-done((bf16[2,32,2048]{2,1,0:T(8,128)(2,1)S(1)}, bf16[2,32,2048]{2,1,0:T(8,128)(2,1)S(1)}, u32[]{:S(2)}, u32[]{:S(2)}) %collective-permute-start.19) | collective-permute-done | bytes 262176 | tf_op jit(solution)/shard_map/ppermute | solution.py:30
  56.7 4.5 %collective-permute-start.23 = (bf16[2,32,2048]{2,1,0:T(8,128)(2,1)S(1)}, bf16[2,32,2048]{2,1,0:T(8,128)(2,1)S(1)}, u32[]{:S(2)}, u32[]{:S(2)}) collective-permute-start(bf16[2,32,2048]{2,1,0:T(8,128)(2,1)S(1)} %collective-permute-done.21), channel_id=1, source_target_pairs={{0,6},{1,7},{2,0},{3,1},{4,2},{5,3},{6,4},{7,5},{8,14},{9,15},{10,... | collective-permute-start | bytes 786440 | tf_op jit(solution)/shard_map/ppermute | solution.py:30
  61.2 2.3 %collective-permute-start.1 = (bf16[2048,128]{1,0:T(8,128)(2,1)S(1)}, bf16[2048,128]{1,0:T(8,128)(2,1)S(1)}, u32[]{:S(2)}, u32[]{:S(2)}) collective-permute-start(bf16[2048,128]{1,0:T(8,128)(2,1)S(1)} %get-tuple-element.138), channel_id=1, source_target_pairs={{0,1},{1,0},{2,3},{3,2},{4,5},{5,4},{6,7},{7,6},{8,9},{9,8},{10,11... | collective-permute-start | bytes 1572872 | tf_op jit(solution)/shard_map/ppermute | solution.py:30
  63.5 1.2 collective-permute-done.23
  65.2 2.7 %collective-permute-done.22 = bf16[2,32,2048]{2,1,0:T(8,128)(2,1)S(1)} collective-permute-done((bf16[2,32,2048]{2,1,0:T(8,128)(2,1)S(1)}, bf16[2,32,2048]{2,1,0:T(8,128)(2,1)S(1)}, u32[]{:S(2)}, u32[]{:S(2)}) %collective-permute-start.22) | collective-permute-done | bytes 262176 | tf_op jit(solution)/shard_map/ppermute | solution.py:30
  69.5 2.0 collective-permute-start.26
  71.6 17.1 %collective-permute-done.11.refs_7_.refs_8_.refs_36_.refs_20_ = bf16[2,128,2048]{2,1,0:T(8,128)(2,1)S(1)} collective-permute-done((bf16[2,128,2048]{2,1,0:T(8,128)(2,1)S(1)}, bf16[2,128,2048]{2,1,0:T(8,128)(2,1)S(1)}, u32[]{:S(2)}, u32[]{:S(2)}) %collective-permute-start.11) | collective-permute-done | bytes 1048608 | tf_op jit(solution)/shard_map/ppermute | solution.py:30
  88.7 1.2 collective-permute-start.28
  89.9 7.2 %collective-permute-start = (bf16[2048,128]{1,0:T(8,128)(2,1)S(1)}, bf16[2048,128]{1,0:T(8,128)(2,1)S(1)}, u32[]{:S(2)}, u32[]{:S(2)}) collective-permute-start(bf16[2048,128]{1,0:T(8,128)(2,1)S(1)} %get-tuple-element.139), channel_id=1, source_target_pairs={{0,1},{1,0},{2,3},{3,2},{4,5},{5,4},{6,7},{7,6},{8,9},{9,8},{10,11... | collective-permute-start | bytes 1572872 | tf_op jit(solution)/shard_map/ppermute | solution.py:30
  97.5 1.2 collective-permute-done
  98.7 3.4 %collective-permute-start.16 = (bf16[1,128,2048]{2,1,0:T(8,128)(2,1)S(1)}, bf16[1,128,2048]{2,1,0:T(8,128)(2,1)S(1)}, u32[]{:S(2)}, u32[]{:S(2)}) collective-permute-start(bf16[1,128,2048]{2,1,0:T(8,128)(2,1)S(1)} %slice.53), channel_id=1, source_target_pairs={{0,48},{1,49},{2,50},{3,51},{4,52},{5,53},{6,54},{7,55},{8,56},{9,... | collective-permute-start | bytes 1572872 | tf_op jit(solution)/shard_map/ppermute | solution.py:30
  102.1 9.7 %collective-permute-done.26.refs_5_.refs_6_.refs_43_.refs_27_ = bf16[2,128,2048]{2,1,0:T(8,128)(2,1)S(1)} collective-permute-done((bf16[2,128,2048]{2,1,0:T(8,128)(2,1)S(1)}, bf16[2,128,2048]{2,1,0:T(8,128)(2,1)S(1)}, u32[]{:S(2)}, u32[]{:S(2)}) %collective-permute-start.26) | collective-permute-done | bytes 1048608 | tf_op jit(solution)/shard_map/ppermute | solution.py:30
  112.6 1.3 collective-permute-done.25.refs_3_.refs_4_.refs_42_.refs_26_
  113.9 2.0 collective-permute-start.14
  116.4 6.0 %collective-permute-done.27.refs_7_.refs_8_.refs_44_.refs_28_ = bf16[2,128,2048]{2,1,0:T(8,128)(2,1)S(1)} collective-permute-done((bf16[2,128,2048]{2,1,0:T(8,128)(2,1)S(1)}, bf16[2,128,2048]{2,1,0:T(8,128)(2,1)S(1)}, u32[]{:S(2)}, u32[]{:S(2)}) %collective-permute-start.27) | collective-permute-done | bytes 1048608 | tf_op jit(solution)/shard_map/ppermute | solution.py:30
  124.4 1.2 collective-permute-start.32
  125.9 7.8 %collective-permute-done.15.refs_5_.refs_39_ = bf16[1,128,2048]{2,1,0:T(8,128)(2,1)S(1)} collective-permute-done((bf16[1,128,2048]{2,1,0:T(8,128)(2,1)S(1)}, bf16[1,128,2048]{2,1,0:T(8,128)(2,1)S(1)}, u32[]{:S(2)}, u32[]{:S(2)}) %collective-permute-start.15) | collective-permute-done | bytes 524320 | tf_op jit(solution)/shard_map/ppermute | solution.py:30
  133.7 2.9 %collective-permute-start.30 = (bf16[1,128,2048]{2,1,0:T(8,128)(2,1)S(1)}, bf16[1,128,2048]{2,1,0:T(8,128)(2,1)S(1)}, u32[]{:S(2)}, u32[]{:S(2)}) collective-permute-start(bf16[1,128,2048]{2,1,0:T(8,128)(2,1)S(1)} %slice.55), channel_id=1, source_target_pairs={{0,6},{1,7},{2,0},{3,1},{4,2},{5,3},{6,4},{7,5},{8,14},{9,15},{10,... | collective-permute-start | bytes 1572872 | tf_op jit(solution)/shard_map/ppermute | solution.py:30
  136.6 1.4 forward.9
  137.9 1.4 forward.6
  139.3 2.5 %forward.7 = (bf16[128,256]{1,0:T(8,128)(2,1)S(1)}, bf16[128,256]{1,0:T(8,128)(2,1)S(1)}, bf16[128,256]{1,0:T(8,128)(2,1)S(1)}, bf16[128,256]{1,0:T(8,128)(2,1)S...) custom-call(bf16[2048,256]{1,0:T(8,128)(2,1)S(1)} %pad_maximum_fusio, ...), custom_call_target="tpu_custom_call" | custom-call | flops 1610612736 | bytes 4194304 | tf_op jit(solution)/shard_map/forward/pallas_call | solution.py:80
  141.9 2.5 %forward.10 = (bf16[128,256]{1,0:T(8,128)(2,1)S(1)}, bf16[128,256]{1,0:T(8,128)(2,1)S(1)}, bf16[128,256]{1,0:T(8,128)(2,1)S(1)}, bf16[128,256]{1,0:T(8,128)(2,1)...) custom-call(bf16[2048,256]{1,0:T(8,128)(2,1)S(1)} %pad_maximum_fusio, ...), custom_call_target="tpu_custom_call" | custom-call | flops 1610612736 | bytes 4194304 | tf_op jit(solution)/shard_map/forward/pallas_call | solution.py:80
  144.4 1.4 forward.8
  146.9 3.1 %collective-permute-done.29.refs_3_.refs_46_ = bf16[1,128,2048]{2,1,0:T(8,128)(2,1)S(1)} collective-permute-done((bf16[1,128,2048]{2,1,0:T(8,128)(2,1)S(1)}, bf16[1,128,2048]{2,1,0:T(8,128)(2,1)S(1)}, u32[]{:S(2)}, u32[]{:S(2)}) %collective-permute-start.29) | collective-permute-done | bytes 524320 | tf_op jit(solution)/shard_map/ppermute | solution.py:30
  150.0 1.4 forward.11
  152.5 8.3 %grad_down.1 = (f32[128,2048]{1,0:T(8,128)S(1)}, bf16[128,2048]{1,0:T(8,128)(2,1)S(1)}) custom-call(bf16[128,256]{1,0:T(8,128)(2,1)S(1)} %get-tuple-element.110.refs_0_, bf16[128,256]{1,0:T(8,128)(2,1)S(1)} %get-tuple-element.111.refs_1_, bf16[128,256]{1,0:T(8,128)(2,1)S(1)} %get-tuple-element.112.refs_2_, bf16[128,256]{1,0:T(8,128)(2,1)S(1)} %get-tuple-element.113.refs_3_, ...), custom_call_target="tpu_custom_call" | custom-call | tf_op jit(solution)/shard_map/grad_down/pallas_call | solution.py:138
  160.8 2.4 %collective-permute-start.35 = (bf16[128,2048]{1,0:T(8,128)(2,1)S(1)}, bf16[128,2048]{1,0:T(8,128)(2,1)S(1)}, u32[]{:S(2)}, u32[]{:S(2)}) collective-permute-start(bf16[128,2048]{1,0:T(8,128)(2,1)S(1)} %get-tuple-element.127), channel_id=1, source_target_pairs={{0,1},{1,0},{2,3},{3,2},{4,5},{5,4},{6,7},{7,6},{8,9},{9,8},{10,11... | collective-permute-start | bytes 1572872 | tf_op jit(solution)/shard_map/ppermute | solution.py:30
  163.2 1.2 copy-done.5
  164.5 14.4 %grad_in.1 = (f32[2,2048,128]{2,1,0:T(8,128)}, bf16[2,2048,128]{2,1,0:T(8,128)(2,1)S(1)}) custom-call(bf16[128,256]{1,0:T(8,128)(2,1)S(1)} %get-tuple-element.68.refs_0_, bf16[128,256]{1,0:T(8,128)(2,1)S(1)} %get-tuple-element.69.refs_1_, bf16[128,256]{1,0:T(8,128)(2,1)S(1)} %get-tuple-element.74.refs_2_, bf16[128,256]{1,0:T(8,128)(2,1)S(1)} %get-tuple-element.75.refs_3_, ...), custom_call_target="tpu_custom_call" | custom-call | tf_op jit(solution)/shard_map/grad_in/pallas_call | solution.py:157
  179.0 2.0 convert_bitcast_fusion.2
  181.0 3.3 %collective-permute-start.36 = (bf16[128,2048]{1,0:T(8,128)(2,1)S(1)}, bf16[128,2048]{1,0:T(8,128)(2,1)S(1)}, u32[]{:S(2)}, u32[]{:S(2)}) collective-permute-start(bf16[128,2048]{1,0:T(8,128)(2,1)S(1)} %get-tuple-element.136), channel_id=1, source_target_pairs={{0,64},{64,0},{1,65},{65,1},{2,66},{66,2},{3,67},{67,3},{4,68},{68... | collective-permute-start | bytes 1572872 | tf_op jit(solution)/shard_map/ppermute | solution.py:259
  184.4 3.5 %convert_bitcast_fusion = (bf16[1,2,2048,128]{3,2,1,0:T(8,128)(2,1)}, bf16[2,2048,128]{2,1,0:T(8,128)(2,1)S(1)}, bf16[1,2,2048,128]{3,2,1,0:T(8,128)(2,1)}) fusion(f32[2,2048,128]{2,1,0:T(8,128)S(1)} %copy-done.21, bf16[2,2048,128]{2,1,0:T(8,128)(2,1)S(1)} %collective-permute-done.33, bf16[1,2,2048,128]{3,2,1,0:T(8,128)(2,1)S(1)} %copy-done.22, ...), kind=kLoop, calls=%fused_computation.28 | loop fusion | flops 12058624 | bytes 12582912 | tf_op jit(solution)/shard_map/broadcast_in_dim | solution.py:278
  189.0 7.2 %collective-permute-done.36 = bf16[128,2048]{1,0:T(8,128)(2,1)S(1)} collective-permute-done((bf16[128,2048]{1,0:T(8,128)(2,1)S(1)}, bf16[128,2048]{1,0:T(8,128)(2,1)S(1)}, u32[]{:S(2)}, u32[]{:S(2)}) %collective-permute-start.36) | collective-permute-done | bytes 524320 | tf_op jit(solution)/shard_map/ppermute | solution.py:259
  196.2 1.7 multiply_subtract_fusion.1
  197.9 20.8 %collective-permute-done.34 = bf16[2,2048,128]{2,1,0:T(8,128)(2,1)S(1)} collective-permute-done((bf16[2,2048,128]{2,1,0:T(8,128)(2,1)S(1)}, bf16[2,2048,128]{2,1,0:T(8,128)(2,1)S(1)}, u32[]{:S(2)}, u32[]{:S(2)}) %collective-permute-start.34) | collective-permute-done | bytes 1048608 | tf_op jit(solution)/shard_map/ppermute | solution.py:267
  218.7 2.7 %multiply_subtract_fusion = (f32[2,2048,128]{2,1,0:T(8,128)}, f32[2,2048,128]{2,1,0:T(8,128)}) fusion(f32[2,2048,128]{2,1,0:T(8,128)S(1)} %copy-done.14, bf16[2,2048,128]{2,1,0:T(8,128)(2,1)S(1)} %collective-permute-done.34, bf16[2,2048,128]{2,1,0:T(8,128)(2,1)S(1)} %get-tuple-element.133, f32[2,2048,128]{2,1,0:T(8,128)S(1)} %copy-done.20), kind=kLoop, calls=%fused_computation.9 | loop fusion | flops 5242880 | bytes 10485760 | tf_op jit(solution)/shard_map/sub | solution.py:183
  (119 shorter events, 12.5 us)
Async XLA Ops:
  2.0 20.7 %collective-permute-start.17 = (bf16[2,32,2048]{2,1,0:T(8,128)(2,1)S(1)}, bf16[2,32,2048]{2,1,0:T(8,128)(2,1)S(1)}, u32[]{:S(2)}, u32[]{:S(2)}) collective-permute-start(bf16[2,32,2048]{2,1,0:T(8,128)(2,1)S(1)} %pad_maximum_fusion.5), channel_id=1, source_target_pairs={{0,8},{1,9},{2,10},{3,11},{4,12},{5,13},{6,14},{7,15},{8,0},{9,1},... | collective-permute-start | bytes 786440 | tf_op jit(solution)/shard_map/ppermute | solution.py:30
  4.5 20.6 %collective-permute-start.5 = (bf16[2,32,2048]{2,1,0:T(8,128)(2,1)S(1)}, bf16[2,32,2048]{2,1,0:T(8,128)(2,1)S(1)}, u32[]{:S(2)}, u32[]{:S(2)}) collective-permute-start(bf16[2,32,2048]{2,1,0:T(8,128)(2,1)S(1)} %pad_maximum_fusion.5), channel_id=1, source_target_pairs={{0,32},{1,33},{2,34},{3,35},{4,36},{5,37},{6,38},{7,39},{8,40},{9,... | collective-permute-start | bytes 786440 | tf_op jit(solution)/shard_map/ppermute | solution.py:30
  7.3 8.1 %collective-permute-start.8 = (bf16[2,32,2048]{2,1,0:T(8,128)(2,1)S(1)}, bf16[2,32,2048]{2,1,0:T(8,128)(2,1)S(1)}, u32[]{:S(2)}, u32[]{:S(2)}) collective-permute-start(bf16[2,32,2048]{2,1,0:T(8,128)(2,1)S(1)} %pad_maximum_fusion.6), channel_id=1, source_target_pairs={{0,4},{1,5},{2,6},{3,7},{4,0},{5,1},{6,2},{7,3},{8,12},{9,13},{10,... | collective-permute-start | bytes 786440 | tf_op jit(solution)/shard_map/ppermute | solution.py:30
  10.3 11.8 %collective-permute-start.7 = (bf16[2,32,2048]{2,1,0:T(8,128)(2,1)S(1)}, bf16[2,32,2048]{2,1,0:T(8,128)(2,1)S(1)}, u32[]{:S(2)}, u32[]{:S(2)}) collective-permute-start(bf16[2,32,2048]{2,1,0:T(8,128)(2,1)S(1)} %pad_maximum_fusion.6), channel_id=1, source_target_pairs={{0,6},{1,7},{2,0},{3,1},{4,2},{5,3},{6,4},{7,5},{8,14},{9,15},{10,... | collective-permute-start | bytes 786440 | tf_op jit(solution)/shard_map/ppermute | solution.py:30
  11.1 11.3 %collective-permute-start.6 = (bf16[2,32,2048]{2,1,0:T(8,128)(2,1)S(1)}, bf16[2,32,2048]{2,1,0:T(8,128)(2,1)S(1)}, u32[]{:S(2)}, u32[]{:S(2)}) collective-permute-start(bf16[2,32,2048]{2,1,0:T(8,128)(2,1)S(1)} %pad_maximum_fusion.6), channel_id=1, source_target_pairs={{0,2},{1,3},{2,4},{3,5},{4,6},{5,7},{6,0},{7,1},{8,10},{9,11},{10,... | collective-permute-start | bytes 786440 | tf_op jit(solution)/shard_map/ppermute | solution.py:30
  15.4 9.7 %collective-permute-start.4 = (bf16[2,32,2048]{2,1,0:T(8,128)(2,1)S(1)}, bf16[2,32,2048]{2,1,0:T(8,128)(2,1)S(1)}, u32[]{:S(2)}, u32[]{:S(2)}) collective-permute-start(bf16[2,32,2048]{2,1,0:T(8,128)(2,1)S(1)} %pad_maximum_fusion.5), channel_id=1, source_target_pairs={{0,48},{1,49},{2,50},{3,51},{4,52},{5,53},{6,54},{7,55},{8,56},{9,... | collective-permute-start | bytes 786440 | tf_op jit(solution)/shard_map/ppermute | solution.py:30
  22.1 7.6 %collective-permute-start.3 = (bf16[2,32,2048]{2,1,0:T(8,128)(2,1)S(1)}, bf16[2,32,2048]{2,1,0:T(8,128)(2,1)S(1)}, u32[]{:S(2)}, u32[]{:S(2)}) collective-permute-start(bf16[2,32,2048]{2,1,0:T(8,128)(2,1)S(1)} %pad_maximum_fusion.5), channel_id=1, source_target_pairs={{0,16},{1,17},{2,18},{3,19},{4,20},{5,21},{6,22},{7,23},{8,24},{9,... | collective-permute-start | bytes 786440 | tf_op jit(solution)/shard_map/ppermute | solution.py:30
  22.4 7.3 %collective-permute-start.21 = (bf16[2,32,2048]{2,1,0:T(8,128)(2,1)S(1)}, bf16[2,32,2048]{2,1,0:T(8,128)(2,1)S(1)}, u32[]{:S(2)}, u32[]{:S(2)}) collective-permute-start(bf16[2,32,2048]{2,1,0:T(8,128)(2,1)S(1)} %pad_maximum_fusion.6), channel_id=1, source_target_pairs={{0,8},{1,9},{2,10},{3,11},{4,12},{5,13},{6,14},{7,15},{8,0},{9,1},... | collective-permute-start | bytes 786440 | tf_op jit(solution)/shard_map/ppermute | solution.py:30
  22.7 48.9 %collective-permute-start.12 = (bf16[2,128,2048]{2,1,0:T(8,128)(2,1)S(1)}, bf16[2,128,2048]{2,1,0:T(8,128)(2,1)S(1)}, u32[]{:S(2)}, u32[]{:S(2)}) collective-permute-start(bf16[2,128,2048]{2,1,0:T(8,128)(2,1)S(1)} %pad_maximum_fusion.4.refs_5_.refs_6_.refs_33_.refs_17_), channel_id=1, source_target_pairs={{0,48},{1,49},{2,50},{3,51},{4,52},{5,53},{6,54},{7,55},{8,56},{9,... | collective-permute-start | bytes 3145736 | tf_op jit(solution)/shard_map/ppermute | solution.py:30
  25.1 9.9 %collective-permute-start.20 = (bf16[2,32,2048]{2,1,0:T(8,128)(2,1)S(1)}, bf16[2,32,2048]{2,1,0:T(8,128)(2,1)S(1)}, u32[]{:S(2)}, u32[]{:S(2)}) collective-permute-start(bf16[2,32,2048]{2,1,0:T(8,128)(2,1)S(1)} %collective-permute-done.17), channel_id=1, source_target_pairs={{0,32},{1,33},{2,34},{3,35},{4,36},{5,37},{6,38},{7,39},{8,40},{9,... | collective-permute-start | bytes 786440 | tf_op jit(solution)/shard_map/ppermute | solution.py:30
  25.1 31.6 %collective-permute-start.19 = (bf16[2,32,2048]{2,1,0:T(8,128)(2,1)S(1)}, bf16[2,32,2048]{2,1,0:T(8,128)(2,1)S(1)}, u32[]{:S(2)}, u32[]{:S(2)}) collective-permute-start(bf16[2,32,2048]{2,1,0:T(8,128)(2,1)S(1)} %collective-permute-done.17), channel_id=1, source_target_pairs={{0,48},{1,49},{2,50},{3,51},{4,52},{5,53},{6,54},{7,55},{8,56},{9,... | collective-permute-start | bytes 786440 | tf_op jit(solution)/shard_map/ppermute | solution.py:30
  29.6 31.5 %collective-permute-start.18 = (bf16[2,32,2048]{2,1,0:T(8,128)(2,1)S(1)}, bf16[2,32,2048]{2,1,0:T(8,128)(2,1)S(1)}, u32[]{:S(2)}, u32[]{:S(2)}) collective-permute-start(bf16[2,32,2048]{2,1,0:T(8,128)(2,1)S(1)} %collective-permute-done.17), channel_id=1, source_target_pairs={{0,16},{1,17},{2,18},{3,19},{4,20},{5,21},{6,22},{7,23},{8,24},{9,... | collective-permute-start | bytes 786440 | tf_op jit(solution)/shard_map/ppermute | solution.py:30
  29.6 31.5 %collective-permute-start.24 = (bf16[2,32,2048]{2,1,0:T(8,128)(2,1)S(1)}, bf16[2,32,2048]{2,1,0:T(8,128)(2,1)S(1)}, u32[]{:S(2)}, u32[]{:S(2)}) collective-permute-start(bf16[2,32,2048]{2,1,0:T(8,128)(2,1)S(1)} %collective-permute-done.21), channel_id=1, source_target_pairs={{0,4},{1,5},{2,6},{3,7},{4,0},{5,1},{6,2},{7,3},{8,12},{9,13},{10,... | collective-permute-start | bytes 786440 | tf_op jit(solution)/shard_map/ppermute | solution.py:30
  35.0 33.6 %collective-permute-start.2 = (bf16[128,2048]{1,0:T(8,128)(2,1)S(1)}, bf16[128,2048]{1,0:T(8,128)(2,1)S(1)}, u32[]{:S(2)}, u32[]{:S(2)}) collective-permute-start(bf16[128,2048]{1,0:T(8,128)(2,1)S(1)} %bitcast_convert_fusion), channel_id=1, source_target_pairs={{0,1},{1,0},{2,3},{3,2},{4,5},{5,4},{6,7},{7,6},{8,9},{9,8},{10,11... | collective-permute-start | bytes 1572872 | tf_op jit(solution)/shard_map/ppermute | solution.py:30
  56.7 8.1 %collective-permute-start.23 = (bf16[2,32,2048]{2,1,0:T(8,128)(2,1)S(1)}, bf16[2,32,2048]{2,1,0:T(8,128)(2,1)S(1)}, u32[]{:S(2)}, u32[]{:S(2)}) collective-permute-start(bf16[2,32,2048]{2,1,0:T(8,128)(2,1)S(1)} %collective-permute-done.21), channel_id=1, source_target_pairs={{0,6},{1,7},{2,0},{3,1},{4,2},{5,3},{6,4},{7,5},{8,14},{9,15},{10,... | collective-permute-start | bytes 786440 | tf_op jit(solution)/shard_map/ppermute | solution.py:30
  61.1 6.8 %collective-permute-start.22 = (bf16[2,32,2048]{2,1,0:T(8,128)(2,1)S(1)}, bf16[2,32,2048]{2,1,0:T(8,128)(2,1)S(1)}, u32[]{:S(2)}, u32[]{:S(2)}) collective-permute-start(bf16[2,32,2048]{2,1,0:T(8,128)(2,1)S(1)} %collective-permute-done.21), channel_id=1, source_target_pairs={{0,2},{1,3},{2,4},{3,5},{4,6},{5,7},{6,0},{7,1},{8,10},{9,11},{10,... | collective-permute-start | bytes 786440 | tf_op jit(solution)/shard_map/ppermute | solution.py:30
  61.2 8.3 %collective-permute-start.1 = (bf16[2048,128]{1,0:T(8,128)(2,1)S(1)}, bf16[2048,128]{1,0:T(8,128)(2,1)S(1)}, u32[]{:S(2)}, u32[]{:S(2)}) collective-permute-start(bf16[2048,128]{1,0:T(8,128)(2,1)S(1)} %get-tuple-element.138), channel_id=1, source_target_pairs={{0,1},{1,0},{2,3},{3,2},{4,5},{5,4},{6,7},{7,6},{8,9},{9,8},{10,11... | collective-permute-start | bytes 1572872 | tf_op jit(solution)/shard_map/ppermute | solution.py:30
  64.8 24.0 %collective-permute-start.11 = (bf16[2,128,2048]{2,1,0:T(8,128)(2,1)S(1)}, bf16[2,128,2048]{2,1,0:T(8,128)(2,1)S(1)}, u32[]{:S(2)}, u32[]{:S(2)}) collective-permute-start(bf16[2,128,2048]{2,1,0:T(8,128)(2,1)S(1)} %pad_maximum_fusion.4.refs_5_.refs_6_.refs_33_.refs_17_), channel_id=1, source_target_pairs={{0,16},{1,17},{2,18},{3,19},{4,20},{5,21},{6,22},{7,23},{8,24},{9,... | collective-permute-start | bytes 3145736 | tf_op jit(solution)/shard_map/ppermute | solution.py:30
  67.9 22.0 %collective-permute-start.10 = (bf16[2,128,2048]{2,1,0:T(8,128)(2,1)S(1)}, bf16[2,128,2048]{2,1,0:T(8,128)(2,1)S(1)}, u32[]{:S(2)}, u32[]{:S(2)}) collective-permute-start(bf16[2,128,2048]{2,1,0:T(8,128)(2,1)S(1)} %pad_maximum_fusion.3.refs_3_.refs_4_.refs_32_.refs_16_), channel_id=1, source_target_pairs={{0,6},{1,7},{2,0},{3,1},{4,2},{5,3},{6,4},{7,5},{8,14},{9,15},{10,... | collective-permute-start | bytes 3145736 | tf_op jit(solution)/shard_map/ppermute | solution.py:30
  68.7 28.5 %collective-permute-start.9 = (bf16[2,128,2048]{2,1,0:T(8,128)(2,1)S(1)}, bf16[2,128,2048]{2,1,0:T(8,128)(2,1)S(1)}, u32[]{:S(2)}, u32[]{:S(2)}) collective-permute-start(bf16[2,128,2048]{2,1,0:T(8,128)(2,1)S(1)} %pad_maximum_fusion.3.refs_3_.refs_4_.refs_32_.refs_16_), channel_id=1, source_target_pairs={{0,2},{1,3},{2,4},{3,5},{4,6},{5,7},{6,0},{7,1},{8,10},{9,11},{10,... | collective-permute-start | bytes 3145736 | tf_op jit(solution)/shard_map/ppermute | solution.py:30
  69.5 81.9 %copy-start.4 = (bf16[2,128,2048]{2,1,0:T(8,128)(2,1)}, bf16[2,128,2048]{2,1,0:T(8,128)(2,1)S(1)}, u32[]{:S(2)}) copy-start(bf16[2,128,2048]{2,1,0:T(8,128)(2,1)S(1)} %constant_dynamic-update-slice_fusion.refs_3_.refs_4_.refs_40_.refs_24_) | copy-start | bytes 3145732
  69.5 42.3 %collective-permute-start.26 = (bf16[2,128,2048]{2,1,0:T(8,128)(2,1)S(1)}, bf16[2,128,2048]{2,1,0:T(8,128)(2,1)S(1)}, u32[]{:S(2)}, u32[]{:S(2)}) collective-permute-start(bf16[2,128,2048]{2,1,0:T(8,128)(2,1)S(1)} %constant_dynamic-update-slice_fusion.refs_3_.refs_4_.refs_40_.refs_24_), channel_id=1, source_target_pairs={{0,6},{1,7},{2,0},{3,1},{4,2},{5,3},{6,4},{7,5},{8,14},{9,15},{10,... | collective-permute-start | bytes 3145736 | tf_op jit(solution)/shard_map/ppermute | solution.py:30
  71.5 42.4 %collective-permute-start.25 = (bf16[2,128,2048]{2,1,0:T(8,128)(2,1)S(1)}, bf16[2,128,2048]{2,1,0:T(8,128)(2,1)S(1)}, u32[]{:S(2)}, u32[]{:S(2)}) collective-permute-start(bf16[2,128,2048]{2,1,0:T(8,128)(2,1)S(1)} %constant_dynamic-update-slice_fusion.refs_3_.refs_4_.refs_40_.refs_24_), channel_id=1, source_target_pairs={{0,2},{1,3},{2,4},{3,5},{4,6},{5,7},{6,0},{7,1},{8,10},{9,11},{10,... | collective-permute-start | bytes 3145736 | tf_op jit(solution)/shard_map/ppermute | solution.py:30
  88.7 27.5 %collective-permute-start.28 = (bf16[2,128,2048]{2,1,0:T(8,128)(2,1)S(1)}, bf16[2,128,2048]{2,1,0:T(8,128)(2,1)S(1)}, u32[]{:S(2)}, u32[]{:S(2)}) collective-permute-start(bf16[2,128,2048]{2,1,0:T(8,128)(2,1)S(1)} %constant_dynamic-update-slice_fusion.4.refs_5_.refs_6_.refs_41_.refs_25_), channel_id=1, source_target_pairs={{0,48},{1,49},{2,50},{3,51},{4,52},{5,53},{6,54},{7,55},{8,56},{9,... | collective-permute-start | bytes 3145736 | tf_op jit(solution)/shard_map/ppermute | solution.py:30
  89.9 8.8 %collective-permute-start = (bf16[2048,128]{1,0:T(8,128)(2,1)S(1)}, bf16[2048,128]{1,0:T(8,128)(2,1)S(1)}, u32[]{:S(2)}, u32[]{:S(2)}) collective-permute-start(bf16[2048,128]{1,0:T(8,128)(2,1)S(1)} %get-tuple-element.139), channel_id=1, source_target_pairs={{0,1},{1,0},{2,3},{3,2},{4,5},{5,4},{6,7},{7,6},{8,9},{9,8},{10,11... | collective-permute-start | bytes 1572872 | tf_op jit(solution)/shard_map/ppermute | solution.py:30
  97.2 25.3 %collective-permute-start.27 = (bf16[2,128,2048]{2,1,0:T(8,128)(2,1)S(1)}, bf16[2,128,2048]{2,1,0:T(8,128)(2,1)S(1)}, u32[]{:S(2)}, u32[]{:S(2)}) collective-permute-start(bf16[2,128,2048]{2,1,0:T(8,128)(2,1)S(1)} %constant_dynamic-update-slice_fusion.4.refs_5_.refs_6_.refs_41_.refs_25_), channel_id=1, source_target_pairs={{0,16},{1,17},{2,18},{3,19},{4,20},{5,21},{6,22},{7,23},{8,24},{9,... | collective-permute-start | bytes 3145736 | tf_op jit(solution)/shard_map/ppermute | solution.py:30
  98.7 26.9 %collective-permute-start.16 = (bf16[1,128,2048]{2,1,0:T(8,128)(2,1)S(1)}, bf16[1,128,2048]{2,1,0:T(8,128)(2,1)S(1)}, u32[]{:S(2)}, u32[]{:S(2)}) collective-permute-start(bf16[1,128,2048]{2,1,0:T(8,128)(2,1)S(1)} %slice.53), channel_id=1, source_target_pairs={{0,48},{1,49},{2,50},{3,51},{4,52},{5,53},{6,54},{7,55},{8,56},{9,... | collective-permute-start | bytes 1572872 | tf_op jit(solution)/shard_map/ppermute | solution.py:30
  111.8 30.0 %copy-start = (bf16[2,128,2048]{2,1,0:T(8,128)(2,1)}, bf16[2,128,2048]{2,1,0:T(8,128)(2,1)S(1)}, u32[]{:S(2)}) copy-start(bf16[2,128,2048]{2,1,0:T(8,128)(2,1)S(1)} %collective-permute-done.26.refs_5_.refs_6_.refs_43_.refs_27_) | copy-start | bytes 3145732
  111.8 21.9 %collective-permute-start.15 = (bf16[1,128,2048]{2,1,0:T(8,128)(2,1)S(1)}, bf16[1,128,2048]{2,1,0:T(8,128)(2,1)S(1)}, u32[]{:S(2)}, u32[]{:S(2)}) collective-permute-start(bf16[1,128,2048]{2,1,0:T(8,128)(2,1)S(1)} %slice.52), channel_id=1, source_target_pairs={{0,16},{1,17},{2,18},{3,19},{4,20},{5,21},{6,22},{7,23},{8,24},{9,... | collective-permute-start | bytes 1572872 | tf_op jit(solution)/shard_map/ppermute | solution.py:30
  113.9 37.5 %copy-start.1 = (bf16[2,128,2048]{2,1,0:T(8,128)(2,1)}, bf16[2,128,2048]{2,1,0:T(8,128)(2,1)S(1)}, u32[]{:S(2)}) copy-start(bf16[2,128,2048]{2,1,0:T(8,128)(2,1)S(1)} %collective-permute-done.25.refs_3_.refs_4_.refs_42_.refs_26_) | copy-start | bytes 3145732
  113.9 22.6 %collective-permute-start.14 = (bf16[1,128,2048]{2,1,0:T(8,128)(2,1)S(1)}, bf16[1,128,2048]{2,1,0:T(8,128)(2,1)S(1)}, u32[]{:S(2)}, u32[]{:S(2)}) collective-permute-start(bf16[1,128,2048]{2,1,0:T(8,128)(2,1)S(1)} %slice.51), channel_id=1, source_target_pairs={{0,6},{1,7},{2,0},{3,1},{4,2},{5,3},{6,4},{7,5},{8,14},{9,15},{10,... | collective-permute-start | bytes 1572872 | tf_op jit(solution)/shard_map/ppermute | solution.py:30
  116.2 25.6 %copy-start.2 = (bf16[2,128,2048]{2,1,0:T(8,128)(2,1)}, bf16[2,128,2048]{2,1,0:T(8,128)(2,1)S(1)}, u32[]{:S(2)}) copy-start(bf16[2,128,2048]{2,1,0:T(8,128)(2,1)S(1)} %collective-permute-done.28.refs_9_.refs_10_.refs_45_.refs_29_) | copy-start | bytes 3145732
  116.2 28.2 %collective-permute-start.13 = (bf16[1,128,2048]{2,1,0:T(8,128)(2,1)S(1)}, bf16[1,128,2048]{2,1,0:T(8,128)(2,1)S(1)}, u32[]{:S(2)}, u32[]{:S(2)}) collective-permute-start(bf16[1,128,2048]{2,1,0:T(8,128)(2,1)S(1)} %slice.50), channel_id=1, source_target_pairs={{0,2},{1,3},{2,4},{3,5},{4,6},{5,7},{6,0},{7,1},{8,10},{9,11},{10,... | collective-permute-start | bytes 1572872 | tf_op jit(solution)/shard_map/ppermute | solution.py:30
  122.5 19.4 %copy-start.3 = (bf16[2,128,2048]{2,1,0:T(8,128)(2,1)}, bf16[2,128,2048]{2,1,0:T(8,128)(2,1)S(1)}, u32[]{:S(2)}) copy-start(bf16[2,128,2048]{2,1,0:T(8,128)(2,1)S(1)} %collective-permute-done.27.refs_7_.refs_8_.refs_44_.refs_28_) | copy-start | bytes 3145732
  124.4 21.4 %collective-permute-start.32 = (bf16[1,128,2048]{2,1,0:T(8,128)(2,1)}, bf16[1,128,2048]{2,1,0:T(8,128)(2,1)S(1)}, u32[]{:S(2)}, u32[]{:S(2)}) collective-permute-start(bf16[1,128,2048]{2,1,0:T(8,128)(2,1)} %slice.57), channel_id=1, source_target_pairs={{0,48},{1,49},{2,50},{3,51},{4,52},{5,53},{6,54},{7,55},{8,56},{9,... | collective-permute-start | bytes 1572872 | tf_op jit(solution)/shard_map/ppermute | solution.py:30
  125.6 18.8 %copy-start.6 = (bf16[1,128,2048]{2,1,0:T(8,128)(2,1)}, bf16[1,128,2048]{2,1,0:T(8,128)(2,1)S(1)}, u32[]{:S(2)}) copy-start(bf16[1,128,2048]{2,1,0:T(8,128)(2,1)S(1)} %collective-permute-done.16.refs_6_.refs_23_) | copy-start | bytes 1572868
  125.6 20.2 %collective-permute-start.31 = (bf16[1,128,2048]{2,1,0:T(8,128)(2,1)}, bf16[1,128,2048]{2,1,0:T(8,128)(2,1)S(1)}, u32[]{:S(2)}, u32[]{:S(2)}) collective-permute-start(bf16[1,128,2048]{2,1,0:T(8,128)(2,1)} %slice.56), channel_id=1, source_target_pairs={{0,16},{1,17},{2,18},{3,19},{4,20},{5,21},{6,22},{7,23},{8,24},{9,... | collective-permute-start | bytes 1572872 | tf_op jit(solution)/shard_map/ppermute | solution.py:30
  133.7 13.2 %collective-permute-start.30 = (bf16[1,128,2048]{2,1,0:T(8,128)(2,1)S(1)}, bf16[1,128,2048]{2,1,0:T(8,128)(2,1)S(1)}, u32[]{:S(2)}, u32[]{:S(2)}) collective-permute-start(bf16[1,128,2048]{2,1,0:T(8,128)(2,1)S(1)} %slice.55), channel_id=1, source_target_pairs={{0,6},{1,7},{2,0},{3,1},{4,2},{5,3},{6,4},{7,5},{8,14},{9,15},{10,... | collective-permute-start | bytes 1572872 | tf_op jit(solution)/shard_map/ppermute | solution.py:30
  136.6 13.4 %collective-permute-start.29 = (bf16[1,128,2048]{2,1,0:T(8,128)(2,1)S(1)}, bf16[1,128,2048]{2,1,0:T(8,128)(2,1)S(1)}, u32[]{:S(2)}, u32[]{:S(2)}) collective-permute-start(bf16[1,128,2048]{2,1,0:T(8,128)(2,1)S(1)} %slice.54), channel_id=1, source_target_pairs={{0,2},{1,3},{2,4},{3,5},{4,6},{5,7},{6,0},{7,1},{8,10},{9,11},{10,... | collective-permute-start | bytes 1572872 | tf_op jit(solution)/shard_map/ppermute | solution.py:30
  160.8 18.1 %collective-permute-start.35 = (bf16[128,2048]{1,0:T(8,128)(2,1)S(1)}, bf16[128,2048]{1,0:T(8,128)(2,1)S(1)}, u32[]{:S(2)}, u32[]{:S(2)}) collective-permute-start(bf16[128,2048]{1,0:T(8,128)(2,1)S(1)} %get-tuple-element.127), channel_id=1, source_target_pairs={{0,1},{1,0},{2,3},{3,2},{4,5},{5,4},{6,7},{7,6},{8,9},{9,8},{10,11... | collective-permute-start | bytes 1572872 | tf_op jit(solution)/shard_map/ppermute | solution.py:30
  164.5 14.5 %copy-start.25 = (bf16[1,128,2048]{2,1,0:T(8,128)(2,1)S(1)}, bf16[1,128,2048]{2,1,0:T(8,128)(2,1)}, u32[]{:S(2)}) copy-start(bf16[1,128,2048]{2,1,0:T(8,128)(2,1)} %param.19) | copy-start | bytes 1572868
  164.5 14.5 %copy-start.26 = (bf16[1,128,2048]{2,1,0:T(8,128)(2,1)S(1)}, bf16[1,128,2048]{2,1,0:T(8,128)(2,1)}, u32[]{:S(2)}) copy-start(bf16[1,128,2048]{2,1,0:T(8,128)(2,1)} %param.17) | copy-start | bytes 1572868
  164.5 19.8 %copy-start.22 = (bf16[1,2,2048,128]{3,2,1,0:T(8,128)(2,1)S(1)}, bf16[1,2,2048,128]{3,2,1,0:T(8,128)(2,1)}, u32[]{:S(2)}) copy-start(bf16[1,2,2048,128]{3,2,1,0:T(8,128)(2,1)} %param.18) | copy-start | bytes 3145732
  164.5 19.8 %copy-start.23 = (bf16[1,2,2048,128]{3,2,1,0:T(8,128)(2,1)S(1)}, bf16[1,2,2048,128]{3,2,1,0:T(8,128)(2,1)}, u32[]{:S(2)}) copy-start(bf16[1,2,2048,128]{3,2,1,0:T(8,128)(2,1)} %param.16) | copy-start | bytes 3145732
  178.9 5.4 %collective-permute-start.33 = (bf16[2,2048,128]{2,1,0:T(8,128)(2,1)S(1)}, bf16[2,2048,128]{2,1,0:T(8,128)(2,1)S(1)}, u32[]{:S(2)}, u32[]{:S(2)}) collective-permute-start(bf16[2,2048,128]{2,1,0:T(8,128)(2,1)S(1)} %get-tuple-element.109), channel_id=1, source_target_pairs={{0,1},{1,0},{2,3},{3,2},{4,5},{5,4},{6,7},{7,6},{8,9},{9,8},{10,11... | collective-permute-start | bytes 3145736 | tf_op jit(solution)/shard_map/ppermute | solution.py:30
  181.0 15.2 %collective-permute-start.36 = (bf16[128,2048]{1,0:T(8,128)(2,1)S(1)}, bf16[128,2048]{1,0:T(8,128)(2,1)S(1)}, u32[]{:S(2)}, u32[]{:S(2)}) collective-permute-start(bf16[128,2048]{1,0:T(8,128)(2,1)S(1)} %get-tuple-element.136), channel_id=1, source_target_pairs={{0,64},{64,0},{1,65},{65,1},{2,66},{66,2},{3,67},{67,3},{4,68},{68... | collective-permute-start | bytes 1572872 | tf_op jit(solution)/shard_map/ppermute | solution.py:259
  187.8 30.8 %copy-start.20 = (f32[2,2048,128]{2,1,0:T(8,128)S(1)}, f32[2,2048,128]{2,1,0:T(8,128)}, u32[]{:S(2)}) copy-start(f32[2,2048,128]{2,1,0:T(8,128)} %param.22) | copy-start | bytes 6291460
  187.8 30.8 %collective-permute-start.34 = (bf16[2,2048,128]{2,1,0:T(8,128)(2,1)S(1)}, bf16[2,2048,128]{2,1,0:T(8,128)(2,1)S(1)}, u32[]{:S(2)}, u32[]{:S(2)}) collective-permute-start(bf16[2,2048,128]{2,1,0:T(8,128)(2,1)S(1)} %get-tuple-element.133), channel_id=1, source_target_pairs={{0,64},{64,0},{1,65},{65,1},{2,66},{66,2},{3,67},{67,3},{4,68},{68... | collective-permute-start | bytes 3145736 | tf_op jit(solution)/shard_map/ppermute | solution.py:267
  (16 other events, 119.9 us)

commit v2 on v0

v2 whole, which is shorter than its diff:
```python
import functools

import jax
import jax.numpy as jnp
from jax import lax
from jax.experimental import pallas as pl
from jax.experimental.pallas import tpu as pltpu
from jax.sharding import PartitionSpec as P

beta_one = 0.9
beta_two = 0.95
bias_one = 1.0 - 0.9**64
bias_two = 1.0 - 0.95**64
inner_rate = 0.004
decay_rate = 0.1
epsilon_adam = 1e-08
momentum_keep = 0.9
outer_rate = 0.7

AXES = {"x": (4, 16), "z": (2, 8), "y": (4, 2), "core": (2, 1)}
FSDP = 64
BF16 = jnp.bfloat16
F32 = jnp.float32
VMEM = pl.BlockSpec(memory_space=pltpu.VMEM)
PARAMS = pltpu.CompilerParams(vmem_limit_bytes=12 * 1024 * 1024)


def move(value, axis, target):
    size, stride = AXES[axis]
    pairs = []
    for i in range(FSDP):
        place = (i // stride) % size
        pairs.append((i, i + (target(place) - place) * stride))
    return lax.ppermute(value, "fsdp", pairs)


def up_y(value):
    return move(value, "y", lambda p: (p + 1) % 4)


def down_y(value):
    return move(value, "y", lambda p: (p + 3) % 4)


def swap_z(value):
    return move(value, "z", lambda p: 1 - p)


def swap_core(value):
    return move(value, "core", lambda p: 1 - p)


def far_x(value):
    return move(value, "x", lambda p: (p + 2) % 4)


def near_x(value):
    return move(value, "x", lambda p: p ^ 1)


def swap_replica(value):
    return lax.ppermute(value, "replica", [(0, 1), (1, 0)])


def struct(shape, dtype):
    return jax.ShapeDtypeStruct(shape, dtype)


def weights_kernel(in_ref, down_ref, out_ref):
    out_ref[0] = in_ref[0, 0].astype(BF16).T
    out_ref[1] = in_ref[0, 1].astype(BF16).T
    out_ref[2] = down_ref[0].astype(BF16)


def own_weights(params_in, params_down):
    depth, width = params_in.shape[2:]
    return pl.pallas_call(
        weights_kernel,
        in_specs=[VMEM] * 2,
        out_specs=VMEM,
        out_shape=struct((3, width, depth), BF16),
        cost_estimate=pl.CostEstimate(
            flops=depth * width * 3, bytes_accessed=depth * width * 18, transcendentals=0
        ),
        compiler_params=PARAMS,
        name="own_weights",
    )(params_in, params_down)


def forward_kernel(planes, in_ref, down_ref, *refs):
    count = len(planes)
    pieces, outs = refs[: 2 * count], refs[2 * count :]
    hidden_ref, dgate_ref, dup_ref, rows_ref, cots_ref = outs
    start = 0
    for k, (x_plane, c_plane) in enumerate(planes):
        rows = pieces[2 * k].shape[1]
        rows_ref[start : start + rows] = pieces[2 * k][x_plane]
        cots_ref[start : start + rows] = pieces[2 * k + 1][c_plane]
        start += rows
    width = down_ref.shape[0]
    sides = (((1,), (1,)), ((), ()))
    both = lax.dot_general(in_ref[...], rows_ref[...], sides, preferred_element_type=F32)
    dhidden = lax.dot_general(down_ref[...], cots_ref[...], sides, preferred_element_type=F32)
    gate_pre, up_proj = both[:width], both[width:]
    sig = 1.0 / (1.0 + jnp.exp(-gate_pre))
    silu = gate_pre * sig
    hidden_ref[...] = (silu * up_proj).astype(BF16)
    dgate_ref[...] = (dhidden * up_proj * (sig * (1.0 + gate_pre * (1.0 - sig)))).astype(BF16)
    dup_ref[...] = (dhidden * silu).astype(BF16)


def forward(weights_in, weights_down, pieces):
    width, depth = weights_down.shape
    total = sum(p[0].shape[1] for p in pieces)
    operands = [a for x, _, c, _ in pieces for a in (x, c)]
    return pl.pallas_call(
        functools.partial(forward_kernel, [(p[1], p[3]) for p in pieces]),
        in_specs=[VMEM] * (2 + len(operands)),
        out_specs=[VMEM] * 5,
        out_shape=[struct((width, total), BF16)] * 3 + [struct((total, depth), BF16)] * 2,
        cost_estimate=pl.CostEstimate(
            flops=2 * total * depth * 3 * width,
            bytes_accessed=total * depth * 8 + 6 * width * depth,
            transcendentals=total * width,
        ),
        compiler_params=PARAMS,
        name="forward",
    )(weights_in, weights_down, *operands)


def gradient_kernel(count, *refs):
    left, right = refs[:count], refs[count : 2 * count]
    own_ref, near_ref, send_ref, all_ref = refs[2 * count :]
    quarter, depth = own_ref.shape
    start = 0
    for piece in left:
        all_ref[:, start : start + piece.shape[1]] = piece[...]
        start += piece.shape[1]
    tile = 256
    for i in range(depth // tile):
        at = slice(i * tile, (i + 1) * tile)
        columns = jnp.concatenate([piece[:, at] for piece in right], axis=0)
        total = jnp.dot(all_ref[...], columns, preferred_element_type=F32)
        own_ref[:, at] = total[:quarter]
        send_ref[0, :, at] = total[quarter : 2 * quarter].astype(BF16)
        near_ref[:, at] = total[2 * quarter : 3 * quarter]
        send_ref[1, :, at] = total[3 * quarter :].astype(BF16)


def gradient(left, right):
    width = left[0].shape[0]
    depth = right[0].shape[1]
    rows = sum(r.shape[0] for r in right)
    quarter = width // 4
    return pl.pallas_call(
        functools.partial(gradient_kernel, len(left)),
        in_specs=[VMEM] * (2 * len(left)),
        out_specs=[VMEM] * 3,
        out_shape=[
            struct((quarter, depth), F32),
            struct((quarter, depth), F32),
            struct((2, quarter, depth), BF16),
        ],
        scratch_shapes=[pltpu.VMEM((width, rows), BF16)],
        cost_estimate=pl.CostEstimate(
            flops=2 * rows * depth * width,
            bytes_accessed=rows * depth * 2 + rows * width * 2 + width * depth * 3,
            transcendentals=0,
        ),
        compiler_params=PARAMS,
        name="gradient",
    )(*left, *right)


def adamw(param, grad, first, second):
    first_new = beta_one * first.astype(F32) + (1.0 - beta_one) * grad
    second_new = beta_two * second.astype(F32) + (1.0 - beta_two) * grad * grad
    update = first_new / bias_one / (jnp.sqrt(second_new / bias_two) + epsilon_adam)
    param_new = param - inner_rate * (update + decay_rate * param)
    return (param_new, first_new.astype(BF16), second_new.astype(BF16))


def inner_kernel(which, *refs):
    own, core, near, param, first, second, base = refs[:7]
    first_out, second_out, delta_out = refs[-3:]
    at = pl.ds(pl.multiple_of(pl.program_id(0) * TILE, TILE), TILE)
    grad = own[:, at] + core[0, :, at].astype(F32) + near[:, at].astype(F32)
    if which is None:
        place, shared = (0, slice(None), at), (slice(None), at)
    else:
        grad = grad.T
        place, shared = (0, which, at), (which, at)
    new, first_new, second_new = adamw(param[place], grad, first[place], second[place])
    first_out[...] = first_new.reshape(first_out.shape)
    second_out[...] = second_new.reshape(second_out.shape)
    delta_out[...] = (base[shared] - new).astype(BF16)


TILE = 512


def inner_step(own, core, near, param, first, second, base, which=None, earlier=()):
    quarter, depth = own.shape
    if which is not None:
        state = pl.BlockSpec((1, 1, TILE, quarter), lambda i: (0, which, i, 0))
        delta = pl.BlockSpec((TILE, quarter), lambda i: (i, 0))
        delta_shape = (depth, quarter)
    else:
        state = pl.BlockSpec((1, quarter, TILE), lambda i: (0, 0, i))
        delta = pl.BlockSpec((quarter, TILE), lambda i: (0, i))
        delta_shape = (quarter, depth)
    return pl.pallas_call(
        functools.partial(inner_kernel, which),
        grid=(depth // TILE,),
        in_specs=[VMEM] * 7 + [pl.BlockSpec(memory_space=pl.ANY)] * len(earlier),
        out_specs=[state, state, delta],
        out_shape=[struct(first.shape, BF16), struct(second.shape, BF16), struct(delta_shape, BF16)],
        input_output_aliases={7 + k: k for k in range(len(earlier))},
        cost_estimate=pl.CostEstimate(
            flops=20 * quarter * depth, bytes_accessed=26 * quarter * depth, transcendentals=quarter * depth
        ),
        compiler_params=PARAMS,
        name="inner_step",
    )(own, core, near, param, first, second, base, *earlier)


def outer_kernel(which, *refs):
    own, other, base, outer = refs[:4]
    base_out, outer_out = refs[-2:]
    at = pl.ds(pl.multiple_of(pl.program_id(0) * TILE, TILE), TILE)
    if which is None:
        part = shared = (slice(None), at)
    else:
        part, shared = (at,), (which, at)
    grad = (own[part].astype(F32) + other[part].astype(F32)) / 2.0
    new_outer = momentum_keep * outer[shared] + grad
    outer_out[...] = new_outer.reshape(outer_out.shape)
    base_out[...] = (base[shared] - outer_rate * (grad + momentum_keep * new_outer)).reshape(base_out.shape)


def outer_step(own, other, base, outer, which=None, earlier=()):
    if which is not None:
        depth, quarter = own.shape
        shared = pl.BlockSpec((1, TILE, quarter), lambda i: (which, i, 0))
    else:
        quarter, depth = own.shape
        shared = pl.BlockSpec((quarter, TILE), lambda i: (0, i))
    return pl.pallas_call(
        functools.partial(outer_kernel, which),
        grid=(depth // TILE,),
        in_specs=[VMEM] * 4 + [pl.BlockSpec(memory_space=pl.ANY)] * len(earlier),
        out_specs=[shared, shared],
        out_shape=[struct(base.shape, F32), struct(outer.shape, F32)],
        input_output_aliases={4 + k: k for k in range(len(earlier))},
        cost_estimate=pl.CostEstimate(
            flops=8 * quarter * depth, bytes_accessed=20 * quarter * depth, transcendentals=0
        ),
        compiler_params=PARAMS,
        name="outer_step",
    )(own, other, base, outer, *earlier)


def after(value, *others):
    return lax.optimization_barrier((value, others))[0]


def y_ring(rows):
    low, high = up_y(rows), down_y(rows)
    return low, high, up_y(low[:1]), down_y(high[1:])


def local(
    inputs,
    cotangent,
    params_in,
    params_down,
    first_in,
    first_down,
    second_in,
    second_down,
    base_in,
    base_down,
    outer_in,
    outer_down,
):
    own = jnp.concatenate([inputs, cotangent])
    by_x = far_x(own)
    by_z = swap_z(own)
    low_own, high_own, far_own_x, far_own_c = y_ring(own)
    mine = own_weights(params_in, params_down)
    core = swap_core(mine)
    near = near_x(mine)
    both = swap_core(near)
    low_x, high_x, far_x_x, far_x_c = y_ring(by_x)
    by_xz = swap_z(by_x)
    low_z, high_z, far_z_x, far_z_c = y_ring(after(by_z, by_xz))
    low_xz, high_xz = swap_z(low_x), swap_z(high_x)
    far_xz_x, far_xz_c = up_y(low_xz[:1]), down_y(high_xz[1:])

    weights_in = jnp.concatenate([w[k] for k in range(2) for w in (mine, core, near, both)])
    weights_down = jnp.concatenate([w[2] for w in (mine, core, near, both)])

    def full(piece):
        return (piece, 0, piece, 1)

    def parted(x_piece, c_piece):
        return (x_piece, 0, c_piece, 0)

    groups = [
        [full(own), full(low_own), full(high_own), parted(far_own_x, far_own_c)],
        [full(by_x), full(low_x), full(high_x), parted(far_x_x, far_x_c)],
        [full(by_z), full(low_z), full(high_z), full(by_xz)],
        [parted(far_z_x, far_z_c), full(low_xz), full(high_xz), parted(far_xz_x, far_xz_c)],
    ]
    results = [forward(weights_in, weights_down, group) for group in groups]
    hidden, dgate, dup, rows, cots = [list(r) for r in zip(*results)]

    def summed(left, right):
        own_part, near_part, send = gradient(left, right)
        core_part = swap_core(send)
        near_part = near_x((near_part + core_part[1].astype(F32)).astype(BF16))
        return own_part, core_part, near_part

    sums_down = summed(hidden, cots)
    sums_gate = summed(dgate, rows)
    sums_up = summed(after(dup, sums_down[1]), rows)
    fdown, sdown, delta_down = inner_step(
        *sums_down, params_down, first_down, second_down, base_down
    )
    other_down = swap_replica(delta_down)
    fin, sin, delta_gate = inner_step(
        *sums_gate, params_in, first_in, second_in, base_in, which=0
    )
    other_gate = swap_replica(delta_gate)
    fin, sin, delta_up = inner_step(
        *sums_up, params_in, first_in, second_in, base_in, which=1, earlier=(fin, sin)
    )
    other_up = swap_replica(delta_up)

    new_base_down, new_outer_down = outer_step(delta_down, other_down, base_down, outer_down)
    new_in = outer_step(delta_gate, other_gate, base_in, outer_in, which=0)
    new_base_in, new_outer_in = outer_step(
        delta_up, other_up, base_in, outer_in, which=1, earlier=new_in
    )
    return (new_base_in, new_base_down, new_outer_in, new_outer_down, fin, fdown, sin, sdown)


def solution(mesh):
    in_specs = (
        P("replica", "fsdp", None),
        P("replica", "fsdp", None),
        P("replica", None, None, "fsdp"),
        P("replica", "fsdp", None),
        P("replica", None, None, "fsdp"),
        P("replica", "fsdp", None),
        P("replica", None, None, "fsdp"),
        P("replica", "fsdp", None),
        P(None, None, "fsdp"),
        P("fsdp", None),
        P(None, None, "fsdp"),
        P("fsdp", None),
    )
    out_specs = (
        P(None, None, "fsdp"),
        P("fsdp", None),
        P(None, None, "fsdp"),
        P("fsdp", None),
        P("replica", None, None, "fsdp"),
        P("replica", "fsdp", None),
        P("replica", None, None, "fsdp"),
        P("replica", "fsdp", None),
    )
    return jax.shard_map(local, mesh=mesh, in_specs=in_specs, out_specs=out_specs, check_vma=False)
```

time: 411 us -> 158 us (0.38)
  waiting for transfers between devices: 310 us -> 73.1 us
  starting transfers between devices: 0.11 us -> 49.8 us
  matrix products: 47.7 us -> 0 us
  Pallas kernels: 0 us -> 27.4 us
  other arithmetic: 19.7 us -> 0.55 us
  local copies, waits for them, and re-layouts: 19.8 us -> 5.44 us
  between operations: 14 us -> 1.08 us
    all_gather x2 -> x0, waiting for transfers between devices: 225 us -> none  [the longest x1 118 us: local(): rows_in = lax.all_gather(inputs, 'fsdp', axis=1, tiled=True)]
    psum x1 -> x0, waiting for transfers between devices: 83.3 us -> none  [local(): total_in, total_down = lax.psum((delta_in, delta_down), 'replica')]
    ppermute x0 -> x31, waiting for transfers between devices: none -> 73.1 us  [the longest x28 65.3 us: move(): return lax.ppermute(value, 'fsdp', pairs)]
    ppermute x0 -> x31, starting transfers between devices: none -> 49.8 us  [the longest x28 40.1 us: move(): return lax.ppermute(value, 'fsdp', pairs)]
    dot_general x6 -> x0, matrix products: 47.7 us -> none  [the longest x3 23 us: contract_rows(): lax.dot_general(left, right, (((0,), (0,)), ((), ())), preferred_element_...]
    pallas_call x0 -> x14, Pallas kernels: none -> 27.4 us  [the longest x4 7.64 us: forward(): pl.pallas_call(functools.partial(forward_kernel, [(p[1], p[3]) for p in p...]
    unnamed x59 -> x32, local copies, waits for them, and re-layouts: 19.8 us -> 4.12 us
    sub x2 -> x0, other arithmetic: 8.58 us -> none  [the longest x1 5.38 us: local(): delta_in = base_in - new_in]
  transfers between devices with their start and end apart: 3 -> 31, of which waited for: 3 -> 14; matrix products, arithmetic and copies ran while one was open for 9% -> 1% of each run, Pallas kernels for 0% -> 14%
where the time goes in v2:
time: 158 us; the launch traced here: 157 us
  waiting for transfers between devices  73.1 us (46%)
  starting transfers between devices  49.8 us (32%)
  Pallas kernels  27.4 us (17%)
  local copies, waits for them, and re-layouts  5.44 us (3%)
    ppermute x28, waiting for transfers between devices, move(): return lax.ppermute(value, 'fsdp', pairs)  65.3 us
    ppermute x28, starting transfers between devices, move(): return lax.ppermute(value, 'fsdp', pairs)  40.1 us
    ppermute x3, starting transfers between devices, swap_replica(): return lax.ppermute(value, 'replica', [(0, 1), (1, 0)])  9.74 us
    ppermute x3, waiting for transfers between devices, swap_replica(): return lax.ppermute(value, 'replica', [(0, 1), (1, 0)])  7.79 us
    pallas_call x4, Pallas kernels, forward(): pl.pallas_call(functools.partial(forward_kernel, [(p[1], p[3]) for p in p...  7.64 us
    pallas_call x3, Pallas kernels, gradient(): pl.pallas_call(functools.partial(gradient_kernel, len(left)), in_specs=[V...  7 us
    pallas_call x3, Pallas kernels, inner_step(): pl.pallas_call(functools.partial(inner_kernel, which), grid=(depth // TIL...  6.81 us
    pallas_call x3, Pallas kernels, outer_step(): pl.pallas_call(functools.partial(outer_kernel, which), grid=(depth // TIL...  5.65 us
  transfers between devices with their start and end apart: 31, of which 14 were waited for; matrix products, arithmetic and copies ran while one was open for 1% of the time, Pallas kernels for 14%

profile of v2, /device:TPU:1, one launch (start us, length us, event | category | flops | bytes accessed | tf_op | source)
XLA Modules:
  0.0 157.4 jit_solution(10972350601561094811)
XLA Ops:
  1.6 1.0 constant_dynamic-update-slice_fusion.refs_0_.refs_1_
  2.6 3.7 %collective-permute-start.7 = (bf16[2,64,2048]{2,1,0:T(8,128)(2,1)S(1)}, bf16[2,64,2048]{2,1,0:T(8,128)(2,1)S(1)}, u32[]{:S(2)}, u32[]{:S(2)}) collective-permute-start(bf16[2,64,2048]{2,1,0:T(8,128)(2,1)S(1)} %constant_dynamic-update-slice_fusion.refs_0_.refs_1_), channel_id=1, source_target_pairs={{0,32},{1,33},{2,34},{3,35},{4,36},{5,37},{6,38},{7,39},{8,40},{9,... | collective-permute-start | bytes 1572872 | tf_op jit(solution)/shard_map/ppermute | solution.py:34
  6.2 1.6 %collective-permute-start.12 = (bf16[2,64,2048]{2,1,0:T(8,128)(2,1)S(1)}, bf16[2,64,2048]{2,1,0:T(8,128)(2,1)S(1)}, u32[]{:S(2)}, u32[]{:S(2)}) collective-permute-start(bf16[2,64,2048]{2,1,0:T(8,128)(2,1)S(1)} %constant_dynamic-update-slice_fusion.refs_0_.refs_1_), channel_id=1, source_target_pairs={{0,8},{1,9},{2,10},{3,11},{4,12},{5,13},{6,14},{7,15},{8,0},{9,1},... | collective-permute-start | bytes 1572872 | tf_op jit(solution)/shard_map/ppermute | solution.py:34
  7.9 9.5 %collective-permute-done.7.refs_0_.refs_1_ = bf16[2,64,2048]{2,1,0:T(8,128)(2,1)S(1)} collective-permute-done((bf16[2,64,2048]{2,1,0:T(8,128)(2,1)S(1)}, bf16[2,64,2048]{2,1,0:T(8,128)(2,1)S(1)}, u32[]{:S(2)}, u32[]{:S(2)}) %collective-permute-start.7) | collective-permute-done | bytes 524320 | tf_op jit(solution)/shard_map/ppermute | solution.py:34
  17.4 2.0 %collective-permute-start.13 = (bf16[2,64,2048]{2,1,0:T(8,128)(2,1)S(1)}, bf16[2,64,2048]{2,1,0:T(8,128)(2,1)S(1)}, u32[]{:S(2)}, u32[]{:S(2)}) collective-permute-start(bf16[2,64,2048]{2,1,0:T(8,128)(2,1)S(1)} %collective-permute-done.7.refs_0_.refs_1_), channel_id=1, source_target_pairs={{0,8},{1,9},{2,10},{3,11},{4,12},{5,13},{6,14},{7,15},{8,0},{9,1},... | collective-permute-start | bytes 1572872 | tf_op jit(solution)/shard_map/ppermute | solution.py:34
  19.4 1.3 collective-permute-start.3
  20.7 1.4 collective-permute-start.4
  22.2 1.6 %copy-done.1 = f32[1,2,2048,128]{3,2,1,0:T(8,128)S(1)} copy-done((f32[1,2,2048,128]{3,2,1,0:T(8,128)S(1)}, f32[1,2,2048,128]{3,2,1,0:T(8,128)}, u32[]{:S(2)}) %copy-start.1) | copy-done | bytes 2097176
  23.8 1.2 copy-done.5
  25.3 1.3 collective-permute-start.1
  26.6 3.5 %collective-permute-done.13.refs_6_.refs_7_ = bf16[2,64,2048]{2,1,0:T(8,128)(2,1)S(1)} collective-permute-done((bf16[2,64,2048]{2,1,0:T(8,128)(2,1)S(1)}, bf16[2,64,2048]{2,1,0:T(8,128)(2,1)S(1)}, u32[]{:S(2)}, u32[]{:S(2)}) %collective-permute-start.13) | collective-permute-done | bytes 524320 | tf_op jit(solution)/shard_map/ppermute | solution.py:34
  30.1 2.6 %collective-permute-start.9 = (bf16[2,64,2048]{2,1,0:T(8,128)(2,1)S(1)}, bf16[2,64,2048]{2,1,0:T(8,128)(2,1)S(1)}, u32[]{:S(2)}, u32[]{:S(2)}) collective-permute-start(bf16[2,64,2048]{2,1,0:T(8,128)(2,1)S(1)} %collective-permute-done.7.refs_0_.refs_1_), channel_id=1, source_target_pairs={{0,6},{1,7},{2,0},{3,1},{4,2},{5,3},{6,4},{7,5},{8,14},{9,15},{10,... | collective-permute-start | bytes 1572872 | tf_op jit(solution)/shard_map/ppermute | solution.py:34
  32.8 4.9 %collective-permute-start = (bf16[3,128,2048]{2,1,0:T(8,128)(2,1)S(1)}, bf16[3,128,2048]{2,1,0:T(8,128)(2,1)S(1)}, u32[]{:S(2)}, u32[]{:S(2)}) collective-permute-start(bf16[3,128,2048]{2,1,0:T(8,128)(2,1)S(1)} %own_weights.1), channel_id=1, source_target_pairs={{0,1},{1,0},{2,3},{3,2},{4,5},{5,4},{6,7},{7,6},{8,9},{9,8},{10,11... | collective-permute-start | bytes 4718600 | tf_op jit(solution)/shard_map/ppermute | solution.py:34
  37.7 5.9 %collective-permute-done.8.refs_2_.refs_3_ = bf16[2,64,2048]{2,1,0:T(8,128)(2,1)S(1)} collective-permute-done((bf16[2,64,2048]{2,1,0:T(8,128)(2,1)S(1)}, bf16[2,64,2048]{2,1,0:T(8,128)(2,1)S(1)}, u32[]{:S(2)}, u32[]{:S(2)}) %collective-permute-start.8) | collective-permute-done | bytes 524320 | tf_op jit(solution)/shard_map/ppermute | solution.py:34
  43.6 1.4 collective-permute-start.15
  45.2 9.6 %collective-permute-done.14.refs_2_.refs_3_ = bf16[2,64,2048]{2,1,0:T(8,128)(2,1)S(1)} collective-permute-done((bf16[2,64,2048]{2,1,0:T(8,128)(2,1)S(1)}, bf16[2,64,2048]{2,1,0:T(8,128)(2,1)S(1)}, u32[]{:S(2)}, u32[]{:S(2)}) %collective-permute-start.14) | collective-permute-done | bytes 524320 | tf_op jit(solution)/shard_map/ppermute | solution.py:34
  55.5 2.7 %collective-permute-start.6 = (bf16[1,64,2048]{2,1,0:T(8,128)(2,1)S(1)}, bf16[1,64,2048]{2,1,0:T(8,128)(2,1)S(1)}, u32[]{:S(2)}, u32[]{:S(2)}) collective-permute-start(bf16[1,64,2048]{2,1,0:T(8,128)(2,1)S(1)} %slice.105), channel_id=1, source_target_pairs={{0,6},{1,7},{2,0},{3,1},{4,2},{5,3},{6,4},{7,5},{8,14},{9,15},{10,... | collective-permute-start | bytes 786440 | tf_op jit(solution)/shard_map/ppermute | solution.py:34
  58.2 10.6 %collective-permute-done.19.refs_4_.refs_5_ = bf16[2,64,2048]{2,1,0:T(8,128)(2,1)S(1)} collective-permute-done((bf16[2,64,2048]{2,1,0:T(8,128)(2,1)S(1)}, bf16[2,64,2048]{2,1,0:T(8,128)(2,1)S(1)}, u32[]{:S(2)}, u32[]{:S(2)}) %collective-permute-start.19) | collective-permute-done | bytes 524320 | tf_op jit(solution)/shard_map/ppermute | solution.py:34
  68.9 2.4 %collective-permute-start.2 = (bf16[3,128,2048]{2,1,0:T(8,128)(2,1)S(1)}, bf16[3,128,2048]{2,1,0:T(8,128)(2,1)S(1)}, u32[]{:S(2)}, u32[]{:S(2)}) collective-permute-start(bf16[3,128,2048]{2,1,0:T(8,128)(2,1)S(1)} %collective-permute-done.1), channel_id=1, source_target_pairs={{0,1},{1,0},{2,3},{3,2},{4,5},{5,4},{6,7},{7,6},{8,9},{9,8},{10,11... | collective-permute-start | bytes 4718600 | tf_op jit(solution)/shard_map/ppermute | solution.py:34
  71.3 2.6 %collective-permute-start.11 = (bf16[1,64,2048]{2,1,0:T(8,128)(2,1)S(1)}, bf16[1,64,2048]{2,1,0:T(8,128)(2,1)S(1)}, u32[]{:S(2)}, u32[]{:S(2)}) collective-permute-start(bf16[1,64,2048]{2,1,0:T(8,128)(2,1)S(1)} %slice.107), channel_id=1, source_target_pairs={{0,6},{1,7},{2,0},{3,1},{4,2},{5,3},{6,4},{7,5},{8,14},{9,15},{10,... | collective-permute-start | bytes 786440 | tf_op jit(solution)/shard_map/ppermute | solution.py:34
  74.3 1.3 collective-permute-start.16
  76.1 1.9 %forward.6 = (bf16[512,256]{1,0:T(8,128)(2,1)S(1)}, bf16[512,256]{1,0:T(8,128)(2,1)S(1)}, bf16[512,256]{1,0:T(8,128)(2,1)S(1)}, bf16[256,2048]{1,0:T(8,128)(2,1)S(1)}, bf16[256,2048]{1,0:T(8,128)(2,1)S(1)}) custom-call(bf16[1024,2048]{1,0:T(8,128)(2,1)S(1)} %fusion.3.in_ref, bf16[512,2048]{1,0:T(8,128)(2,1)S(1)} %pad_maximum_fusion.down_ref, ...), custom_call_target="tpu_custom_call" | custom-call | flops 1610612736 | bytes 10485760 | tf_op jit(solution)/shard_map/forward/pallas_call | solution.py:116
  78.1 1.5 collective-permute-start.17
  79.7 3.4 %collective-permute-start.21 = (bf16[1,64,2048]{2,1,0:T(8,128)(2,1)S(1)}, bf16[1,64,2048]{2,1,0:T(8,128)(2,1)S(1)}, u32[]{:S(2)}, u32[]{:S(2)}) collective-permute-start(bf16[1,64,2048]{2,1,0:T(8,128)(2,1)S(1)} %slice.111), channel_id=1, source_target_pairs={{0,6},{1,7},{2,0},{3,1},{4,2},{5,3},{6,4},{7,5},{8,14},{9,15},{10,... | collective-permute-start | bytes 786440 | tf_op jit(solution)/shard_map/ppermute | solution.py:34
  83.1 1.9 %forward.5 = (bf16[512,256]{1,0:T(8,128)(2,1)S(1)}, bf16[512,256]{1,0:T(8,128)(2,1)S(1)}, bf16[512,256]{1,0:T(8,128)(2,1)S(1)}, bf16[256,2048]{1,0:T(8,128)(2,1)S(1)}, bf16[256,2048]{1,0:T(8,128)(2,1)S(1)}) custom-call(bf16[1024,2048]{1,0:T(8,128)(2,1)S(1)} %fusion.3.in_ref, bf16[512,2048]{1,0:T(8,128)(2,1)S(1)} %pad_maximum_fusion.down_ref, ...), custom_call_target="tpu_custom_call" | custom-call | flops 1610612736 | bytes 10485760 | tf_op jit(solution)/shard_map/forward/pallas_call | solution.py:116
  85.0 1.9 %forward.4 = (bf16[512,256]{1,0:T(8,128)(2,1)S(1)}, bf16[512,256]{1,0:T(8,128)(2,1)S(1)}, bf16[512,256]{1,0:T(8,128)(2,1)S(1)}, bf16[256,2048]{1,0:T(8,128)(2,1)S(1)}, bf16[256,2048]{1,0:T(8,128)(2,1)S(1)}) custom-call(bf16[1024,2048]{1,0:T(8,128)(2,1)S(1)} %fusion.3.in_ref, bf16[512,2048]{1,0:T(8,128)(2,1)S(1)} %pad_maximum_fusion.down_ref, ...), custom_call_target="tpu_custom_call" | custom-call | flops 1610612736 | bytes 10485760 | tf_op jit(solution)/shard_map/forward/pallas_call | solution.py:116
  87.0 1.7 %collective-permute-done.20.refs_6_ = bf16[1,64,2048]{2,1,0:T(8,128)(2,1)S(1)} collective-permute-done((bf16[1,64,2048]{2,1,0:T(8,128)(2,1)S(1)}, bf16[1,64,2048]{2,1,0:T(8,128)(2,1)S(1)}, u32[]{:S(2)}, u32[]{:S(2)}) %collective-permute-start.20) | collective-permute-done | bytes 262176 | tf_op jit(solution)/shard_map/ppermute | solution.py:34
  88.7 2.3 %collective-permute-done.21.refs_7_ = bf16[1,64,2048]{2,1,0:T(8,128)(2,1)S(1)} collective-permute-done((bf16[1,64,2048]{2,1,0:T(8,128)(2,1)S(1)}, bf16[1,64,2048]{2,1,0:T(8,128)(2,1)S(1)}, u32[]{:S(2)}, u32[]{:S(2)}) %collective-permute-start.21) | collective-permute-done | bytes 262176 | tf_op jit(solution)/shard_map/ppermute | solution.py:34
  91.0 1.9 %forward.7 = (bf16[512,256]{1,0:T(8,128)(2,1)S(1)}, bf16[512,256]{1,0:T(8,128)(2,1)S(1)}, bf16[512,256]{1,0:T(8,128)(2,1)S(1)}, bf16[256,2048]{1,0:T(8,128)(2,1)S(1)}, bf16[256,2048]{1,0:T(8,128)(2,1)S(1)}) custom-call(bf16[1024,2048]{1,0:T(8,128)(2,1)S(1)} %fusion.3.in_ref, bf16[512,2048]{1,0:T(8,128)(2,1)S(1)} %pad_maximum_fusion.down_ref, ...), custom_call_target="tpu_custom_call" | custom-call | flops 1610612736 | bytes 10485760 | tf_op jit(solution)/shard_map/forward/pallas_call | solution.py:116
  92.9 2.3 %gradient.3 = (f32[128,2048]{1,0:T(8,128)S(1)}, f32[128,2048]{1,0:T(8,128)S(1)}, bf16[2,128,2048]{2,1,0:T(8,128)(2,1)S(1)}) custom-call(bf16[512,256]{1,0:T(8,128)(2,1)S(1)} %get-tuple-element.62.refs_0_, bf16[512,256]{1,0:T(8,128)(2,1)S(1)} %get-tuple-element.63.refs_1_, bf16[512,256]{1,0:T(8,128)(2,1)S(1)} %get-tuple-element.64.refs_2_, ...), custom_call_target="tpu_custom_call" | custom-call | flops 2147483648 | bytes 8388608 | tf_op jit(solution)/shard_map/gradient/pallas_call | solution.py:155
  95.2 1.6 %collective-permute-start.22 = (bf16[2,128,2048]{2,1,0:T(8,128)(2,1)S(1)}, bf16[2,128,2048]{2,1,0:T(8,128)(2,1)S(1)}, u32[]{:S(2)}, u32[]{:S(2)}) collective-permute-start(bf16[2,128,2048]{2,1,0:T(8,128)(2,1)S(1)} %get-tuple-element.70), channel_id=1, source_target_pairs={{0,1},{1,0},{2,3},{3,2},{4,5},{5,4},{6,7},{7,6},{8,9},{9,8},{10,11... | collective-permute-start | bytes 3145736 | tf_op jit(solution)/shard_map/ppermute | solution.py:34
  96.8 2.3 %gradient.5 = (f32[128,2048]{1,0:T(8,128)S(1)}, f32[128,2048]{1,0:T(8,128)S(1)}, bf16[2,128,2048]{2,1,0:T(8,128)(2,1)S(1)}) custom-call(bf16[512,256]{1,0:T(8,128)(2,1)S(1)} %get-tuple-element.82.refs_0_, bf16[512,256]{1,0:T(8,128)(2,1)S(1)} %get-tuple-element.83.refs_1_, bf16[512,256]{1,0:T(8,128)(2,1)S(1)} %get-tuple-element.84.refs_2_, ...), custom_call_target="tpu_custom_call" | custom-call | flops 2147483648 | bytes 8388608 | tf_op jit(solution)/shard_map/gradient/pallas_call | solution.py:155
  99.3 2.3 %gradient.4 = (f32[128,2048]{1,0:T(8,128)S(1)}, f32[128,2048]{1,0:T(8,128)S(1)}, bf16[2,128,2048]{2,1,0:T(8,128)(2,1)S(1)}) custom-call(bf16[512,256]{1,0:T(8,128)(2,1)S(1)} %get-tuple-element.71.refs_0_, bf16[512,256]{1,0:T(8,128)(2,1)S(1)} %get-tuple-element.72.refs_1_, bf16[512,256]{1,0:T(8,128)(2,1)S(1)} %get-tuple-element.73.refs_2_, ...), custom_call_target="tpu_custom_call" | custom-call | flops 2147483648 | bytes 8388608 | tf_op jit(solution)/shard_map/gradient/pallas_call | solution.py:155
  102.3 1.3 collective-permute-start.29
  104.6 1.3 collective-permute-start.24
  105.9 10.0 %collective-permute-done.29.refs_2_ = bf16[128,2048]{1,0:T(8,128)(2,1)S(1)} collective-permute-done((bf16[128,2048]{1,0:T(8,128)(2,1)S(1)}, bf16[128,2048]{1,0:T(8,128)(2,1)S(1)}, u32[]{:S(2)}, u32[]{:S(2)}) %collective-permute-start.29) | collective-permute-done | bytes 524320 | tf_op jit(solution)/shard_map/ppermute | solution.py:34
  116.0 2.2 %inner_step.5 = (bf16[1,128,2048]{2,1,0:T(8,128)(2,1)}, bf16[1,128,2048]{2,1,0:T(8,128)(2,1)}, bf16[128,2048]{1,0:T(8,128)(2,1)S(1)}) custom-call(f32[128,2048]{1,0:T(8,128)S(1)} %get-tuple-element.96.refs_0_, bf16[2,128,2048]{2,1,0:T(8,128)(2,1)S(1)} %collective-permute-done.22.refs_1_, bf16[128,2048]{1,0:T(8,128)(2,1)S(1)} %collective-permute-done.29.refs_2_, ...), custom_call_target="tpu_custom_call" | custom-call | flops 5242880 | bytes 6815744 | tf_op jit(solution)/shard_map/inner_step/pallas_call | solution.py:212
  118.1 3.2 %collective-permute-start.30 = (bf16[128,2048]{1,0:T(8,128)(2,1)S(1)}, bf16[128,2048]{1,0:T(8,128)(2,1)S(1)}, u32[]{:S(2)}, u32[]{:S(2)}) collective-permute-start(bf16[128,2048]{1,0:T(8,128)(2,1)S(1)} %get-tuple-element.98.refs_0_), channel_id=1, source_target_pairs={{0,64},{64,0},{1,65},{65,1},{2,66},{66,2},{3,67},{67,3},{4,68},{68... | collective-permute-start | bytes 1572872 | tf_op jit(solution)/shard_map/ppermute | solution.py:62
  121.4 5.8 %collective-permute-done.26.refs_2_ = bf16[128,2048]{1,0:T(8,128)(2,1)S(1)} collective-permute-done((bf16[128,2048]{1,0:T(8,128)(2,1)S(1)}, bf16[128,2048]{1,0:T(8,128)(2,1)S(1)}, u32[]{:S(2)}, u32[]{:S(2)}) %collective-permute-start.26) | collective-permute-done | bytes 524320 | tf_op jit(solution)/shard_map/ppermute | solution.py:34
  127.2 2.3 %inner_step.3 = (bf16[1,2,2048,128]{3,2,1,0:T(8,128)(2,1)}, bf16[1,2,2048,128]{3,2,1,0:T(8,128)(2,1)}, bf16[2048,128]{1,0:T(8,128)(2,1)S(1)}) custom-call(f32[128,2048]{1,0:T(8,128)S(1)} %get-tuple-element.86.refs_0_, bf16[2,128,2048]{2,1,0:T(8,128)(2,1)S(1)} %collective-permute-done.25.refs_1_, bf16[128,2048]{1,0:T(8,128)(2,1)S(1)} %collective-permute-done.26.refs_2_, ...), custom_call_target="tpu_custom_call" | custom-call | flops 5242880 | bytes 6815744 | tf_op jit(solution)/shard_map/inner_step/pallas_call | solution.py:212
  129.5 3.2 %collective-permute-start.28 = (bf16[2048,128]{1,0:T(8,128)(2,1)S(1)}, bf16[2048,128]{1,0:T(8,128)(2,1)S(1)}, u32[]{:S(2)}, u32[]{:S(2)}) collective-permute-start(bf16[2048,128]{1,0:T(8,128)(2,1)S(1)} %get-tuple-element.92.refs_0_), channel_id=1, source_target_pairs={{0,64},{64,0},{1,65},{65,1},{2,66},{66,2},{3,67},{67,3},{4,68},{68... | collective-permute-start | bytes 1572872 | tf_op jit(solution)/shard_map/ppermute | solution.py:62
  132.8 5.6 %collective-permute-done.24.refs_2_ = bf16[128,2048]{1,0:T(8,128)(2,1)S(1)} collective-permute-done((bf16[128,2048]{1,0:T(8,128)(2,1)S(1)}, bf16[128,2048]{1,0:T(8,128)(2,1)S(1)}, u32[]{:S(2)}, u32[]{:S(2)}) %collective-permute-start.24) | collective-permute-done | bytes 524320 | tf_op jit(solution)/shard_map/ppermute | solution.py:34
  138.4 2.3 %inner_step.4 = (bf16[1,2,2048,128]{3,2,1,0:T(8,128)(2,1)}, bf16[1,2,2048,128]{3,2,1,0:T(8,128)(2,1)}, bf16[2048,128]{1,0:T(8,128)(2,1)S(1)}) custom-call(f32[128,2048]{1,0:T(8,128)S(1)} %get-tuple-element.79.refs_0_, bf16[2,128,2048]{2,1,0:T(8,128)(2,1)S(1)} %collective-permute-done.23.refs_1_, ...), custom_call_target="tpu_custom_call", output_to_operand_aliasing={{0}: (7, {}), {1}: (8, {})} | custom-call | flops 5242880 | bytes 6815744 | tf_op jit(solution)/shard_map/inner_step/pallas_call | solution.py:212
  140.7 3.2 %collective-permute-start.27 = (bf16[2048,128]{1,0:T(8,128)(2,1)S(1)}, bf16[2048,128]{1,0:T(8,128)(2,1)S(1)}, u32[]{:S(2)}, u32[]{:S(2)}) collective-permute-start(bf16[2048,128]{1,0:T(8,128)(2,1)S(1)} %get-tuple-element.91.refs_0_), channel_id=1, source_target_pairs={{0,64},{64,0},{1,65},{65,1},{2,66},{66,2},{3,67},{67,3},{4,68},{68... | collective-permute-start | bytes 1572872 | tf_op jit(solution)/shard_map/ppermute | solution.py:62
  144.0 1.9 %outer_step.5 = (f32[128,2048]{1,0:T(8,128)}, f32[128,2048]{1,0:T(8,128)}) custom-call(bf16[128,2048]{1,0:T(8,128)(2,1)S(1)} %get-tuple-element.98.refs_0_, bf16[128,2048]{1,0:T(8,128)(2,1)S(1)} %collective-permute-done.30.refs_1_, f32[128,2048]{1,0:T(8,128)S(1)} %copy-done.4, f32[128,2048]{1,0:T(8,128)S(1)} %copy-done.9), custom_call_target="tpu_custom_call" | custom-call | flops 2097152 | bytes 5242880 | tf_op jit(solution)/shard_map/outer_step/pallas_call | solution.py:248
  145.9 1.9 %outer_step.3 = (f32[2,2048,128]{2,1,0:T(8,128)}, f32[2,2048,128]{2,1,0:T(8,128)}) custom-call(bf16[2048,128]{1,0:T(8,128)(2,1)S(1)} %get-tuple-element.92.refs_0_, bf16[2048,128]{1,0:T(8,128)(2,1)S(1)} %collective-permute-done.28.refs_1_, f32[2,2048,128]{2,1,0:T(8,128)S(1)} %copy-done, f32[2,2048,128]{2,1,0:T(8,128)S(1)} %copy-done.3), custom_call_target="tpu_custom_call" | custom-call | flops 2097152 | bytes 5242880 | tf_op jit(solution)/shard_map/outer_step/pallas_call | solution.py:248
  147.8 7.8 %collective-permute-done.27.refs_1_ = bf16[2048,128]{1,0:T(8,128)(2,1)S(1)} collective-permute-done((bf16[2048,128]{1,0:T(8,128)(2,1)S(1)}, bf16[2048,128]{1,0:T(8,128)(2,1)S(1)}, u32[]{:S(2)}, u32[]{:S(2)}) %collective-permute-start.27) | collective-permute-done | bytes 524320 | tf_op jit(solution)/shard_map/ppermute | solution.py:62
  155.6 1.9 %outer_step.4 = (f32[2,2048,128]{2,1,0:T(8,128)}, f32[2,2048,128]{2,1,0:T(8,128)}) custom-call(bf16[2048,128]{1,0:T(8,128)(2,1)S(1)} %get-tuple-element.91.refs_0_, bf16[2048,128]{1,0:T(8,128)(2,1)S(1)} %collective-permute-done.27.refs_1_, f32[2,2048,128]{2,1,0:T(8,128)S(1)} %copy-done, ...), custom_call_target="tpu_custom_call", output_to_operand_aliasing={{0}: (4, {}), {1}: (5, {})} | custom-call | flops 2097152 | bytes 5242880 | tf_op jit(solution)/shard_map/outer_step/pallas_call | solution.py:248
  (78 shorter events, 4.9 us)
Async XLA Ops:
  2.6 14.8 %collective-permute-start.7 = (bf16[2,64,2048]{2,1,0:T(8,128)(2,1)S(1)}, bf16[2,64,2048]{2,1,0:T(8,128)(2,1)S(1)}, u32[]{:S(2)}, u32[]{:S(2)}) collective-permute-start(bf16[2,64,2048]{2,1,0:T(8,128)(2,1)S(1)} %constant_dynamic-update-slice_fusion.refs_0_.refs_1_), channel_id=1, source_target_pairs={{0,32},{1,33},{2,34},{3,35},{4,36},{5,37},{6,38},{7,39},{8,40},{9,... | collective-permute-start | bytes 1572872 | tf_op jit(solution)/shard_map/ppermute | solution.py:34
  6.2 20.4 %collective-permute-start.12 = (bf16[2,64,2048]{2,1,0:T(8,128)(2,1)S(1)}, bf16[2,64,2048]{2,1,0:T(8,128)(2,1)S(1)}, u32[]{:S(2)}, u32[]{:S(2)}) collective-permute-start(bf16[2,64,2048]{2,1,0:T(8,128)(2,1)S(1)} %constant_dynamic-update-slice_fusion.refs_0_.refs_1_), channel_id=1, source_target_pairs={{0,8},{1,9},{2,10},{3,11},{4,12},{5,13},{6,14},{7,15},{8,0},{9,1},... | collective-permute-start | bytes 1572872 | tf_op jit(solution)/shard_map/ppermute | solution.py:34
  17.4 12.7 %collective-permute-start.13 = (bf16[2,64,2048]{2,1,0:T(8,128)(2,1)S(1)}, bf16[2,64,2048]{2,1,0:T(8,128)(2,1)S(1)}, u32[]{:S(2)}, u32[]{:S(2)}) collective-permute-start(bf16[2,64,2048]{2,1,0:T(8,128)(2,1)S(1)} %collective-permute-done.7.refs_0_.refs_1_), channel_id=1, source_target_pairs={{0,8},{1,9},{2,10},{3,11},{4,12},{5,13},{6,14},{7,15},{8,0},{9,1},... | collective-permute-start | bytes 1572872 | tf_op jit(solution)/shard_map/ppermute | solution.py:34
  19.4 13.3 %collective-permute-start.3 = (bf16[2,64,2048]{2,1,0:T(8,128)(2,1)S(1)}, bf16[2,64,2048]{2,1,0:T(8,128)(2,1)S(1)}, u32[]{:S(2)}, u32[]{:S(2)}) collective-permute-start(bf16[2,64,2048]{2,1,0:T(8,128)(2,1)S(1)} %constant_dynamic-update-slice_fusion.refs_0_.refs_1_), channel_id=1, source_target_pairs={{0,2},{1,3},{2,4},{3,5},{4,6},{5,7},{6,0},{7,1},{8,10},{9,11},{10,... | collective-permute-start | bytes 1572872 | tf_op jit(solution)/shard_map/ppermute | solution.py:34
  20.7 12.0 %collective-permute-start.4 = (bf16[2,64,2048]{2,1,0:T(8,128)(2,1)S(1)}, bf16[2,64,2048]{2,1,0:T(8,128)(2,1)S(1)}, u32[]{:S(2)}, u32[]{:S(2)}) collective-permute-start(bf16[2,64,2048]{2,1,0:T(8,128)(2,1)S(1)} %constant_dynamic-update-slice_fusion.refs_0_.refs_1_), channel_id=1, source_target_pairs={{0,6},{1,7},{2,0},{3,1},{4,2},{5,3},{6,4},{7,5},{8,14},{9,15},{10,... | collective-permute-start | bytes 1572872 | tf_op jit(solution)/shard_map/ppermute | solution.py:34
  22.2 1.6 %copy-start.1 = (f32[1,2,2048,128]{3,2,1,0:T(8,128)S(1)}, f32[1,2,2048,128]{3,2,1,0:T(8,128)}, u32[]{:S(2)}) copy-start(f32[1,2,2048,128]{3,2,1,0:T(8,128)} %refs_3_.7) | copy-start | bytes 6291460
  23.7 1.2 copy-start.5
  25.3 43.5 %collective-permute-start.1 = (bf16[3,128,2048]{2,1,0:T(8,128)(2,1)S(1)}, bf16[3,128,2048]{2,1,0:T(8,128)(2,1)S(1)}, u32[]{:S(2)}, u32[]{:S(2)}) collective-permute-start(bf16[3,128,2048]{2,1,0:T(8,128)(2,1)S(1)} %own_weights.1), channel_id=1, source_target_pairs={{0,16},{1,17},{2,18},{3,19},{4,20},{5,21},{6,22},{7,23},{8,24},{9,... | collective-permute-start | bytes 4718600 | tf_op jit(solution)/shard_map/ppermute | solution.py:34
  26.6 17.0 %collective-permute-start.8 = (bf16[2,64,2048]{2,1,0:T(8,128)(2,1)S(1)}, bf16[2,64,2048]{2,1,0:T(8,128)(2,1)S(1)}, u32[]{:S(2)}, u32[]{:S(2)}) collective-permute-start(bf16[2,64,2048]{2,1,0:T(8,128)(2,1)S(1)} %collective-permute-done.7.refs_0_.refs_1_), channel_id=1, source_target_pairs={{0,2},{1,3},{2,4},{3,5},{4,6},{5,7},{6,0},{7,1},{8,10},{9,11},{10,... | collective-permute-start | bytes 1572872 | tf_op jit(solution)/shard_map/ppermute | solution.py:34
  30.1 14.9 %collective-permute-start.9 = (bf16[2,64,2048]{2,1,0:T(8,128)(2,1)S(1)}, bf16[2,64,2048]{2,1,0:T(8,128)(2,1)S(1)}, u32[]{:S(2)}, u32[]{:S(2)}) collective-permute-start(bf16[2,64,2048]{2,1,0:T(8,128)(2,1)S(1)} %collective-permute-done.7.refs_0_.refs_1_), channel_id=1, source_target_pairs={{0,6},{1,7},{2,0},{3,1},{4,2},{5,3},{6,4},{7,5},{8,14},{9,15},{10,... | collective-permute-start | bytes 1572872 | tf_op jit(solution)/shard_map/ppermute | solution.py:34
  32.7 22.1 %collective-permute-start.14 = (bf16[2,64,2048]{2,1,0:T(8,128)(2,1)S(1)}, bf16[2,64,2048]{2,1,0:T(8,128)(2,1)S(1)}, u32[]{:S(2)}, u32[]{:S(2)}) collective-permute-start(bf16[2,64,2048]{2,1,0:T(8,128)(2,1)S(1)} %collective-permute-done.12.refs_0_.refs_1_), channel_id=1, source_target_pairs={{0,2},{1,3},{2,4},{3,5},{4,6},{5,7},{6,0},{7,1},{8,10},{9,11},{10,... | collective-permute-start | bytes 1572872 | tf_op jit(solution)/shard_map/ppermute | solution.py:34
  32.8 38.6 %collective-permute-start = (bf16[3,128,2048]{2,1,0:T(8,128)(2,1)S(1)}, bf16[3,128,2048]{2,1,0:T(8,128)(2,1)S(1)}, u32[]{:S(2)}, u32[]{:S(2)}) collective-permute-start(bf16[3,128,2048]{2,1,0:T(8,128)(2,1)S(1)} %own_weights.1), channel_id=1, source_target_pairs={{0,1},{1,0},{2,3},{3,2},{4,5},{5,4},{6,7},{7,6},{8,9},{9,8},{10,11... | collective-permute-start | bytes 4718600 | tf_op jit(solution)/shard_map/ppermute | solution.py:34
  43.6 11.8 %collective-permute-start.15 = (bf16[2,64,2048]{2,1,0:T(8,128)(2,1)S(1)}, bf16[2,64,2048]{2,1,0:T(8,128)(2,1)S(1)}, u32[]{:S(2)}, u32[]{:S(2)}) collective-permute-start(bf16[2,64,2048]{2,1,0:T(8,128)(2,1)S(1)} %collective-permute-done.12.refs_0_.refs_1_), channel_id=1, source_target_pairs={{0,6},{1,7},{2,0},{3,1},{4,2},{5,3},{6,4},{7,5},{8,14},{9,15},{10,... | collective-permute-start | bytes 1572872 | tf_op jit(solution)/shard_map/ppermute | solution.py:34
  45.0 10.5 %collective-permute-start.18 = (bf16[2,64,2048]{2,1,0:T(8,128)(2,1)S(1)}, bf16[2,64,2048]{2,1,0:T(8,128)(2,1)S(1)}, u32[]{:S(2)}, u32[]{:S(2)}) collective-permute-start(bf16[2,64,2048]{2,1,0:T(8,128)(2,1)S(1)} %collective-permute-done.8.refs_2_.refs_3_), channel_id=1, source_target_pairs={{0,8},{1,9},{2,10},{3,11},{4,12},{5,13},{6,14},{7,15},{8,0},{9,1},... | collective-permute-start | bytes 1572872 | tf_op jit(solution)/shard_map/ppermute | solution.py:34
  54.8 14.0 %collective-permute-start.19 = (bf16[2,64,2048]{2,1,0:T(8,128)(2,1)S(1)}, bf16[2,64,2048]{2,1,0:T(8,128)(2,1)S(1)}, u32[]{:S(2)}, u32[]{:S(2)}) collective-permute-start(bf16[2,64,2048]{2,1,0:T(8,128)(2,1)S(1)} %collective-permute-done.9.refs_4_.refs_5_), channel_id=1, source_target_pairs={{0,8},{1,9},{2,10},{3,11},{4,12},{5,13},{6,14},{7,15},{8,0},{9,1},... | collective-permute-start | bytes 1572872 | tf_op jit(solution)/shard_map/ppermute | solution.py:34
  55.3 22.7 %collective-permute-start.5 = (bf16[1,64,2048]{2,1,0:T(8,128)(2,1)S(1)}, bf16[1,64,2048]{2,1,0:T(8,128)(2,1)S(1)}, u32[]{:S(2)}, u32[]{:S(2)}) collective-permute-start(bf16[1,64,2048]{2,1,0:T(8,128)(2,1)S(1)} %slice.104), channel_id=1, source_target_pairs={{0,2},{1,3},{2,4},{3,5},{4,6},{5,7},{6,0},{7,1},{8,10},{9,11},{10,... | collective-permute-start | bytes 786440 | tf_op jit(solution)/shard_map/ppermute | solution.py:34
  55.5 29.6 %collective-permute-start.6 = (bf16[1,64,2048]{2,1,0:T(8,128)(2,1)S(1)}, bf16[1,64,2048]{2,1,0:T(8,128)(2,1)S(1)}, u32[]{:S(2)}, u32[]{:S(2)}) collective-permute-start(bf16[1,64,2048]{2,1,0:T(8,128)(2,1)S(1)} %slice.105), channel_id=1, source_target_pairs={{0,6},{1,7},{2,0},{3,1},{4,2},{5,3},{6,4},{7,5},{8,14},{9,15},{10,... | collective-permute-start | bytes 786440 | tf_op jit(solution)/shard_map/ppermute | solution.py:34
  68.8 10.7 %collective-permute-start.10 = (bf16[1,64,2048]{2,1,0:T(8,128)(2,1)S(1)}, bf16[1,64,2048]{2,1,0:T(8,128)(2,1)S(1)}, u32[]{:S(2)}, u32[]{:S(2)}) collective-permute-start(bf16[1,64,2048]{2,1,0:T(8,128)(2,1)S(1)} %slice.106), channel_id=1, source_target_pairs={{0,2},{1,3},{2,4},{3,5},{4,6},{5,7},{6,0},{7,1},{8,10},{9,11},{10,... | collective-permute-start | bytes 786440 | tf_op jit(solution)/shard_map/ppermute | solution.py:34
  68.9 5.5 %collective-permute-start.2 = (bf16[3,128,2048]{2,1,0:T(8,128)(2,1)S(1)}, bf16[3,128,2048]{2,1,0:T(8,128)(2,1)S(1)}, u32[]{:S(2)}, u32[]{:S(2)}) collective-permute-start(bf16[3,128,2048]{2,1,0:T(8,128)(2,1)S(1)} %collective-permute-done.1), channel_id=1, source_target_pairs={{0,1},{1,0},{2,3},{3,2},{4,5},{5,4},{6,7},{7,6},{8,9},{9,8},{10,11... | collective-permute-start | bytes 4718600 | tf_op jit(solution)/shard_map/ppermute | solution.py:34
  71.3 8.4 %collective-permute-start.11 = (bf16[1,64,2048]{2,1,0:T(8,128)(2,1)S(1)}, bf16[1,64,2048]{2,1,0:T(8,128)(2,1)S(1)}, u32[]{:S(2)}, u32[]{:S(2)}) collective-permute-start(bf16[1,64,2048]{2,1,0:T(8,128)(2,1)S(1)} %slice.107), channel_id=1, source_target_pairs={{0,6},{1,7},{2,0},{3,1},{4,2},{5,3},{6,4},{7,5},{8,14},{9,15},{10,... | collective-permute-start | bytes 786440 | tf_op jit(solution)/shard_map/ppermute | solution.py:34
  74.3 12.7 %collective-permute-start.16 = (bf16[1,64,2048]{2,1,0:T(8,128)(2,1)S(1)}, bf16[1,64,2048]{2,1,0:T(8,128)(2,1)S(1)}, u32[]{:S(2)}, u32[]{:S(2)}) collective-permute-start(bf16[1,64,2048]{2,1,0:T(8,128)(2,1)S(1)} %slice.108), channel_id=1, source_target_pairs={{0,2},{1,3},{2,4},{3,5},{4,6},{5,7},{6,0},{7,1},{8,10},{9,11},{10,... | collective-permute-start | bytes 786440 | tf_op jit(solution)/shard_map/ppermute | solution.py:34
  78.1 8.9 %collective-permute-start.17 = (bf16[1,64,2048]{2,1,0:T(8,128)(2,1)S(1)}, bf16[1,64,2048]{2,1,0:T(8,128)(2,1)S(1)}, u32[]{:S(2)}, u32[]{:S(2)}) collective-permute-start(bf16[1,64,2048]{2,1,0:T(8,128)(2,1)S(1)} %slice.109), channel_id=1, source_target_pairs={{0,6},{1,7},{2,0},{3,1},{4,2},{5,3},{6,4},{7,5},{8,14},{9,15},{10,... | collective-permute-start | bytes 786440 | tf_op jit(solution)/shard_map/ppermute | solution.py:34
  79.5 9.1 %collective-permute-start.20 = (bf16[1,64,2048]{2,1,0:T(8,128)(2,1)S(1)}, bf16[1,64,2048]{2,1,0:T(8,128)(2,1)S(1)}, u32[]{:S(2)}, u32[]{:S(2)}) collective-permute-start(bf16[1,64,2048]{2,1,0:T(8,128)(2,1)S(1)} %slice.110), channel_id=1, source_target_pairs={{0,2},{1,3},{2,4},{3,5},{4,6},{5,7},{6,0},{7,1},{8,10},{9,11},{10,... | collective-permute-start | bytes 786440 | tf_op jit(solution)/shard_map/ppermute | solution.py:34
  79.7 11.3 %collective-permute-start.21 = (bf16[1,64,2048]{2,1,0:T(8,128)(2,1)S(1)}, bf16[1,64,2048]{2,1,0:T(8,128)(2,1)S(1)}, u32[]{:S(2)}, u32[]{:S(2)}) collective-permute-start(bf16[1,64,2048]{2,1,0:T(8,128)(2,1)S(1)} %slice.111), channel_id=1, source_target_pairs={{0,6},{1,7},{2,0},{3,1},{4,2},{5,3},{6,4},{7,5},{8,14},{9,15},{10,... | collective-permute-start | bytes 786440 | tf_op jit(solution)/shard_map/ppermute | solution.py:34
  95.2 4.0 %collective-permute-start.22 = (bf16[2,128,2048]{2,1,0:T(8,128)(2,1)S(1)}, bf16[2,128,2048]{2,1,0:T(8,128)(2,1)S(1)}, u32[]{:S(2)}, u32[]{:S(2)}) collective-permute-start(bf16[2,128,2048]{2,1,0:T(8,128)(2,1)S(1)} %get-tuple-element.70), channel_id=1, source_target_pairs={{0,1},{1,0},{2,3},{3,2},{4,5},{5,4},{6,7},{7,6},{8,9},{9,8},{10,11... | collective-permute-start | bytes 3145736 | tf_op jit(solution)/shard_map/ppermute | solution.py:34
  99.2 4.5 %collective-permute-start.25 = (bf16[2,128,2048]{2,1,0:T(8,128)(2,1)S(1)}, bf16[2,128,2048]{2,1,0:T(8,128)(2,1)S(1)}, u32[]{:S(2)}, u32[]{:S(2)}) collective-permute-start(bf16[2,128,2048]{2,1,0:T(8,128)(2,1)S(1)} %get-tuple-element.87), channel_id=1, source_target_pairs={{0,1},{1,0},{2,3},{3,2},{4,5},{5,4},{6,7},{7,6},{8,9},{9,8},{10,11... | collective-permute-start | bytes 3145736 | tf_op jit(solution)/shard_map/ppermute | solution.py:34
  101.6 14.3 %copy-start.4 = (f32[128,2048]{1,0:T(8,128)S(1)}, f32[128,2048]{1,0:T(8,128)}, u32[]{:S(2)}) copy-start(f32[128,2048]{1,0:T(8,128)} %refs_2_.5) | copy-start | bytes 3145732
  101.6 14.3 %copy-start.6 = (f32[1,128,2048]{2,1,0:T(8,128)S(1)}, f32[1,128,2048]{2,1,0:T(8,128)}, u32[]{:S(2)}) copy-start(f32[1,128,2048]{2,1,0:T(8,128)} %refs_3_.10) | copy-start | bytes 3145732
  101.6 14.3 %copy-start.10 = (bf16[1,128,2048]{2,1,0:T(8,128)(2,1)S(1)}, bf16[1,128,2048]{2,1,0:T(8,128)(2,1)}, u32[]{:S(2)}) copy-start(bf16[1,128,2048]{2,1,0:T(8,128)(2,1)} %refs_4_.5) | copy-start | bytes 1572868
  101.7 14.3 %copy-start.11 = (bf16[1,128,2048]{2,1,0:T(8,128)(2,1)S(1)}, bf16[1,128,2048]{2,1,0:T(8,128)(2,1)}, u32[]{:S(2)}) copy-start(bf16[1,128,2048]{2,1,0:T(8,128)(2,1)} %refs_5_.5) | copy-start | bytes 1572868
  101.7 2.9 %collective-permute-start.23 = (bf16[2,128,2048]{2,1,0:T(8,128)(2,1)S(1)}, bf16[2,128,2048]{2,1,0:T(8,128)(2,1)S(1)}, u32[]{:S(2)}, u32[]{:S(2)}) collective-permute-start(bf16[2,128,2048]{2,1,0:T(8,128)(2,1)S(1)} %get-tuple-element.80), channel_id=1, source_target_pairs={{0,1},{1,0},{2,3},{3,2},{4,5},{5,4},{6,7},{7,6},{8,9},{9,8},{10,11... | collective-permute-start | bytes 3145736 | tf_op jit(solution)/shard_map/ppermute | solution.py:34
  102.3 13.6 %collective-permute-start.29 = (bf16[128,2048]{1,0:T(8,128)(2,1)S(1)}, bf16[128,2048]{1,0:T(8,128)(2,1)S(1)}, u32[]{:S(2)}, u32[]{:S(2)}) collective-permute-start(bf16[128,2048]{1,0:T(8,128)(2,1)S(1)} %fusion), channel_id=1, source_target_pairs={{0,16},{1,17},{2,18},{3,19},{4,20},{5,21},{6,22},{7,23},{8,24},{9,... | collective-permute-start | bytes 1572872 | tf_op jit(solution)/shard_map/ppermute | solution.py:34
  103.7 23.4 %copy-start = (f32[2,2048,128]{2,1,0:T(8,128)S(1)}, f32[2,2048,128]{2,1,0:T(8,128)}, u32[]{:S(2)}) copy-start(f32[2,2048,128]{2,1,0:T(8,128)} %refs_2_.4) | copy-start | bytes 6291460
  103.8 23.4 %copy-start.2 = (f32[1,2,2048,128]{3,2,1,0:T(8,128)S(1)}, f32[1,2,2048,128]{3,2,1,0:T(8,128)}, u32[]{:S(2)}) copy-start(f32[1,2,2048,128]{3,2,1,0:T(8,128)} %refs_3_.7) | copy-start | bytes 6291460
  103.8 23.4 %copy-start.7 = (bf16[1,2,2048,128]{3,2,1,0:T(8,128)(2,1)S(1)}, bf16[1,2,2048,128]{3,2,1,0:T(8,128)(2,1)}, u32[]{:S(2)}) copy-start(bf16[1,2,2048,128]{3,2,1,0:T(8,128)(2,1)} %refs_4_.4) | copy-start | bytes 3145732
  103.8 23.4 %copy-start.8 = (bf16[1,2,2048,128]{3,2,1,0:T(8,128)(2,1)S(1)}, bf16[1,2,2048,128]{3,2,1,0:T(8,128)(2,1)}, u32[]{:S(2)}) copy-start(bf16[1,2,2048,128]{3,2,1,0:T(8,128)(2,1)} %refs_5_.4) | copy-start | bytes 3145732
  103.8 23.4 %collective-permute-start.26 = (bf16[128,2048]{1,0:T(8,128)(2,1)S(1)}, bf16[128,2048]{1,0:T(8,128)(2,1)S(1)}, u32[]{:S(2)}, u32[]{:S(2)}) collective-permute-start(bf16[128,2048]{1,0:T(8,128)(2,1)S(1)} %fusion.1), channel_id=1, source_target_pairs={{0,16},{1,17},{2,18},{3,19},{4,20},{5,21},{6,22},{7,23},{8,24},{9,... | collective-permute-start | bytes 1572872 | tf_op jit(solution)/shard_map/ppermute | solution.py:34
  104.6 33.8 %collective-permute-start.24 = (bf16[128,2048]{1,0:T(8,128)(2,1)S(1)}, bf16[128,2048]{1,0:T(8,128)(2,1)S(1)}, u32[]{:S(2)}, u32[]{:S(2)}) collective-permute-start(bf16[128,2048]{1,0:T(8,128)(2,1)S(1)} %fusion.2), channel_id=1, source_target_pairs={{0,16},{1,17},{2,18},{3,19},{4,20},{5,21},{6,22},{7,23},{8,24},{9,... | collective-permute-start | bytes 1572872 | tf_op jit(solution)/shard_map/ppermute | solution.py:34
  118.1 25.8 %collective-permute-start.30 = (bf16[128,2048]{1,0:T(8,128)(2,1)S(1)}, bf16[128,2048]{1,0:T(8,128)(2,1)S(1)}, u32[]{:S(2)}, u32[]{:S(2)}) collective-permute-start(bf16[128,2048]{1,0:T(8,128)(2,1)S(1)} %get-tuple-element.98.refs_0_), channel_id=1, source_target_pairs={{0,64},{64,0},{1,65},{65,1},{2,66},{66,2},{3,67},{67,3},{4,68},{68... | collective-permute-start | bytes 1572872 | tf_op jit(solution)/shard_map/ppermute | solution.py:62
  129.5 16.3 %collective-permute-start.28 = (bf16[2048,128]{1,0:T(8,128)(2,1)S(1)}, bf16[2048,128]{1,0:T(8,128)(2,1)S(1)}, u32[]{:S(2)}, u32[]{:S(2)}) collective-permute-start(bf16[2048,128]{1,0:T(8,128)(2,1)S(1)} %get-tuple-element.92.refs_0_), channel_id=1, source_target_pairs={{0,64},{64,0},{1,65},{65,1},{2,66},{66,2},{3,67},{67,3},{4,68},{68... | collective-permute-start | bytes 1572872 | tf_op jit(solution)/shard_map/ppermute | solution.py:62
  138.4 5.6 %copy-start.9 = (f32[128,2048]{1,0:T(8,128)S(1)}, f32[128,2048]{1,0:T(8,128)}, u32[]{:S(2)}) copy-start(f32[128,2048]{1,0:T(8,128)} %refs_3_.11) | copy-start | bytes 3145732
  140.7 5.1 %copy-start.3 = (f32[2,2048,128]{2,1,0:T(8,128)S(1)}, f32[2,2048,128]{2,1,0:T(8,128)}, u32[]{:S(2)}) copy-start(f32[2,2048,128]{2,1,0:T(8,128)} %refs_3_.9) | copy-start | bytes 6291460
  140.7 14.8 %collective-permute-start.27 = (bf16[2048,128]{1,0:T(8,128)(2,1)S(1)}, bf16[2048,128]{1,0:T(8,128)(2,1)S(1)}, u32[]{:S(2)}, u32[]{:S(2)}) collective-permute-start(bf16[2048,128]{1,0:T(8,128)(2,1)S(1)} %get-tuple-element.91.refs_0_), channel_id=1, source_target_pairs={{0,64},{64,0},{1,65},{65,1},{2,66},{66,2},{3,67},{67,3},{4,68},{68... | collective-permute-start | bytes 1572872 | tf_op jit(solution)/shard_map/ppermute | solution.py:62

commit v3 on v2

v3 whole, which is shorter than its diff:
```python
import functools

import jax
import jax.numpy as jnp
from jax import lax
from jax.experimental import pallas as pl
from jax.experimental.pallas import tpu as pltpu
from jax.sharding import PartitionSpec as P

beta_one = 0.9
beta_two = 0.95
bias_one = 1.0 - 0.9**64
bias_two = 1.0 - 0.95**64
inner_rate = 0.004
decay_rate = 0.1
epsilon_adam = 1e-08
momentum_keep = 0.9
outer_rate = 0.7

AXES = {"x": (4, 16), "z": (2, 8), "y": (4, 2), "core": (2, 1)}
FSDP = 64
BF16 = jnp.bfloat16
F32 = jnp.float32
VMEM = pl.BlockSpec(memory_space=pltpu.VMEM)
PARAMS = pltpu.CompilerParams(vmem_limit_bytes=12 * 1024 * 1024)


def move(value, axis, target):
    size, stride = AXES[axis]
    pairs = []
    for i in range(FSDP):
        place = (i // stride) % size
        pairs.append((i, i + (target(place) - place) * stride))
    return lax.ppermute(value, "fsdp", pairs)


def up_y(value):
    return move(value, "y", lambda p: (p + 1) % 4)


def down_y(value):
    return move(value, "y", lambda p: (p + 3) % 4)


def swap_z(value):
    return move(value, "z", lambda p: 1 - p)


def swap_core(value):
    return move(value, "core", lambda p: 1 - p)


def far_x(value):
    return move(value, "x", lambda p: (p + 2) % 4)


def near_x(pair):
    first, second = pair
    return [move(first, "x", lambda p: p ^ 1), move(second, "x", lambda p: 3 - p)]


def swap_replica(value):
    return lax.ppermute(value, "replica", [(0, 1), (1, 0)])


def struct(shape, dtype):
    return jax.ShapeDtypeStruct(shape, dtype)


def weights_kernel(in_ref, down_ref, all_ref, *outs):
    half = all_ref.shape[2]
    whole = [in_ref[0, 0].astype(BF16).T, in_ref[0, 1].astype(BF16).T, down_ref[0].astype(BF16)]
    for k, out_ref in enumerate(outs):
        for i in range(3):
            part = whole[i][k * half : (k + 1) * half]
            out_ref[i] = part
            all_ref[k, i] = part


def own_weights(params_in, params_down):
    depth, width = params_in.shape[2:]
    half = (3, width // 2, depth)
    return pl.pallas_call(
        weights_kernel,
        in_specs=[VMEM] * 2,
        out_specs=[VMEM] * 3,
        out_shape=[struct((2, *half), BF16), struct(half, BF16), struct(half, BF16)],
        cost_estimate=pl.CostEstimate(
            flops=depth * width * 3, bytes_accessed=depth * width * 18, transcendentals=0
        ),
        compiler_params=PARAMS,
        name="own_weights",
    )(params_in, params_down)


def forward_kernel(planes, in_ref, down_ref, *refs):
    count = len(planes)
    pieces, outs = refs[: 2 * count], refs[2 * count :]
    hidden_ref, dgate_ref, dup_ref, rows_ref, cots_ref = outs
    start = 0
    for k, (x_plane, c_plane) in enumerate(planes):
        rows = pieces[2 * k].shape[1]
        rows_ref[start : start + rows] = pieces[2 * k][x_plane]
        cots_ref[start : start + rows] = pieces[2 * k + 1][c_plane]
        start += rows
    width = down_ref.shape[0]
    sides = (((1,), (1,)), ((), ()))
    both = lax.dot_general(in_ref[...], rows_ref[...], sides, preferred_element_type=F32)
    dhidden = lax.dot_general(down_ref[...], cots_ref[...], sides, preferred_element_type=F32)
    gate_pre, up_proj = both[:width], both[width:]
    sig = 1.0 / (1.0 + jnp.exp(-gate_pre))
    silu = gate_pre * sig
    hidden_ref[...] = (silu * up_proj).astype(BF16)
    dgate_ref[...] = (dhidden * up_proj * (sig * (1.0 + gate_pre * (1.0 - sig)))).astype(BF16)
    dup_ref[...] = (dhidden * silu).astype(BF16)


def forward(weights_in, weights_down, pieces):
    width, depth = weights_down.shape
    total = sum(p[0].shape[1] for p in pieces)
    operands = [a for x, _, c, _ in pieces for a in (x, c)]
    return pl.pallas_call(
        functools.partial(forward_kernel, [(p[1], p[3]) for p in pieces]),
        in_specs=[VMEM] * (2 + len(operands)),
        out_specs=[VMEM] * 5,
        out_shape=[struct((width, total), BF16)] * 3 + [struct((total, depth), BF16)] * 2,
        cost_estimate=pl.CostEstimate(
            flops=2 * total * depth * 3 * width,
            bytes_accessed=total * depth * 8 + 6 * width * depth,
            transcendentals=total * width,
        ),
        compiler_params=PARAMS,
        name="forward",
    )(weights_in, weights_down, *operands)


def gradient_kernel(count, start, *refs):
    left, right = refs[:count], refs[count : 2 * count]
    own_ref, near_ref, send_ref, all_ref = refs[2 * count :]
    quarter, depth = own_ref.shape
    row = 0
    for piece in left:
        all_ref[:, row : row + piece.shape[1]] = piece[...]
        row += piece.shape[1]
    tile = 256
    for i in range(depth // tile):
        at = slice(i * tile, (i + 1) * tile)
        here = slice(start + i * tile, start + (i + 1) * tile)
        columns = jnp.concatenate([piece[:, here] for piece in right], axis=0)
        total = jnp.dot(all_ref[...], columns, preferred_element_type=F32)
        own_ref[:, at] = total[:quarter]
        send_ref[0, :, at] = total[quarter : 2 * quarter].astype(BF16)
        near_ref[:, at] = total[2 * quarter : 3 * quarter]
        send_ref[1, :, at] = total[3 * quarter :].astype(BF16)


def gradient(left, right, start, size):
    width = left[0].shape[0]
    rows = sum(r.shape[0] for r in right)
    quarter = width // 4
    return pl.pallas_call(
        functools.partial(gradient_kernel, len(left), start),
        in_specs=[VMEM] * (2 * len(left)),
        out_specs=[VMEM] * 3,
        out_shape=[
            struct((quarter, size), F32),
            struct((quarter, size), F32),
            struct((2, quarter, size), BF16),
        ],
        scratch_shapes=[pltpu.VMEM((width, rows), BF16)],
        cost_estimate=pl.CostEstimate(
            flops=2 * rows * size * width,
            bytes_accessed=rows * size * 2 + rows * width * 2 + width * size * 3,
            transcendentals=0,
        ),
        compiler_params=PARAMS,
        name="gradient",
    )(*left, *right)


def near_sum_kernel(part_ref, core_ref, *outs):
    half = outs[0].shape[0]
    for k, out_ref in enumerate(outs):
        at = slice(k * half, (k + 1) * half)
        out_ref[...] = (part_ref[at] + core_ref[1, at].astype(F32)).astype(BF16)


def near_sum(part, core):
    quarter, size = part.shape
    return pl.pallas_call(
        near_sum_kernel,
        in_specs=[VMEM] * 2,
        out_specs=[VMEM] * 2,
        out_shape=[struct((quarter // 2, size), BF16)] * 2,
        cost_estimate=pl.CostEstimate(
            flops=quarter * size, bytes_accessed=quarter * size * 10, transcendentals=0
        ),
        compiler_params=PARAMS,
        name="near_sum",
    )(part, core)


def adamw(param, grad, first, second):
    first_new = beta_one * first.astype(F32) + (1.0 - beta_one) * grad
    second_new = beta_two * second.astype(F32) + (1.0 - beta_two) * grad * grad
    update = first_new / bias_one / (jnp.sqrt(second_new / bias_two) + epsilon_adam)
    param_new = param - inner_rate * (update + decay_rate * param)
    return (param_new, first_new.astype(BF16), second_new.astype(BF16))


TILE = 512


def inner_kernel(which, start, *refs):
    own, core, near_a, near_b, param, first, second, base = refs[:8]
    first_out, second_out, delta_out = refs[-3:]
    step = pl.program_id(0) * TILE
    part = pl.ds(pl.multiple_of(step, TILE), TILE)
    at = pl.ds(pl.multiple_of(start + step, TILE), TILE)
    near = jnp.concatenate([near_a[:, part].astype(F32), near_b[:, part].astype(F32)], axis=0)
    grad = own[:, part] + core[0, :, part].astype(F32) + near
    if which is None:
        place, shared = (0, slice(None), at), (slice(None), at)
    else:
        grad = grad.T
        place, shared = (0, which, at), (which, at)
    new, first_new, second_new = adamw(param[place], grad, first[place], second[place])
    first_out[...] = first_new.reshape(first_out.shape)
    second_out[...] = second_new.reshape(second_out.shape)
    delta_out[...] = (base[shared] - new).astype(BF16)


def inner_step(sums, param, first, second, base, which=None, start=0, earlier=()):
    own, core, near = sums
    quarter, size = own.shape
    skip = start // TILE
    if which is not None:
        state = pl.BlockSpec((1, 1, TILE, quarter), lambda i: (0, which, i + skip, 0))
        delta = pl.BlockSpec((TILE, quarter), lambda i: (i, 0))
        delta_shape = (size, quarter)
    else:
        state = pl.BlockSpec((1, quarter, TILE), lambda i: (0, 0, i + skip))
        delta = pl.BlockSpec((quarter, TILE), lambda i: (0, i))
        delta_shape = (quarter, size)
    return pl.pallas_call(
        functools.partial(inner_kernel, which, start),
        grid=(size // TILE,),
        in_specs=[VMEM] * 8 + [pl.BlockSpec(memory_space=pl.ANY)] * len(earlier),
        out_specs=[state, state, delta],
        out_shape=[struct(first.shape, BF16), struct(second.shape, BF16), struct(delta_shape, BF16)],
        input_output_aliases={8 + k: k for k in range(len(earlier))},
        cost_estimate=pl.CostEstimate(
            flops=20 * quarter * size, bytes_accessed=26 * quarter * size, transcendentals=quarter * size
        ),
        compiler_params=PARAMS,
        name="inner_step",
    )(own, core, *near, param, first, second, base, *earlier)


def outer_kernel(which, start, *refs):
    own, other, base, outer = refs[:4]
    base_out, outer_out = refs[-2:]
    step = pl.program_id(0) * TILE
    part = pl.ds(pl.multiple_of(step, TILE), TILE)
    at = pl.ds(pl.multiple_of(start + step, TILE), TILE)
    if which is None:
        part, shared = (slice(None), part), (slice(None), at)
    else:
        part, shared = (part,), (which, at)
    grad = (own[part].astype(F32) + other[part].astype(F32)) / 2.0
    new_outer = momentum_keep * outer[shared] + grad
    outer_out[...] = new_outer.reshape(outer_out.shape)
    base_out[...] = (base[shared] - outer_rate * (grad + momentum_keep * new_outer)).reshape(base_out.shape)


def outer_step(own, other, base, outer, which=None, start=0, earlier=()):
    skip = start // TILE
    if which is not None:
        size, quarter = own.shape
        shared = pl.BlockSpec((1, TILE, quarter), lambda i: (which, i + skip, 0))
    else:
        quarter, size = own.shape
        shared = pl.BlockSpec((quarter, TILE), lambda i: (0, i + skip))
    return pl.pallas_call(
        functools.partial(outer_kernel, which, start),
        grid=(size // TILE,),
        in_specs=[VMEM] * 4 + [pl.BlockSpec(memory_space=pl.ANY)] * len(earlier),
        out_specs=[shared, shared],
        out_shape=[struct(base.shape, F32), struct(outer.shape, F32)],
        input_output_aliases={4 + k: k for k in range(len(earlier))},
        cost_estimate=pl.CostEstimate(
            flops=8 * quarter * size, bytes_accessed=20 * quarter * size, transcendentals=0
        ),
        compiler_params=PARAMS,
        name="outer_step",
    )(own, other, base, outer, *earlier)


def after(value, *others):
    return lax.optimization_barrier((value, others))[0]


def local(
    inputs,
    cotangent,
    params_in,
    params_down,
    first_in,
    first_down,
    second_in,
    second_down,
    base_in,
    base_down,
    outer_in,
    outer_down,
):
    own = jnp.concatenate([inputs, cotangent])
    low, high = up_y(own), down_y(own)
    by_x, by_z = far_x(own), swap_z(own)
    mine, *halves = own_weights(params_in, params_down)
    core = swap_core(mine)
    by_xz = swap_z(after(by_x, by_z))
    far = up_y(low)
    near = jnp.stack(near_x(after(halves, by_x)))
    both = swap_core(near)
    low_x, high_x = far_x(after(low, near)), down_y(after(by_x, high))
    beside_z = swap_z(after(jnp.concatenate([low, high]), by_xz))
    low_xz, high_xz = up_y(after(by_xz, far, core)), down_y(after(by_xz, high_x, core))
    far_of_x = far_x(after(far, low_x))
    far_xz_x, far_xz_c = up_y(after(low_xz[:1], both)), down_y(after(high_xz[1:], both))
    far_z_x, far_z_c = up_y(beside_z[:1]), down_y(beside_z[3:])

    parts = [half for quarter in (mine, core, near, both) for half in quarter]
    weights_in = jnp.concatenate([w[k] for k in range(2) for w in parts])
    weights_down = jnp.concatenate([w[2] for w in parts])

    def full(piece):
        return (piece, 0, piece, 1)

    groups = [
        [full(own), full(low), full(high), full(far)],
        [full(by_x), full(low_x), full(high_x), full(far_of_x)],
        [full(by_z), full(by_xz), (beside_z, 0, beside_z, 1), (beside_z, 2, beside_z, 3)],
        [full(low_xz), full(high_xz), (far_xz_x, 0, far_xz_c, 0), (far_z_x, 0, far_z_c, 0)],
    ]
    results = [forward(weights_in, weights_down, group) for group in groups]
    hidden, dgate, dup, rows, cots = [list(r) for r in zip(*results)]

    depth = inputs.shape[2]
    states = (
        (params_down, first_down, second_down, base_down, outer_down),
        (params_in, first_in, second_in, base_in, outer_in),
    )
    steps = (
        (dgate, rows, 1, 0, 0, depth),
        (dup, rows, 1, 1, 0, depth),
        (hidden, cots, 0, None, 0, depth),
    )
    moments, sums, deltas, others, news = [(), ()], [], [], [], [(), ()]
    cores, nears = [], []
    for k, (left, right, array, which, start, size) in enumerate(steps):
        if k >= 2:
            left = after(left, cores[k - 2])
        own_part, near_part, send = gradient(left, right, start, size)
        core_part = swap_core(send)
        cores.append(core_part)
        near_parts = near_sum(near_part, core_part)
        nears.append(near_parts)
        sums.append(near_x(near_parts))
        param, first, second, base, _ = states[array]
        *moments[array], delta = inner_step(
            (own_part, core_part, sums[k]), param, first, second, base, which, start, moments[array]
        )
        deltas.append(delta)
        others.append(swap_replica(delta))
    for k, (_, _, array, which, start, _) in enumerate(steps):
        base, outer = states[array][3:]
        news[array] = outer_step(deltas[k], others[k], base, outer, which, start, news[array])
    (new_base_down, new_outer_down), (new_base_in, new_outer_in) = news
    (fdown, sdown), (fin, sin) = moments
    return (new_base_in, new_base_down, new_outer_in, new_outer_down, fin, fdown, sin, sdown)


def solution(mesh):
    in_specs = (
        P("replica", "fsdp", None),
        P("replica", "fsdp", None),
        P("replica", None, None, "fsdp"),
        P("replica", "fsdp", None),
        P("replica", None, None, "fsdp"),
        P("replica", "fsdp", None),
        P("replica", None, None, "fsdp"),
        P("replica", "fsdp", None),
        P(None, None, "fsdp"),
        P("fsdp", None),
        P(None, None, "fsdp"),
        P("fsdp", None),
    )
    out_specs = (
        P(None, None, "fsdp"),
        P("fsdp", None),
        P(None, None, "fsdp"),
        P("fsdp", None),
        P("replica", None, None, "fsdp"),
        P("replica", "fsdp", None),
        P("replica", None, None, "fsdp"),
        P("replica", "fsdp", None),
    )
    return jax.shard_map(local, mesh=mesh, in_specs=in_specs, out_specs=out_specs, check_vma=False)
```

time: 158 us -> 137 us (0.87)
  waiting for transfers between devices: 73.1 us -> 56 us
  starting transfers between devices: 49.8 us -> 46.1 us
    ppermute x28 -> x29, waiting for transfers between devices: 65.3 us -> 37 us  [move(): return lax.ppermute(value, 'fsdp', pairs)]
    ppermute x3, waiting for transfers between devices: 7.79 us -> 19 us  [swap_replica(): return lax.ppermute(value, 'replica', [(0, 1), (1, 0)])]
    ppermute x28 -> x29, starting transfers between devices: 40.1 us -> 37 us  [move(): return lax.ppermute(value, 'fsdp', pairs)]
    pallas_call x10 -> x13, Pallas kernels: 19.8 us -> 20.2 us  [the longest x3 7 us: gradient(): pl.pallas_call(functools.partial(gradient_kernel, len(left), start), in_s...]
    unnamed x32 -> x40, local copies, waits for them, and re-layouts: 4.12 us -> 4.24 us
  transfers between devices with their start and end apart: 31 -> 32, of which waited for: 14 -> 15; matrix products, arithmetic and copies ran while one was open for 1% -> 1% of each run, Pallas kernels for 14% -> 16%
where the time goes in v3:
time: 137 us; the launch traced here: 136 us
  waiting for transfers between devices  56 us (41%)
  starting transfers between devices  46.1 us (34%)
  Pallas kernels  27.8 us (20%)
  local copies, waits for them, and re-layouts  5.32 us (4%)
    ppermute x29, waiting for transfers between devices, move(): return lax.ppermute(value, 'fsdp', pairs)  37 us
    ppermute x29, starting transfers between devices, move(): return lax.ppermute(value, 'fsdp', pairs)  37 us
    ppermute x3, waiting for transfers between devices, swap_replica(): return lax.ppermute(value, 'replica', [(0, 1), (1, 0)])  19 us
    ppermute x3, starting transfers between devices, swap_replica(): return lax.ppermute(value, 'replica', [(0, 1), (1, 0)])  9.09 us
    pallas_call x4, Pallas kernels, forward(): pl.pallas_call(functools.partial(forward_kernel, [(p[1], p[3]) for p in p...  7.65 us
    pallas_call x3, Pallas kernels, gradient(): pl.pallas_call(functools.partial(gradient_kernel, len(left), start), in_s...  7 us
    pallas_call x3, Pallas kernels, inner_step(): pl.pallas_call(functools.partial(inner_kernel, which, start), grid=(size...  6.91 us
    pallas_call x3, Pallas kernels, outer_step(): pl.pallas_call(functools.partial(outer_kernel, which, start), grid=(size...  5.6 us
  transfers between devices with their start and end apart: 32, of which 15 were waited for; matrix products, arithmetic and copies ran while one was open for 1% of the time, Pallas kernels for 16%

profile of v3, /device:TPU:1, one launch (start us, length us, event | category | flops | bytes accessed | tf_op | source)
XLA Modules:
  0.0 136.5 jit_solution(2439452432609841682)
XLA Ops:
  0.6 1.0 constant_dynamic-update-slice_fusion.1
  1.6 1.0 constant_dynamic-update-slice_fusion.refs_0_.refs_1_
  2.6 3.7 %collective-permute-start.1 = (bf16[2,64,2048]{2,1,0:T(8,128)(2,1)S(1)}, bf16[2,64,2048]{2,1,0:T(8,128)(2,1)S(1)}, u32[]{:S(2)}, u32[]{:S(2)}) collective-permute-start(bf16[2,64,2048]{2,1,0:T(8,128)(2,1)S(1)} %constant_dynamic-update-slice_fusion.refs_0_.refs_1_), channel_id=1, source_target_pairs={{0,32},{1,33},{2,34},{3,35},{4,36},{5,37},{6,38},{7,39},{8,40},{9,... | collective-permute-start | bytes 1572872 | tf_op jit(solution)/shard_map/ppermute | solution.py:34
  6.2 1.6 %collective-permute-start.11 = (bf16[2,64,2048]{2,1,0:T(8,128)(2,1)S(1)}, bf16[2,64,2048]{2,1,0:T(8,128)(2,1)S(1)}, u32[]{:S(2)}, u32[]{:S(2)}) collective-permute-start(bf16[2,64,2048]{2,1,0:T(8,128)(2,1)S(1)} %constant_dynamic-update-slice_fusion.refs_0_.refs_1_), channel_id=1, source_target_pairs={{0,8},{1,9},{2,10},{3,11},{4,12},{5,13},{6,14},{7,15},{8,0},{9,1},... | collective-permute-start | bytes 1572872 | tf_op jit(solution)/shard_map/ppermute | solution.py:34
  7.9 2.7 %collective-permute-start.6 = (bf16[2,64,2048]{2,1,0:T(8,128)(2,1)S(1)}, bf16[2,64,2048]{2,1,0:T(8,128)(2,1)S(1)}, u32[]{:S(2)}, u32[]{:S(2)}) collective-permute-start(bf16[2,64,2048]{2,1,0:T(8,128)(2,1)S(1)} %constant_dynamic-update-slice_fusion.refs_0_.refs_1_), channel_id=1, source_target_pairs={{0,6},{1,7},{2,0},{3,1},{4,2},{5,3},{6,4},{7,5},{8,14},{9,15},{10,... | collective-permute-start | bytes 1572872 | tf_op jit(solution)/shard_map/ppermute | solution.py:34
  10.6 1.6 %copy-done.1 = f32[1,2,2048,128]{3,2,1,0:T(8,128)S(1)} copy-done((f32[1,2,2048,128]{3,2,1,0:T(8,128)S(1)}, f32[1,2,2048,128]{3,2,1,0:T(8,128)}, u32[]{:S(2)}) %copy-start.1) | copy-done | bytes 2097176
  12.2 1.2 copy-done.4
  13.8 1.6 %collective-permute-start = (bf16[2,3,64,2048]{3,2,1,0:T(8,128)(2,1)S(1)}, bf16[2,3,64,2048]{3,2,1,0:T(8,128)(2,1)S(1)}, u32[]{:S(2)}, u32[]{:S(2)}) collective-permute-start(bf16[2,3,64,2048]{3,2,1,0:T(8,128)(2,1)S(1)} %get-tuple-element.76), channel_id=1, source_target_pairs={{0,1},{1,0},{2,3},{3,2},{4,5},{5,4},{6,7},{7,6},{8,9},{9,8},{10,11... | collective-permute-start | bytes 4718600 | tf_op jit(solution)/shard_map/ppermute | solution.py:34
  15.4 2.0 %collective-permute-done.1.refs_0_.refs_1_ = bf16[2,64,2048]{2,1,0:T(8,128)(2,1)S(1)} collective-permute-done((bf16[2,64,2048]{2,1,0:T(8,128)(2,1)S(1)}, bf16[2,64,2048]{2,1,0:T(8,128)(2,1)S(1)}, u32[]{:S(2)}, u32[]{:S(2)}) %collective-permute-start.1) | collective-permute-done | bytes 524320 | tf_op jit(solution)/shard_map/ppermute | solution.py:34
  17.4 1.7 %collective-permute-done.11.refs_0_.refs_1_ = bf16[2,64,2048]{2,1,0:T(8,128)(2,1)S(1)} collective-permute-done((bf16[2,64,2048]{2,1,0:T(8,128)(2,1)S(1)}, bf16[2,64,2048]{2,1,0:T(8,128)(2,1)S(1)}, u32[]{:S(2)}, u32[]{:S(2)}) %collective-permute-start.11) | collective-permute-done | bytes 524320 | tf_op jit(solution)/shard_map/ppermute | solution.py:34
  19.1 1.3 collective-permute-start.12
  20.7 1.8 %collective-permute-start.3 = (bf16[3,64,2048]{2,1,0:T(8,128)(2,1)S(1)}, bf16[3,64,2048]{2,1,0:T(8,128)(2,1)S(1)}, u32[]{:S(2)}, u32[]{:S(2)}) collective-permute-start(bf16[3,64,2048]{2,1,0:T(8,128)(2,1)S(1)} %get-tuple-element.80), channel_id=1, source_target_pairs={{0,48},{1,49},{2,50},{3,51},{4,52},{5,53},{6,54},{7,55},{8,56},{9,... | collective-permute-start | bytes 2359304 | tf_op jit(solution)/shard_map/ppermute | solution.py:34
  22.5 7.6 %collective-permute-done.5.refs_2_.refs_3_ = bf16[2,64,2048]{2,1,0:T(8,128)(2,1)S(1)} collective-permute-done((bf16[2,64,2048]{2,1,0:T(8,128)(2,1)S(1)}, bf16[2,64,2048]{2,1,0:T(8,128)(2,1)S(1)}, u32[]{:S(2)}, u32[]{:S(2)}) %collective-permute-start.5) | collective-permute-done | bytes 524320 | tf_op jit(solution)/shard_map/ppermute | solution.py:34
  30.8 1.3 collective-permute-start.7
  32.2 5.0 %collective-permute-done.2 = bf16[3,64,2048]{2,1,0:T(8,128)(2,1)S(1)} collective-permute-done((bf16[3,64,2048]{2,1,0:T(8,128)(2,1)S(1)}, bf16[3,64,2048]{2,1,0:T(8,128)(2,1)S(1)}, u32[]{:S(2)}, u32[]{:S(2)}) %collective-permute-start.2) | collective-permute-done | bytes 786464 | tf_op jit(solution)/shard_map/ppermute | solution.py:34
  37.6 0.9 collective-permute-done.3
  38.6 3.4 %collective-permute-start.4 = (bf16[2,3,64,2048]{3,2,1,0:T(8,128)(2,1)S(1)}, bf16[2,3,64,2048]{3,2,1,0:T(8,128)(2,1)S(1)}, u32[]{:S(2)}, u32[]{:S(2)}) collective-permute-start(bf16[2,3,64,2048]{3,2,1,0:T(8,128)(2,1)S(1)} %pad_maximum_fusion), channel_id=1, source_target_pairs={{0,1},{1,0},{2,3},{3,2},{4,5},{5,4},{6,7},{7,6},{8,9},{9,8},{10,11... | collective-permute-start | bytes 4718600 | tf_op jit(solution)/shard_map/ppermute | solution.py:34
  43.3 2.8 %collective-permute-start.15 = (bf16[2,64,2048]{2,1,0:T(8,128)(2,1)S(1)}, bf16[2,64,2048]{2,1,0:T(8,128)(2,1)S(1)}, u32[]{:S(2)}, u32[]{:S(2)}) collective-permute-start(bf16[2,64,2048]{2,1,0:T(8,128)(2,1)S(1)} %collective-permute-done.12.refs_2_.refs_3_), channel_id=1, source_target_pairs={{0,6},{1,7},{2,0},{3,1},{4,2},{5,3},{6,4},{7,5},{8,14},{9,15},{10,... | collective-permute-start | bytes 1572872 | tf_op jit(solution)/shard_map/ppermute | solution.py:34
  46.1 9.7 %collective-permute-done.8.refs_2_.refs_3_ = bf16[2,64,2048]{2,1,0:T(8,128)(2,1)S(1)} collective-permute-done((bf16[2,64,2048]{2,1,0:T(8,128)(2,1)S(1)}, bf16[2,64,2048]{2,1,0:T(8,128)(2,1)S(1)}, u32[]{:S(2)}, u32[]{:S(2)}) %collective-permute-start.8) | collective-permute-done | bytes 524320 | tf_op jit(solution)/shard_map/ppermute | solution.py:34
  55.9 0.9 collective-permute-start.10
  56.8 2.0 %collective-permute-done.13.refs_4_.refs_5_.refs_6_.refs_7_ = bf16[4,64,2048]{2,1,0:T(8,128)(2,1)S(1)} collective-permute-done((bf16[4,64,2048]{2,1,0:T(8,128)(2,1)S(1)}, bf16[4,64,2048]{2,1,0:T(8,128)(2,1)S(1)}, u32[]{:S(2)}, u32[]{:S(2)}) %collective-permute-start.13) | collective-permute-done | bytes 1048608 | tf_op jit(solution)/shard_map/ppermute | solution.py:34
  58.9 1.4 %collective-permute-start.18 = (bf16[1,64,2048]{2,1,0:T(8,128)(2,1)S(1)}, bf16[1,64,2048]{2,1,0:T(8,128)(2,1)S(1)}, u32[]{:S(2)}, u32[]{:S(2)}) collective-permute-start(bf16[1,64,2048]{2,1,0:T(8,128)(2,1)S(1)} %get-tuple-element.157), channel_id=1, source_target_pairs={{0,2},{1,3},{2,4},{3,5},{4,6},{5,7},{6,0},{7,1},{8,10},{9,11},{10,... | collective-permute-start | bytes 786440 | tf_op jit(solution)/shard_map/ppermute | solution.py:34
  60.2 1.5 %collective-permute-start.19 = (bf16[1,64,2048]{2,1,0:T(8,128)(2,1)S(1)}, bf16[1,64,2048]{2,1,0:T(8,128)(2,1)S(1)}, u32[]{:S(2)}, u32[]{:S(2)}) collective-permute-start(bf16[1,64,2048]{2,1,0:T(8,128)(2,1)S(1)} %get-tuple-element.156), channel_id=1, source_target_pairs={{0,6},{1,7},{2,0},{3,1},{4,2},{5,3},{6,4},{7,5},{8,14},{9,15},{10,... | collective-permute-start | bytes 786440 | tf_op jit(solution)/shard_map/ppermute | solution.py:34
  61.9 1.4 %collective-permute-start.17 = (bf16[1,64,2048]{2,1,0:T(8,128)(2,1)S(1)}, bf16[1,64,2048]{2,1,0:T(8,128)(2,1)S(1)}, u32[]{:S(2)}, u32[]{:S(2)}) collective-permute-start(bf16[1,64,2048]{2,1,0:T(8,128)(2,1)S(1)} %slice.167), channel_id=1, source_target_pairs={{0,6},{1,7},{2,0},{3,1},{4,2},{5,3},{6,4},{7,5},{8,14},{9,15},{10,... | collective-permute-start | bytes 786440 | tf_op jit(solution)/shard_map/ppermute | solution.py:34
  63.8 1.9 %forward.6 = (bf16[512,256]{1,0:T(8,128)(2,1)S(1)}, bf16[512,256]{1,0:T(8,128)(2,1)S(1)}, bf16[512,256]{1,0:T(8,128)(2,1)S(1)}, bf16[256,2048]{1,0:T(8,128)(2,1)S(1)}, bf16[256,2048]{1,0:T(8,128)(2,1)S(1)}) custom-call(bf16[1024,2048]{1,0:T(8,128)(2,1)S(1)} %get-tuple-element.145.in_ref, bf16[512,2048]{1,0:T(8,128)(2,1)S(1)} %get-tuple-element.144.down_ref, ...), custom_call_target="tpu_custom_call" | custom-call | flops 1610612736 | bytes 10485760 | tf_op jit(solution)/shard_map/forward/pallas_call | solution.py:122
  65.7 1.9 %forward.4 = (bf16[512,256]{1,0:T(8,128)(2,1)S(1)}, bf16[512,256]{1,0:T(8,128)(2,1)S(1)}, bf16[512,256]{1,0:T(8,128)(2,1)S(1)}, bf16[256,2048]{1,0:T(8,128)(2,1)S(1)}, bf16[256,2048]{1,0:T(8,128)(2,1)S(1)}) custom-call(bf16[1024,2048]{1,0:T(8,128)(2,1)S(1)} %get-tuple-element.145.in_ref, bf16[512,2048]{1,0:T(8,128)(2,1)S(1)} %get-tuple-element.144.down_ref, ...), custom_call_target="tpu_custom_call" | custom-call | flops 1610612736 | bytes 10485760 | tf_op jit(solution)/shard_map/forward/pallas_call | solution.py:122
  68.1 1.9 %forward.5 = (bf16[512,256]{1,0:T(8,128)(2,1)S(1)}, bf16[512,256]{1,0:T(8,128)(2,1)S(1)}, bf16[512,256]{1,0:T(8,128)(2,1)S(1)}, bf16[256,2048]{1,0:T(8,128)(2,1)S(1)}, bf16[256,2048]{1,0:T(8,128)(2,1)S(1)}) custom-call(bf16[1024,2048]{1,0:T(8,128)(2,1)S(1)} %get-tuple-element.145.in_ref, bf16[512,2048]{1,0:T(8,128)(2,1)S(1)} %get-tuple-element.144.down_ref, ...), custom_call_target="tpu_custom_call" | custom-call | flops 1610612736 | bytes 10485760 | tf_op jit(solution)/shard_map/forward/pallas_call | solution.py:122
  70.1 2.9 %collective-permute-done.16.refs_4_ = bf16[1,64,2048]{2,1,0:T(8,128)(2,1)S(1)} collective-permute-done((bf16[1,64,2048]{2,1,0:T(8,128)(2,1)S(1)}, bf16[1,64,2048]{2,1,0:T(8,128)(2,1)S(1)}, u32[]{:S(2)}, u32[]{:S(2)}) %collective-permute-start.16) | collective-permute-done | bytes 262176 | tf_op jit(solution)/shard_map/ppermute | solution.py:34
  72.9 1.9 %forward.7 = (bf16[512,256]{1,0:T(8,128)(2,1)S(1)}, bf16[512,256]{1,0:T(8,128)(2,1)S(1)}, bf16[512,256]{1,0:T(8,128)(2,1)S(1)}, bf16[256,2048]{1,0:T(8,128)(2,1)S(1)}, bf16[256,2048]{1,0:T(8,128)(2,1)S(1)}) custom-call(bf16[1024,2048]{1,0:T(8,128)(2,1)S(1)} %get-tuple-element.145.in_ref, bf16[512,2048]{1,0:T(8,128)(2,1)S(1)} %get-tuple-element.144.down_ref, ...), custom_call_target="tpu_custom_call" | custom-call | flops 1610612736 | bytes 10485760 | tf_op jit(solution)/shard_map/forward/pallas_call | solution.py:122
  74.8 2.3 %gradient.4 = (f32[128,2048]{1,0:T(8,128)S(1)}, f32[128,2048]{1,0:T(8,128)S(1)}, bf16[2,128,2048]{2,1,0:T(8,128)(2,1)S(1)}) custom-call(bf16[512,256]{1,0:T(8,128)(2,1)S(1)} %get-tuple-element.103.refs_0_, bf16[512,256]{1,0:T(8,128)(2,1)S(1)} %get-tuple-element.104.refs_1_, bf16[512,256]{1,0:T(8,128)(2,1)S(1)} %get-tuple-element.105.refs_2_, ...), custom_call_target="tpu_custom_call" | custom-call | flops 2147483648 | bytes 8388608 | tf_op jit(solution)/shard_map/gradient/pallas_call | solution.py:161
  77.2 3.3 %collective-permute-start.23 = (bf16[2,128,2048]{2,1,0:T(8,128)(2,1)S(1)}, bf16[2,128,2048]{2,1,0:T(8,128)(2,1)S(1)}, u32[]{:S(2)}, u32[]{:S(2)}) collective-permute-start(bf16[2,128,2048]{2,1,0:T(8,128)(2,1)S(1)} %get-tuple-element.108), channel_id=1, source_target_pairs={{0,1},{1,0},{2,3},{3,2},{4,5},{5,4},{6,7},{7,6},{8,9},{9,8},{10,11... | collective-permute-start | bytes 3145736 | tf_op jit(solution)/shard_map/ppermute | solution.py:34
  80.4 2.3 %gradient.3 = (f32[128,2048]{1,0:T(8,128)S(1)}, f32[128,2048]{1,0:T(8,128)S(1)}, bf16[2,128,2048]{2,1,0:T(8,128)(2,1)S(1)}) custom-call(bf16[512,256]{1,0:T(8,128)(2,1)S(1)} %get-tuple-element.81.refs_0_, bf16[512,256]{1,0:T(8,128)(2,1)S(1)} %get-tuple-element.85.refs_1_, bf16[512,256]{1,0:T(8,128)(2,1)S(1)} %get-tuple-element.88.refs_2_, ...), custom_call_target="tpu_custom_call" | custom-call | flops 2147483648 | bytes 8388608 | tf_op jit(solution)/shard_map/gradient/pallas_call | solution.py:161
  82.9 2.3 %gradient.5 = (f32[128,2048]{1,0:T(8,128)S(1)}, f32[128,2048]{1,0:T(8,128)S(1)}, bf16[2,128,2048]{2,1,0:T(8,128)(2,1)S(1)}) custom-call(bf16[512,256]{1,0:T(8,128)(2,1)S(1)} %get-tuple-element.123.refs_0_, bf16[512,256]{1,0:T(8,128)(2,1)S(1)} %get-tuple-element.124.refs_1_, bf16[512,256]{1,0:T(8,128)(2,1)S(1)} %get-tuple-element.125.refs_2_, ...), custom_call_target="tpu_custom_call" | custom-call | flops 2147483648 | bytes 8388608 | tf_op jit(solution)/shard_map/gradient/pallas_call | solution.py:161
  86.3 2.1 %collective-permute-start.25 = (bf16[64,2048]{1,0:T(8,128)(2,1)S(1)}, bf16[64,2048]{1,0:T(8,128)(2,1)S(1)}, u32[]{:S(2)}, u32[]{:S(2)}) collective-permute-start(bf16[64,2048]{1,0:T(8,128)(2,1)S(1)} %get-tuple-element.111), channel_id=1, source_target_pairs={{0,48},{1,49},{2,50},{3,51},{4,52},{5,53},{6,54},{7,55},{8,56},{9,... | collective-permute-start | bytes 786440 | tf_op jit(solution)/shard_map/ppermute | solution.py:34
  88.9 0.8 collective-permute-start.22
  90.5 3.4 %collective-permute-done.24.refs_2_ = bf16[64,2048]{1,0:T(8,128)(2,1)S(1)} collective-permute-done((bf16[64,2048]{1,0:T(8,128)(2,1)S(1)}, bf16[64,2048]{1,0:T(8,128)(2,1)S(1)}, u32[]{:S(2)}, u32[]{:S(2)}) %collective-permute-start.24) | collective-permute-done | bytes 262176 | tf_op jit(solution)/shard_map/ppermute | solution.py:34
  93.9 1.9 %collective-permute-start.30 = (bf16[64,2048]{1,0:T(8,128)(2,1)S(1)}, bf16[64,2048]{1,0:T(8,128)(2,1)S(1)}, u32[]{:S(2)}, u32[]{:S(2)}) collective-permute-start(bf16[64,2048]{1,0:T(8,128)(2,1)S(1)} %get-tuple-element.135), channel_id=1, source_target_pairs={{0,48},{1,49},{2,50},{3,51},{4,52},{5,53},{6,54},{7,55},{8,56},{9,... | collective-permute-start | bytes 786440 | tf_op jit(solution)/shard_map/ppermute | solution.py:34
  95.8 2.3 %inner_step.3 = (bf16[1,2,2048,128]{3,2,1,0:T(8,128)(2,1)}, bf16[1,2,2048,128]{3,2,1,0:T(8,128)(2,1)}, bf16[2048,128]{1,0:T(8,128)(2,1)S(1)}) custom-call(f32[128,2048]{1,0:T(8,128)S(1)} %get-tuple-element.107.refs_0_, bf16[2,128,2048]{2,1,0:T(8,128)(2,1)S(1)} %collective-permute-done.23.core_ref.refs_1_, ...), custom_call_target="tpu_custom_call" | custom-call | flops 5242880 | bytes 6815744 | tf_op jit(solution)/shard_map/inner_step/pallas_call | solution.py:245
  98.1 3.3 %collective-permute-start.27 = (bf16[2048,128]{1,0:T(8,128)(2,1)S(1)}, bf16[2048,128]{1,0:T(8,128)(2,1)S(1)}, u32[]{:S(2)}, u32[]{:S(2)}) collective-permute-start(bf16[2048,128]{1,0:T(8,128)(2,1)S(1)} %get-tuple-element.115.refs_0_), channel_id=1, source_target_pairs={{0,64},{64,0},{1,65},{65,1},{2,66},{66,2},{3,67},{67,3},{4,68},{68... | collective-permute-start | bytes 1572872 | tf_op jit(solution)/shard_map/ppermute | solution.py:63
  101.5 2.3 %inner_step.4 = (bf16[1,2,2048,128]{3,2,1,0:T(8,128)(2,1)}, bf16[1,2,2048,128]{3,2,1,0:T(8,128)(2,1)}, bf16[2048,128]{1,0:T(8,128)(2,1)S(1)}) custom-call(f32[128,2048]{1,0:T(8,128)S(1)} %get-tuple-element.98.refs_0_, bf16[2,128,2048]{2,1,0:T(8,128)(2,1)S(1)} %collective-permute-done.20.core_ref.refs_1_, ...), custom_call_target="tpu_custom_call", output_to_operand_aliasing={{0}: (8, {}), {1}: (9, {})} | custom-call | flops 5242880 | bytes 6815744 | tf_op jit(solution)/shard_map/inner_step/pallas_call | solution.py:245
  103.8 2.5 %collective-permute-start.26 = (bf16[2048,128]{1,0:T(8,128)(2,1)S(1)}, bf16[2048,128]{1,0:T(8,128)(2,1)S(1)}, u32[]{:S(2)}, u32[]{:S(2)}) collective-permute-start(bf16[2048,128]{1,0:T(8,128)(2,1)S(1)} %get-tuple-element.114.refs_0_), channel_id=1, source_target_pairs={{0,64},{64,0},{1,65},{65,1},{2,66},{66,2},{3,67},{67,3},{4,68},{68... | collective-permute-start | bytes 1572872 | tf_op jit(solution)/shard_map/ppermute | solution.py:63
  106.4 2.2 %inner_step.5 = (bf16[1,128,2048]{2,1,0:T(8,128)(2,1)}, bf16[1,128,2048]{2,1,0:T(8,128)(2,1)}, bf16[128,2048]{1,0:T(8,128)(2,1)S(1)}) custom-call(f32[128,2048]{1,0:T(8,128)S(1)} %get-tuple-element.131.refs_0_, bf16[2,128,2048]{2,1,0:T(8,128)(2,1)S(1)} %collective-permute-done.28.core_ref.refs_1_, bf16[64,2048]{1,0:T(8,128)(2,1)S(1)} %collective-permute-done.29.refs_2_, ...), custom_call_target="tpu_custom_call" | custom-call | flops 5242880 | bytes 6815744 | tf_op jit(solution)/shard_map/inner_step/pallas_call | solution.py:245
  108.7 3.2 %collective-permute-start.31 = (bf16[128,2048]{1,0:T(8,128)(2,1)S(1)}, bf16[128,2048]{1,0:T(8,128)(2,1)S(1)}, u32[]{:S(2)}, u32[]{:S(2)}) collective-permute-start(bf16[128,2048]{1,0:T(8,128)(2,1)S(1)} %get-tuple-element.136.refs_0_), channel_id=1, source_target_pairs={{0,64},{64,0},{1,65},{65,1},{2,66},{66,2},{3,67},{67,3},{4,68},{68... | collective-permute-start | bytes 1572872 | tf_op jit(solution)/shard_map/ppermute | solution.py:63
  112.1 1.9 %outer_step.3 = (f32[2,2048,128]{2,1,0:T(8,128)}, f32[2,2048,128]{2,1,0:T(8,128)}) custom-call(bf16[2048,128]{1,0:T(8,128)(2,1)S(1)} %get-tuple-element.115.refs_0_, bf16[2048,128]{1,0:T(8,128)(2,1)S(1)} %collective-permute-done.27.refs_1_, f32[2,2048,128]{2,1,0:T(8,128)S(1)} %copy-done, f32[2,2048,128]{2,1,0:T(8,128)S(1)} %copy-done.3), custom_call_target="tpu_custom_call" | custom-call | flops 2097152 | bytes 5242880 | tf_op jit(solution)/shard_map/outer_step/pallas_call | solution.py:284
  114.0 9.4 %collective-permute-done.26.refs_1_ = bf16[2048,128]{1,0:T(8,128)(2,1)S(1)} collective-permute-done((bf16[2048,128]{1,0:T(8,128)(2,1)S(1)}, bf16[2048,128]{1,0:T(8,128)(2,1)S(1)}, u32[]{:S(2)}, u32[]{:S(2)}) %collective-permute-start.26) | collective-permute-done | bytes 524320 | tf_op jit(solution)/shard_map/ppermute | solution.py:63
  123.4 1.9 %outer_step.4 = (f32[2,2048,128]{2,1,0:T(8,128)}, f32[2,2048,128]{2,1,0:T(8,128)}) custom-call(bf16[2048,128]{1,0:T(8,128)(2,1)S(1)} %get-tuple-element.114.refs_0_, bf16[2048,128]{1,0:T(8,128)(2,1)S(1)} %collective-permute-done.26.refs_1_, f32[2,2048,128]{2,1,0:T(8,128)S(1)} %copy-done, ...), custom_call_target="tpu_custom_call", output_to_operand_aliasing={{0}: (4, {}), {1}: (5, {})} | custom-call | flops 2097152 | bytes 5242880 | tf_op jit(solution)/shard_map/outer_step/pallas_call | solution.py:284
  125.2 9.4 %collective-permute-done.31.refs_1_ = bf16[128,2048]{1,0:T(8,128)(2,1)S(1)} collective-permute-done((bf16[128,2048]{1,0:T(8,128)(2,1)S(1)}, bf16[128,2048]{1,0:T(8,128)(2,1)S(1)}, u32[]{:S(2)}, u32[]{:S(2)}) %collective-permute-start.31) | collective-permute-done | bytes 524320 | tf_op jit(solution)/shard_map/ppermute | solution.py:63
  134.6 1.9 %outer_step.5 = (f32[128,2048]{1,0:T(8,128)}, f32[128,2048]{1,0:T(8,128)}) custom-call(bf16[128,2048]{1,0:T(8,128)(2,1)S(1)} %get-tuple-element.136.refs_0_, bf16[128,2048]{1,0:T(8,128)(2,1)S(1)} %collective-permute-done.31.refs_1_, f32[128,2048]{1,0:T(8,128)S(1)} %copy-done.6, f32[128,2048]{1,0:T(8,128)S(1)} %copy-done.9), custom_call_target="tpu_custom_call" | custom-call | flops 2097152 | bytes 5242880 | tf_op jit(solution)/shard_map/outer_step/pallas_call | solution.py:284
  (80 shorter events, 7.1 us)
Async XLA Ops:
  2.6 14.8 %collective-permute-start.1 = (bf16[2,64,2048]{2,1,0:T(8,128)(2,1)S(1)}, bf16[2,64,2048]{2,1,0:T(8,128)(2,1)S(1)}, u32[]{:S(2)}, u32[]{:S(2)}) collective-permute-start(bf16[2,64,2048]{2,1,0:T(8,128)(2,1)S(1)} %constant_dynamic-update-slice_fusion.refs_0_.refs_1_), channel_id=1, source_target_pairs={{0,32},{1,33},{2,34},{3,35},{4,36},{5,37},{6,38},{7,39},{8,40},{9,... | collective-permute-start | bytes 1572872 | tf_op jit(solution)/shard_map/ppermute | solution.py:34
  6.2 12.8 %collective-permute-start.11 = (bf16[2,64,2048]{2,1,0:T(8,128)(2,1)S(1)}, bf16[2,64,2048]{2,1,0:T(8,128)(2,1)S(1)}, u32[]{:S(2)}, u32[]{:S(2)}) collective-permute-start(bf16[2,64,2048]{2,1,0:T(8,128)(2,1)S(1)} %constant_dynamic-update-slice_fusion.refs_0_.refs_1_), channel_id=1, source_target_pairs={{0,8},{1,9},{2,10},{3,11},{4,12},{5,13},{6,14},{7,15},{8,0},{9,1},... | collective-permute-start | bytes 1572872 | tf_op jit(solution)/shard_map/ppermute | solution.py:34
  7.9 12.8 %collective-permute-start.6 = (bf16[2,64,2048]{2,1,0:T(8,128)(2,1)S(1)}, bf16[2,64,2048]{2,1,0:T(8,128)(2,1)S(1)}, u32[]{:S(2)}, u32[]{:S(2)}) collective-permute-start(bf16[2,64,2048]{2,1,0:T(8,128)(2,1)S(1)} %constant_dynamic-update-slice_fusion.refs_0_.refs_1_), channel_id=1, source_target_pairs={{0,6},{1,7},{2,0},{3,1},{4,2},{5,3},{6,4},{7,5},{8,14},{9,15},{10,... | collective-permute-start | bytes 1572872 | tf_op jit(solution)/shard_map/ppermute | solution.py:34
  10.6 1.6 %copy-start.1 = (f32[1,2,2048,128]{3,2,1,0:T(8,128)S(1)}, f32[1,2,2048,128]{3,2,1,0:T(8,128)}, u32[]{:S(2)}) copy-start(f32[1,2,2048,128]{3,2,1,0:T(8,128)} %refs_4_.4) | copy-start | bytes 6291460
  12.2 1.2 copy-start.4
  13.8 29.5 %collective-permute-start = (bf16[2,3,64,2048]{3,2,1,0:T(8,128)(2,1)S(1)}, bf16[2,3,64,2048]{3,2,1,0:T(8,128)(2,1)S(1)}, u32[]{:S(2)}, u32[]{:S(2)}) collective-permute-start(bf16[2,3,64,2048]{3,2,1,0:T(8,128)(2,1)S(1)} %get-tuple-element.76), channel_id=1, source_target_pairs={{0,1},{1,0},{2,3},{3,2},{4,5},{5,4},{6,7},{7,6},{8,9},{9,8},{10,11... | collective-permute-start | bytes 4718600 | tf_op jit(solution)/shard_map/ppermute | solution.py:34
  15.4 14.7 %collective-permute-start.5 = (bf16[2,64,2048]{2,1,0:T(8,128)(2,1)S(1)}, bf16[2,64,2048]{2,1,0:T(8,128)(2,1)S(1)}, u32[]{:S(2)}, u32[]{:S(2)}) collective-permute-start(bf16[2,64,2048]{2,1,0:T(8,128)(2,1)S(1)} %constant_dynamic-update-slice_fusion.refs_0_.refs_1_), channel_id=1, source_target_pairs={{0,2},{1,3},{2,4},{3,5},{4,6},{5,7},{6,0},{7,1},{8,10},{9,11},{10,... | collective-permute-start | bytes 1572872 | tf_op jit(solution)/shard_map/ppermute | solution.py:34
  19.1 11.7 %collective-permute-start.12 = (bf16[2,64,2048]{2,1,0:T(8,128)(2,1)S(1)}, bf16[2,64,2048]{2,1,0:T(8,128)(2,1)S(1)}, u32[]{:S(2)}, u32[]{:S(2)}) collective-permute-start(bf16[2,64,2048]{2,1,0:T(8,128)(2,1)S(1)} %collective-permute-done.1.refs_0_.refs_1_), channel_id=1, source_target_pairs={{0,8},{1,9},{2,10},{3,11},{4,12},{5,13},{6,14},{7,15},{8,0},{9,1},... | collective-permute-start | bytes 1572872 | tf_op jit(solution)/shard_map/ppermute | solution.py:34
  20.3 16.9 %collective-permute-start.2 = (bf16[3,64,2048]{2,1,0:T(8,128)(2,1)S(1)}, bf16[3,64,2048]{2,1,0:T(8,128)(2,1)S(1)}, u32[]{:S(2)}, u32[]{:S(2)}) collective-permute-start(bf16[3,64,2048]{2,1,0:T(8,128)(2,1)S(1)} %get-tuple-element.79), channel_id=1, source_target_pairs={{0,16},{1,17},{2,18},{3,19},{4,20},{5,21},{6,22},{7,23},{8,24},{9,... | collective-permute-start | bytes 2359304 | tf_op jit(solution)/shard_map/ppermute | solution.py:34
  20.7 17.8 %collective-permute-start.3 = (bf16[3,64,2048]{2,1,0:T(8,128)(2,1)S(1)}, bf16[3,64,2048]{2,1,0:T(8,128)(2,1)S(1)}, u32[]{:S(2)}, u32[]{:S(2)}) collective-permute-start(bf16[3,64,2048]{2,1,0:T(8,128)(2,1)S(1)} %get-tuple-element.80), channel_id=1, source_target_pairs={{0,48},{1,49},{2,50},{3,51},{4,52},{5,53},{6,54},{7,55},{8,56},{9,... | collective-permute-start | bytes 2359304 | tf_op jit(solution)/shard_map/ppermute | solution.py:34
  30.1 12.6 %collective-permute-start.9 = (bf16[2,64,2048]{2,1,0:T(8,128)(2,1)S(1)}, bf16[2,64,2048]{2,1,0:T(8,128)(2,1)S(1)}, u32[]{:S(2)}, u32[]{:S(2)}) collective-permute-start(bf16[2,64,2048]{2,1,0:T(8,128)(2,1)S(1)} %collective-permute-done.1.refs_0_.refs_1_), channel_id=1, source_target_pairs={{0,6},{1,7},{2,0},{3,1},{4,2},{5,3},{6,4},{7,5},{8,14},{9,15},{10,... | collective-permute-start | bytes 1572872 | tf_op jit(solution)/shard_map/ppermute | solution.py:34
  30.8 15.2 %collective-permute-start.7 = (bf16[2,64,2048]{2,1,0:T(8,128)(2,1)S(1)}, bf16[2,64,2048]{2,1,0:T(8,128)(2,1)S(1)}, u32[]{:S(2)}, u32[]{:S(2)}) collective-permute-start(bf16[2,64,2048]{2,1,0:T(8,128)(2,1)S(1)} %collective-permute-done.5.refs_2_.refs_3_), channel_id=1, source_target_pairs={{0,2},{1,3},{2,4},{3,5},{4,6},{5,7},{6,0},{7,1},{8,10},{9,11},{10,... | collective-permute-start | bytes 1572872 | tf_op jit(solution)/shard_map/ppermute | solution.py:34
  37.2 21.6 %collective-permute-start.13 = (bf16[4,64,2048]{2,1,0:T(8,128)(2,1)S(1)}, bf16[4,64,2048]{2,1,0:T(8,128)(2,1)S(1)}, u32[]{:S(2)}, u32[]{:S(2)}) collective-permute-start(bf16[4,64,2048]{2,1,0:T(8,128)(2,1)S(1)} %pad_maximum_fusion.1), channel_id=1, source_target_pairs={{0,8},{1,9},{2,10},{3,11},{4,12},{5,13},{6,14},{7,15},{8,0},{9,1},... | collective-permute-start | bytes 3145736 | tf_op jit(solution)/shard_map/ppermute | solution.py:34
  38.6 23.2 %collective-permute-start.4 = (bf16[2,3,64,2048]{3,2,1,0:T(8,128)(2,1)S(1)}, bf16[2,3,64,2048]{3,2,1,0:T(8,128)(2,1)S(1)}, u32[]{:S(2)}, u32[]{:S(2)}) collective-permute-start(bf16[2,3,64,2048]{3,2,1,0:T(8,128)(2,1)S(1)} %pad_maximum_fusion), channel_id=1, source_target_pairs={{0,1},{1,0},{2,3},{3,2},{4,5},{5,4},{6,7},{7,6},{8,9},{9,8},{10,11... | collective-permute-start | bytes 4718600 | tf_op jit(solution)/shard_map/ppermute | solution.py:34
  42.7 13.2 %collective-permute-start.8 = (bf16[2,64,2048]{2,1,0:T(8,128)(2,1)S(1)}, bf16[2,64,2048]{2,1,0:T(8,128)(2,1)S(1)}, u32[]{:S(2)}, u32[]{:S(2)}) collective-permute-start(bf16[2,64,2048]{2,1,0:T(8,128)(2,1)S(1)} %collective-permute-done.5.refs_2_.refs_3_), channel_id=1, source_target_pairs={{0,32},{1,33},{2,34},{3,35},{4,36},{5,37},{6,38},{7,39},{8,40},{9,... | collective-permute-start | bytes 1572872 | tf_op jit(solution)/shard_map/ppermute | solution.py:34
  43.3 16.9 %collective-permute-start.15 = (bf16[2,64,2048]{2,1,0:T(8,128)(2,1)S(1)}, bf16[2,64,2048]{2,1,0:T(8,128)(2,1)S(1)}, u32[]{:S(2)}, u32[]{:S(2)}) collective-permute-start(bf16[2,64,2048]{2,1,0:T(8,128)(2,1)S(1)} %collective-permute-done.12.refs_2_.refs_3_), channel_id=1, source_target_pairs={{0,6},{1,7},{2,0},{3,1},{4,2},{5,3},{6,4},{7,5},{8,14},{9,15},{10,... | collective-permute-start | bytes 1572872 | tf_op jit(solution)/shard_map/ppermute | solution.py:34
  46.0 15.7 %collective-permute-start.14 = (bf16[2,64,2048]{2,1,0:T(8,128)(2,1)S(1)}, bf16[2,64,2048]{2,1,0:T(8,128)(2,1)S(1)}, u32[]{:S(2)}, u32[]{:S(2)}) collective-permute-start(bf16[2,64,2048]{2,1,0:T(8,128)(2,1)S(1)} %collective-permute-done.12.refs_2_.refs_3_), channel_id=1, source_target_pairs={{0,2},{1,3},{2,4},{3,5},{4,6},{5,7},{6,0},{7,1},{8,10},{9,11},{10,... | collective-permute-start | bytes 1572872 | tf_op jit(solution)/shard_map/ppermute | solution.py:34
  55.9 12.2 %collective-permute-start.10 = (bf16[2,64,2048]{2,1,0:T(8,128)(2,1)S(1)}, bf16[2,64,2048]{2,1,0:T(8,128)(2,1)S(1)}, u32[]{:S(2)}, u32[]{:S(2)}) collective-permute-start(bf16[2,64,2048]{2,1,0:T(8,128)(2,1)S(1)} %collective-permute-done.7.refs_6_.refs_7_), channel_id=1, source_target_pairs={{0,32},{1,33},{2,34},{3,35},{4,36},{5,37},{6,38},{7,39},{8,40},{9,... | collective-permute-start | bytes 1572872 | tf_op jit(solution)/shard_map/ppermute | solution.py:34
  58.9 11.2 %collective-permute-start.18 = (bf16[1,64,2048]{2,1,0:T(8,128)(2,1)S(1)}, bf16[1,64,2048]{2,1,0:T(8,128)(2,1)S(1)}, u32[]{:S(2)}, u32[]{:S(2)}) collective-permute-start(bf16[1,64,2048]{2,1,0:T(8,128)(2,1)S(1)} %get-tuple-element.157), channel_id=1, source_target_pairs={{0,2},{1,3},{2,4},{3,5},{4,6},{5,7},{6,0},{7,1},{8,10},{9,11},{10,... | collective-permute-start | bytes 786440 | tf_op jit(solution)/shard_map/ppermute | solution.py:34
  60.2 9.8 %collective-permute-start.19 = (bf16[1,64,2048]{2,1,0:T(8,128)(2,1)S(1)}, bf16[1,64,2048]{2,1,0:T(8,128)(2,1)S(1)}, u32[]{:S(2)}, u32[]{:S(2)}) collective-permute-start(bf16[1,64,2048]{2,1,0:T(8,128)(2,1)S(1)} %get-tuple-element.156), channel_id=1, source_target_pairs={{0,6},{1,7},{2,0},{3,1},{4,2},{5,3},{6,4},{7,5},{8,14},{9,15},{10,... | collective-permute-start | bytes 786440 | tf_op jit(solution)/shard_map/ppermute | solution.py:34
  61.9 8.1 %collective-permute-start.17 = (bf16[1,64,2048]{2,1,0:T(8,128)(2,1)S(1)}, bf16[1,64,2048]{2,1,0:T(8,128)(2,1)S(1)}, u32[]{:S(2)}, u32[]{:S(2)}) collective-permute-start(bf16[1,64,2048]{2,1,0:T(8,128)(2,1)S(1)} %slice.167), channel_id=1, source_target_pairs={{0,6},{1,7},{2,0},{3,1},{4,2},{5,3},{6,4},{7,5},{8,14},{9,15},{10,... | collective-permute-start | bytes 786440 | tf_op jit(solution)/shard_map/ppermute | solution.py:34
  63.4 9.5 %collective-permute-start.16 = (bf16[1,64,2048]{2,1,0:T(8,128)(2,1)S(1)}, bf16[1,64,2048]{2,1,0:T(8,128)(2,1)S(1)}, u32[]{:S(2)}, u32[]{:S(2)}) collective-permute-start(bf16[1,64,2048]{2,1,0:T(8,128)(2,1)S(1)} %slice.166), channel_id=1, source_target_pairs={{0,2},{1,3},{2,4},{3,5},{4,6},{5,7},{6,0},{7,1},{8,10},{9,11},{10,... | collective-permute-start | bytes 786440 | tf_op jit(solution)/shard_map/ppermute | solution.py:34
  77.2 5.7 %collective-permute-start.23 = (bf16[2,128,2048]{2,1,0:T(8,128)(2,1)S(1)}, bf16[2,128,2048]{2,1,0:T(8,128)(2,1)S(1)}, u32[]{:S(2)}, u32[]{:S(2)}) collective-permute-start(bf16[2,128,2048]{2,1,0:T(8,128)(2,1)S(1)} %get-tuple-element.108), channel_id=1, source_target_pairs={{0,1},{1,0},{2,3},{3,2},{4,5},{5,4},{6,7},{7,6},{8,9},{9,8},{10,11... | collective-permute-start | bytes 3145736 | tf_op jit(solution)/shard_map/ppermute | solution.py:34
  82.8 5.6 %collective-permute-start.20 = (bf16[2,128,2048]{2,1,0:T(8,128)(2,1)S(1)}, bf16[2,128,2048]{2,1,0:T(8,128)(2,1)S(1)}, u32[]{:S(2)}, u32[]{:S(2)}) collective-permute-start(bf16[2,128,2048]{2,1,0:T(8,128)(2,1)S(1)} %get-tuple-element.99), channel_id=1, source_target_pairs={{0,1},{1,0},{2,3},{3,2},{4,5},{5,4},{6,7},{7,6},{8,9},{9,8},{10,11... | collective-permute-start | bytes 3145736 | tf_op jit(solution)/shard_map/ppermute | solution.py:34
  85.2 4.5 %collective-permute-start.28 = (bf16[2,128,2048]{2,1,0:T(8,128)(2,1)S(1)}, bf16[2,128,2048]{2,1,0:T(8,128)(2,1)S(1)}, u32[]{:S(2)}, u32[]{:S(2)}) collective-permute-start(bf16[2,128,2048]{2,1,0:T(8,128)(2,1)S(1)} %get-tuple-element.132), channel_id=1, source_target_pairs={{0,1},{1,0},{2,3},{3,2},{4,5},{5,4},{6,7},{7,6},{8,9},{9,8},{10,11... | collective-permute-start | bytes 3145736 | tf_op jit(solution)/shard_map/ppermute | solution.py:34
  85.8 10.0 %copy-start.7 = (bf16[1,2,2048,128]{3,2,1,0:T(8,128)(2,1)S(1)}, bf16[1,2,2048,128]{3,2,1,0:T(8,128)(2,1)}, u32[]{:S(2)}) copy-start(bf16[1,2,2048,128]{3,2,1,0:T(8,128)(2,1)} %refs_5_.4) | copy-start | bytes 3145732
  85.8 10.0 %copy-start.8 = (bf16[1,2,2048,128]{3,2,1,0:T(8,128)(2,1)S(1)}, bf16[1,2,2048,128]{3,2,1,0:T(8,128)(2,1)}, u32[]{:S(2)}) copy-start(bf16[1,2,2048,128]{3,2,1,0:T(8,128)(2,1)} %refs_6_.4) | copy-start | bytes 3145732
  85.9 8.0 %collective-permute-start.24 = (bf16[64,2048]{1,0:T(8,128)(2,1)S(1)}, bf16[64,2048]{1,0:T(8,128)(2,1)S(1)}, u32[]{:S(2)}, u32[]{:S(2)}) collective-permute-start(bf16[64,2048]{1,0:T(8,128)(2,1)S(1)} %get-tuple-element.110), channel_id=1, source_target_pairs={{0,16},{1,17},{2,18},{3,19},{4,20},{5,21},{6,22},{7,23},{8,24},{9,... | collective-permute-start | bytes 786440 | tf_op jit(solution)/shard_map/ppermute | solution.py:34
  86.3 9.5 %collective-permute-start.25 = (bf16[64,2048]{1,0:T(8,128)(2,1)S(1)}, bf16[64,2048]{1,0:T(8,128)(2,1)S(1)}, u32[]{:S(2)}, u32[]{:S(2)}) collective-permute-start(bf16[64,2048]{1,0:T(8,128)(2,1)S(1)} %get-tuple-element.111), channel_id=1, source_target_pairs={{0,48},{1,49},{2,50},{3,51},{4,52},{5,53},{6,54},{7,55},{8,56},{9,... | collective-permute-start | bytes 786440 | tf_op jit(solution)/shard_map/ppermute | solution.py:34
  88.4 7.4 %copy-start = (f32[2,2048,128]{2,1,0:T(8,128)S(1)}, f32[2,2048,128]{2,1,0:T(8,128)}, u32[]{:S(2)}) copy-start(f32[2,2048,128]{2,1,0:T(8,128)} %refs_2_.4) | copy-start | bytes 6291460
  88.4 7.4 %copy-start.2 = (f32[1,2,2048,128]{3,2,1,0:T(8,128)S(1)}, f32[1,2,2048,128]{3,2,1,0:T(8,128)}, u32[]{:S(2)}) copy-start(f32[1,2,2048,128]{3,2,1,0:T(8,128)} %refs_4_.4) | copy-start | bytes 6291460
  88.5 12.9 %collective-permute-start.21 = (bf16[64,2048]{1,0:T(8,128)(2,1)S(1)}, bf16[64,2048]{1,0:T(8,128)(2,1)S(1)}, u32[]{:S(2)}, u32[]{:S(2)}) collective-permute-start(bf16[64,2048]{1,0:T(8,128)(2,1)S(1)} %get-tuple-element.101), channel_id=1, source_target_pairs={{0,16},{1,17},{2,18},{3,19},{4,20},{5,21},{6,22},{7,23},{8,24},{9,... | collective-permute-start | bytes 786440 | tf_op jit(solution)/shard_map/ppermute | solution.py:34
  88.9 12.5 %collective-permute-start.22 = (bf16[64,2048]{1,0:T(8,128)(2,1)S(1)}, bf16[64,2048]{1,0:T(8,128)(2,1)S(1)}, u32[]{:S(2)}, u32[]{:S(2)}) collective-permute-start(bf16[64,2048]{1,0:T(8,128)(2,1)S(1)} %get-tuple-element.102), channel_id=1, source_target_pairs={{0,48},{1,49},{2,50},{3,51},{4,52},{5,53},{6,54},{7,55},{8,56},{9,... | collective-permute-start | bytes 786440 | tf_op jit(solution)/shard_map/ppermute | solution.py:34
  89.8 16.6 %collective-permute-start.29 = (bf16[64,2048]{1,0:T(8,128)(2,1)S(1)}, bf16[64,2048]{1,0:T(8,128)(2,1)S(1)}, u32[]{:S(2)}, u32[]{:S(2)}) collective-permute-start(bf16[64,2048]{1,0:T(8,128)(2,1)S(1)} %get-tuple-element.134), channel_id=1, source_target_pairs={{0,16},{1,17},{2,18},{3,19},{4,20},{5,21},{6,22},{7,23},{8,24},{9,... | collective-permute-start | bytes 786440 | tf_op jit(solution)/shard_map/ppermute | solution.py:34
  93.9 12.5 %collective-permute-start.30 = (bf16[64,2048]{1,0:T(8,128)(2,1)S(1)}, bf16[64,2048]{1,0:T(8,128)(2,1)S(1)}, u32[]{:S(2)}, u32[]{:S(2)}) collective-permute-start(bf16[64,2048]{1,0:T(8,128)(2,1)S(1)} %get-tuple-element.135), channel_id=1, source_target_pairs={{0,48},{1,49},{2,50},{3,51},{4,52},{5,53},{6,54},{7,55},{8,56},{9,... | collective-permute-start | bytes 786440 | tf_op jit(solution)/shard_map/ppermute | solution.py:34
  98.1 14.0 %collective-permute-start.27 = (bf16[2048,128]{1,0:T(8,128)(2,1)S(1)}, bf16[2048,128]{1,0:T(8,128)(2,1)S(1)}, u32[]{:S(2)}, u32[]{:S(2)}) collective-permute-start(bf16[2048,128]{1,0:T(8,128)(2,1)S(1)} %get-tuple-element.115.refs_0_), channel_id=1, source_target_pairs={{0,64},{64,0},{1,65},{65,1},{2,66},{66,2},{3,67},{67,3},{4,68},{68... | collective-permute-start | bytes 1572872 | tf_op jit(solution)/shard_map/ppermute | solution.py:63
  101.4 4.9 %copy-start.5 = (f32[1,128,2048]{2,1,0:T(8,128)S(1)}, f32[1,128,2048]{2,1,0:T(8,128)}, u32[]{:S(2)}) copy-start(f32[1,128,2048]{2,1,0:T(8,128)} %refs_4_.5) | copy-start | bytes 3145732
  101.4 4.9 %copy-start.6 = (f32[128,2048]{1,0:T(8,128)S(1)}, f32[128,2048]{1,0:T(8,128)}, u32[]{:S(2)}) copy-start(f32[128,2048]{1,0:T(8,128)} %refs_2_.5) | copy-start | bytes 3145732
  101.5 4.9 %copy-start.10 = (bf16[1,128,2048]{2,1,0:T(8,128)(2,1)S(1)}, bf16[1,128,2048]{2,1,0:T(8,128)(2,1)}, u32[]{:S(2)}) copy-start(bf16[1,128,2048]{2,1,0:T(8,128)(2,1)} %refs_5_.5) | copy-start | bytes 1572868
  101.5 4.9 %copy-start.11 = (bf16[1,128,2048]{2,1,0:T(8,128)(2,1)S(1)}, bf16[1,128,2048]{2,1,0:T(8,128)(2,1)}, u32[]{:S(2)}) copy-start(bf16[1,128,2048]{2,1,0:T(8,128)(2,1)} %refs_6_.5) | copy-start | bytes 1572868
  103.8 19.5 %collective-permute-start.26 = (bf16[2048,128]{1,0:T(8,128)(2,1)S(1)}, bf16[2048,128]{1,0:T(8,128)(2,1)S(1)}, u32[]{:S(2)}, u32[]{:S(2)}) collective-permute-start(bf16[2048,128]{1,0:T(8,128)(2,1)S(1)} %get-tuple-element.114.refs_0_), channel_id=1, source_target_pairs={{0,64},{64,0},{1,65},{65,1},{2,66},{66,2},{3,67},{67,3},{4,68},{68... | collective-permute-start | bytes 1572872 | tf_op jit(solution)/shard_map/ppermute | solution.py:63
  106.4 5.7 %copy-start.3 = (f32[2,2048,128]{2,1,0:T(8,128)S(1)}, f32[2,2048,128]{2,1,0:T(8,128)}, u32[]{:S(2)}) copy-start(f32[2,2048,128]{2,1,0:T(8,128)} %refs_3_.4) | copy-start | bytes 6291460
  108.7 25.9 %collective-permute-start.31 = (bf16[128,2048]{1,0:T(8,128)(2,1)S(1)}, bf16[128,2048]{1,0:T(8,128)(2,1)S(1)}, u32[]{:S(2)}, u32[]{:S(2)}) collective-permute-start(bf16[128,2048]{1,0:T(8,128)(2,1)S(1)} %get-tuple-element.136.refs_0_), channel_id=1, source_target_pairs={{0,64},{64,0},{1,65},{65,1},{2,66},{66,2},{3,67},{67,3},{4,68},{68... | collective-permute-start | bytes 1572872 | tf_op jit(solution)/shard_map/ppermute | solution.py:63
  123.4 11.2 %copy-start.9 = (f32[128,2048]{1,0:T(8,128)S(1)}, f32[128,2048]{1,0:T(8,128)}, u32[]{:S(2)}) copy-start(f32[128,2048]{1,0:T(8,128)} %refs_3_.5) | copy-start | bytes 3145732

commit v4 on v3

--- a/solution.py
+++ b/solution.py
@@ -50,6 +50,11 @@
     return move(value, "core", lambda p: 1 - p)
 
 
+def both_cores(value):
+    pairs = [[i, i + 1] for i in range(0, FSDP, 2)]
+    return lax.all_gather(value, "fsdp", axis_index_groups=pairs)
+
+
 def far_x(value):
     return move(value, "x", lambda p: (p + 2) % 4)
 
@@ -91,6 +96,36 @@
         compiler_params=PARAMS,
         name="own_weights",
     )(params_in, params_down)
+
+
+def all_weights_kernel(*refs):
+    parts, (in_ref, down_ref) = refs[:8], refs[8:]
+    cores, mine, near, both = parts[:2], parts[2:4], parts[4:6], parts[6:]
+    half = mine[0].shape[1]
+    width = down_ref.shape[0]
+    for i in range(3):
+        pieces = [ref[i] for ref in mine] + [ref[i] for ref in cores]
+        pieces += [ref[i] for ref in (*near, *both)]
+        for k, piece in enumerate(pieces):
+            if i < 2:
+                in_ref[i * width + k * half : i * width + (k + 1) * half] = piece
+            else:
+                down_ref[k * half : (k + 1) * half] = piece
+
+
+def all_weights(cores, mine, near, both):
+    half, depth = mine[0].shape[1:]
+    return pl.pallas_call(
+        all_weights_kernel,
+        in_specs=[VMEM] * 8,
+        out_specs=[VMEM] * 2,
+        out_shape=[struct((16 * half, depth), BF16), struct((8 * half, depth), BF16)],
+        cost_estimate=pl.CostEstimate(
+            flops=0, bytes_accessed=8 * half * depth * 12, transcendentals=0
+        ),
+        compiler_params=PARAMS,
+        name="all_weights",
+    )(*cores, *mine, *near, *both)
 
 
 def forward_kernel(planes, in_ref, down_ref, *refs):
@@ -162,11 +197,7 @@
         functools.partial(gradient_kernel, len(left), start),
         in_specs=[VMEM] * (2 * len(left)),
         out_specs=[VMEM] * 3,
-        out_shape=[
-            struct((quarter, size), F32),
-            struct((quarter, size), F32),
-            struct((2, quarter, size), BF16),
-        ],
+        out_shape=[struct((quarter, size), F32)] * 2 + [struct((2, quarter, size), BF16)],
         scratch_shapes=[pltpu.VMEM((width, rows), BF16)],
         cost_estimate=pl.CostEstimate(
             flops=2 * rows * size * width,
@@ -208,7 +239,7 @@
     return (param_new, first_new.astype(BF16), second_new.astype(BF16))
 
 
-TILE = 512
+TILE = 1024
 
 
 def inner_kernel(which, start, *refs):
@@ -318,30 +349,28 @@
     low, high = up_y(own), down_y(own)
     by_x, by_z = far_x(own), swap_z(own)
     mine, *halves = own_weights(params_in, params_down)
-    core = swap_core(mine)
+    cores = [swap_core(w) for w in halves]
     by_xz = swap_z(after(by_x, by_z))
     far = up_y(low)
-    near = jnp.stack(near_x(after(halves, by_x)))
-    both = swap_core(near)
+    near = near_x(after(halves, by_x))
+    both = [swap_core(w) for w in near]
     low_x, high_x = far_x(after(low, near)), down_y(after(by_x, high))
     beside_z = swap_z(after(jnp.concatenate([low, high]), by_xz))
-    low_xz, high_xz = up_y(after(by_xz, far, core)), down_y(after(by_xz, high_x, core))
+    low_xz, high_xz = up_y(after(by_xz, far)), down_y(after(by_xz, high_x))
     far_of_x = far_x(after(far, low_x))
-    far_xz_x, far_xz_c = up_y(after(low_xz[:1], both)), down_y(after(high_xz[1:], both))
+    far_xz_x, far_xz_c = up_y(low_xz[:1]), down_y(high_xz[1:])
     far_z_x, far_z_c = up_y(beside_z[:1]), down_y(beside_z[3:])
 
-    parts = [half for quarter in (mine, core, near, both) for half in quarter]
-    weights_in = jnp.concatenate([w[k] for k in range(2) for w in parts])
-    weights_down = jnp.concatenate([w[2] for w in parts])
+    weights_in, weights_down = all_weights(cores, halves, near, both)
 
     def full(piece):
         return (piece, 0, piece, 1)
 
     groups = [
         [full(own), full(low), full(high), full(far)],
-        [full(by_x), full(low_x), full(high_x), full(far_of_x)],
+        [full(by_x), full(low_x), full(high_x), full(low_xz)],
         [full(by_z), full(by_xz), (beside_z, 0, beside_z, 1), (beside_z, 2, beside_z, 3)],
-        [full(low_xz), full(high_xz), (far_xz_x, 0, far_xz_c, 0), (far_z_x, 0, far_z_c, 0)],
+        [full(far_of_x), full(high_xz), (far_xz_x, 0, far_xz_c, 0), (far_z_x, 0, far_z_c, 0)],
     ]
     results = [forward(weights_in, weights_down, group) for group in groups]
     hidden, dgate, dup, rows, cots = [list(r) for r in zip(*results)]

time: 137 us -> 134 us (0.978)
  waiting for transfers between devices: 56 us -> 38 us
  starting transfers between devices: 46.1 us -> 61.9 us
    ppermute x29 -> x31, waiting for transfers between devices: 37 us -> 19.3 us  [move(): return lax.ppermute(value, 'fsdp', pairs)]
    ppermute x29 -> x31, starting transfers between devices: 37 us -> 51.4 us  [move(): return lax.ppermute(value, 'fsdp', pairs)]
    ppermute x3, starting transfers between devices: 9.09 us -> 10.5 us  [swap_replica(): return lax.ppermute(value, 'replica', [(0, 1), (1, 0)])]
    unnamed x40 -> x25, local copies, waits for them, and re-layouts: 4.24 us -> 3.82 us
  transfers between devices with their start and end apart: 32 -> 34, of which waited for: 15 -> 11; matrix products, arithmetic and copies ran while one was open for 1% -> 0% of each run, Pallas kernels for 16% -> 16%
where the time goes in v4:
time: 134 us; the launch traced here: 133 us
  starting transfers between devices  61.9 us (46%)
  waiting for transfers between devices  38 us (28%)
  Pallas kernels  26.9 us (20%)
  local copies, waits for them, and re-layouts  4.86 us (4%)
    ppermute x31, starting transfers between devices, move(): return lax.ppermute(value, 'fsdp', pairs)  51.4 us
    ppermute x31, waiting for transfers between devices, move(): return lax.ppermute(value, 'fsdp', pairs)  19.3 us
    ppermute x3, waiting for transfers between devices, swap_replica(): return lax.ppermute(value, 'replica', [(0, 1), (1, 0)])  18.7 us
    ppermute x3, starting transfers between devices, swap_replica(): return lax.ppermute(value, 'replica', [(0, 1), (1, 0)])  10.5 us
    pallas_call x4, Pallas kernels, forward(): pl.pallas_call(functools.partial(forward_kernel, [(p[1], p[3]) for p in p...  7.65 us
    pallas_call x3, Pallas kernels, gradient(): pl.pallas_call(functools.partial(gradient_kernel, len(left), start), in_s...  7 us
    pallas_call x3, Pallas kernels, inner_step(): pl.pallas_call(functools.partial(inner_kernel, which, start), grid=(size...  5.77 us
    pallas_call x3, Pallas kernels, outer_step(): pl.pallas_call(functools.partial(outer_kernel, which, start), grid=(size...  4.28 us
  transfers between devices with their start and end apart: 34, of which 11 were waited for; matrix products, arithmetic and copies ran while one was open for 0% of the time, Pallas kernels for 16%

profile of v4, /device:TPU:1, one launch (start us, length us, event | category | flops | bytes accessed | tf_op | source)
XLA Modules:
  0.0 132.7 jit_solution(10280021354904054055)
XLA Ops:
  0.6 1.0 constant_dynamic-update-slice_fusion.1
  1.6 1.0 constant_dynamic-update-slice_fusion.refs_0_.refs_1_
  2.6 3.7 %collective-permute-start.2 = (bf16[2,64,2048]{2,1,0:T(8,128)(2,1)S(1)}, bf16[2,64,2048]{2,1,0:T(8,128)(2,1)S(1)}, u32[]{:S(2)}, u32[]{:S(2)}) collective-permute-start(bf16[2,64,2048]{2,1,0:T(8,128)(2,1)S(1)} %constant_dynamic-update-slice_fusion.refs_0_.refs_1_), channel_id=1, source_target_pairs={{0,32},{1,33},{2,34},{3,35},{4,36},{5,37},{6,38},{7,39},{8,40},{9,... | collective-permute-start | bytes 1572872 | tf_op jit(solution)/shard_map/ppermute | solution.py:34
  6.2 1.6 %collective-permute-start.12 = (bf16[2,64,2048]{2,1,0:T(8,128)(2,1)S(1)}, bf16[2,64,2048]{2,1,0:T(8,128)(2,1)S(1)}, u32[]{:S(2)}, u32[]{:S(2)}) collective-permute-start(bf16[2,64,2048]{2,1,0:T(8,128)(2,1)S(1)} %constant_dynamic-update-slice_fusion.refs_0_.refs_1_), channel_id=1, source_target_pairs={{0,8},{1,9},{2,10},{3,11},{4,12},{5,13},{6,14},{7,15},{8,0},{9,1},... | collective-permute-start | bytes 1572872 | tf_op jit(solution)/shard_map/ppermute | solution.py:34
  7.9 2.7 %collective-permute-start.8 = (bf16[2,64,2048]{2,1,0:T(8,128)(2,1)S(1)}, bf16[2,64,2048]{2,1,0:T(8,128)(2,1)S(1)}, u32[]{:S(2)}, u32[]{:S(2)}) collective-permute-start(bf16[2,64,2048]{2,1,0:T(8,128)(2,1)S(1)} %constant_dynamic-update-slice_fusion.refs_0_.refs_1_), channel_id=1, source_target_pairs={{0,6},{1,7},{2,0},{3,1},{4,2},{5,3},{6,4},{7,5},{8,14},{9,15},{10,... | collective-permute-start | bytes 1572872 | tf_op jit(solution)/shard_map/ppermute | solution.py:34
  10.6 1.6 %copy-done.1 = f32[1,2,2048,128]{3,2,1,0:T(8,128)S(1)} copy-done((f32[1,2,2048,128]{3,2,1,0:T(8,128)S(1)}, f32[1,2,2048,128]{3,2,1,0:T(8,128)}, u32[]{:S(2)}) %copy-start.1) | copy-done | bytes 2097176
  12.2 1.2 copy-done.4
  13.4 1.6 %own_weights.1 = (bf16[2,3,64,2048]{3,2,1,0:T(8,128)(2,1)}, bf16[3,64,2048]{2,1,0:T(8,128)(2,1)S(1)}, bf16[3,64,2048]{2,1,0:T(8,128)(2,1)S(1)}) custom-call(f32[1,2,2048,128]{3,2,1,0:T(8,128)S(1)} %copy-done.1, f32[1,128,2048]{2,1,0:T(8,128)S(1)} %copy-done.4), custom_call_target="tpu_custom_call" | custom-call | flops 786432 | bytes 4718592 | tf_op jit(solution)/shard_map/own_weights/pallas_call | solution.py:88
  15.0 2.4 %collective-permute-done.2.refs_0_.refs_1_ = bf16[2,64,2048]{2,1,0:T(8,128)(2,1)S(1)} collective-permute-done((bf16[2,64,2048]{2,1,0:T(8,128)(2,1)S(1)}, bf16[2,64,2048]{2,1,0:T(8,128)(2,1)S(1)}, u32[]{:S(2)}, u32[]{:S(2)}) %collective-permute-start.2) | collective-permute-done | bytes 524320 | tf_op jit(solution)/shard_map/ppermute | solution.py:34
  17.4 1.6 %collective-permute-start.3 = (bf16[3,64,2048]{2,1,0:T(8,128)(2,1)S(1)}, bf16[3,64,2048]{2,1,0:T(8,128)(2,1)S(1)}, u32[]{:S(2)}, u32[]{:S(2)}) collective-permute-start(bf16[3,64,2048]{2,1,0:T(8,128)(2,1)S(1)} %get-tuple-element.77.refs_2_), channel_id=1, source_target_pairs={{0,16},{1,17},{2,18},{3,19},{4,20},{5,21},{6,22},{7,23},{8,24},{9,... | collective-permute-start | bytes 2359304 | tf_op jit(solution)/shard_map/ppermute | solution.py:34
  19.0 1.8 %collective-permute-start.4 = (bf16[3,64,2048]{2,1,0:T(8,128)(2,1)S(1)}, bf16[3,64,2048]{2,1,0:T(8,128)(2,1)S(1)}, u32[]{:S(2)}, u32[]{:S(2)}) collective-permute-start(bf16[3,64,2048]{2,1,0:T(8,128)(2,1)S(1)} %get-tuple-element.78.refs_3_), channel_id=1, source_target_pairs={{0,48},{1,49},{2,50},{3,51},{4,52},{5,53},{6,54},{7,55},{8,56},{9,... | collective-permute-start | bytes 2359304 | tf_op jit(solution)/shard_map/ppermute | solution.py:34
  20.8 1.6 %collective-permute-start.13 = (bf16[2,64,2048]{2,1,0:T(8,128)(2,1)S(1)}, bf16[2,64,2048]{2,1,0:T(8,128)(2,1)S(1)}, u32[]{:S(2)}, u32[]{:S(2)}) collective-permute-start(bf16[2,64,2048]{2,1,0:T(8,128)(2,1)S(1)} %collective-permute-done.2.refs_0_.refs_1_), channel_id=1, source_target_pairs={{0,8},{1,9},{2,10},{3,11},{4,12},{5,13},{6,14},{7,15},{8,0},{9,1},... | collective-permute-start | bytes 1572872 | tf_op jit(solution)/shard_map/ppermute | solution.py:34
  22.5 2.7 %collective-permute-start.11 = (bf16[2,64,2048]{2,1,0:T(8,128)(2,1)S(1)}, bf16[2,64,2048]{2,1,0:T(8,128)(2,1)S(1)}, u32[]{:S(2)}, u32[]{:S(2)}) collective-permute-start(bf16[2,64,2048]{2,1,0:T(8,128)(2,1)S(1)} %collective-permute-done.2.refs_0_.refs_1_), channel_id=1, source_target_pairs={{0,6},{1,7},{2,0},{3,1},{4,2},{5,3},{6,4},{7,5},{8,14},{9,15},{10,... | collective-permute-start | bytes 1572872 | tf_op jit(solution)/shard_map/ppermute | solution.py:34
  25.3 7.2 %collective-permute-done.13.refs_2_.refs_3_ = bf16[2,64,2048]{2,1,0:T(8,128)(2,1)S(1)} collective-permute-done((bf16[2,64,2048]{2,1,0:T(8,128)(2,1)S(1)}, bf16[2,64,2048]{2,1,0:T(8,128)(2,1)S(1)}, u32[]{:S(2)}, u32[]{:S(2)}) %collective-permute-start.13) | collective-permute-done | bytes 524320 | tf_op jit(solution)/shard_map/ppermute | solution.py:34
  32.5 1.3 collective-permute-start.15
  34.0 3.4 %collective-permute-start.17 = (bf16[2,64,2048]{2,1,0:T(8,128)(2,1)S(1)}, bf16[2,64,2048]{2,1,0:T(8,128)(2,1)S(1)}, u32[]{:S(2)}, u32[]{:S(2)}) collective-permute-start(bf16[2,64,2048]{2,1,0:T(8,128)(2,1)S(1)} %collective-permute-done.13.refs_2_.refs_3_), channel_id=1, source_target_pairs={{0,6},{1,7},{2,0},{3,1},{4,2},{5,3},{6,4},{7,5},{8,14},{9,15},{10,... | collective-permute-start | bytes 1572872 | tf_op jit(solution)/shard_map/ppermute | solution.py:34
  37.5 1.2 collective-permute-start.10
  38.7 3.4 %collective-permute-start = (bf16[3,64,2048]{2,1,0:T(8,128)(2,1)S(1)}, bf16[3,64,2048]{2,1,0:T(8,128)(2,1)S(1)}, u32[]{:S(2)}, u32[]{:S(2)}) collective-permute-start(bf16[3,64,2048]{2,1,0:T(8,128)(2,1)S(1)} %get-tuple-element.77.refs_2_), channel_id=1, source_target_pairs={{0,1},{1,0},{2,3},{3,2},{4,5},{5,4},{6,7},{7,6},{8,9},{9,8},{10,11... | collective-permute-start | bytes 2359304 | tf_op jit(solution)/shard_map/ppermute | solution.py:34
  42.0 3.3 %collective-permute-done.17.refs_2_.refs_3_ = bf16[2,64,2048]{2,1,0:T(8,128)(2,1)S(1)} collective-permute-done((bf16[2,64,2048]{2,1,0:T(8,128)(2,1)S(1)}, bf16[2,64,2048]{2,1,0:T(8,128)(2,1)S(1)}, u32[]{:S(2)}, u32[]{:S(2)}) %collective-permute-start.17) | collective-permute-done | bytes 524320 | tf_op jit(solution)/shard_map/ppermute | solution.py:34
  45.3 4.2 %collective-permute-start.1 = (bf16[3,64,2048]{2,1,0:T(8,128)(2,1)S(1)}, bf16[3,64,2048]{2,1,0:T(8,128)(2,1)S(1)}, u32[]{:S(2)}, u32[]{:S(2)}) collective-permute-start(bf16[3,64,2048]{2,1,0:T(8,128)(2,1)S(1)} %get-tuple-element.78.refs_3_), channel_id=1, source_target_pairs={{0,1},{1,0},{2,3},{3,2},{4,5},{5,4},{6,7},{7,6},{8,9},{9,8},{10,11... | collective-permute-start | bytes 2359304 | tf_op jit(solution)/shard_map/ppermute | solution.py:34
  49.6 3.4 %collective-permute-start.5 = (bf16[3,64,2048]{2,1,0:T(8,128)(2,1)S(1)}, bf16[3,64,2048]{2,1,0:T(8,128)(2,1)S(1)}, u32[]{:S(2)}, u32[]{:S(2)}) collective-permute-start(bf16[3,64,2048]{2,1,0:T(8,128)(2,1)S(1)} %collective-permute-done.3.refs_4_), channel_id=1, source_target_pairs={{0,1},{1,0},{2,3},{3,2},{4,5},{5,4},{6,7},{7,6},{8,9},{9,8},{10,11... | collective-permute-start | bytes 2359304 | tf_op jit(solution)/shard_map/ppermute | solution.py:34
  54.3 1.2 collective-permute-start.16
  55.5 2.8 %collective-permute-start.19 = (bf16[1,64,2048]{2,1,0:T(8,128)(2,1)S(1)}, bf16[1,64,2048]{2,1,0:T(8,128)(2,1)S(1)}, u32[]{:S(2)}, u32[]{:S(2)}) collective-permute-start(bf16[1,64,2048]{2,1,0:T(8,128)(2,1)S(1)} %slice.17), channel_id=1, source_target_pairs={{0,6},{1,7},{2,0},{3,1},{4,2},{5,3},{6,4},{7,5},{8,14},{9,15},{10,... | collective-permute-start | bytes 786440 | tf_op jit(solution)/shard_map/ppermute | solution.py:34
  58.4 2.8 %collective-permute-start.21 = (bf16[1,64,2048]{2,1,0:T(8,128)(2,1)S(1)}, bf16[1,64,2048]{2,1,0:T(8,128)(2,1)S(1)}, u32[]{:S(2)}, u32[]{:S(2)}) collective-permute-start(bf16[1,64,2048]{2,1,0:T(8,128)(2,1)S(1)} %get-tuple-element.142), channel_id=1, source_target_pairs={{0,6},{1,7},{2,0},{3,1},{4,2},{5,3},{6,4},{7,5},{8,14},{9,15},{10,... | collective-permute-start | bytes 786440 | tf_op jit(solution)/shard_map/ppermute | solution.py:34
  61.7 1.9 %forward.6 = (bf16[512,256]{1,0:T(8,128)(2,1)S(1)}, bf16[512,256]{1,0:T(8,128)(2,1)S(1)}, bf16[512,256]{1,0:T(8,128)(2,1)S(1)}, bf16[256,2048]{1,0:T(8,128)(2,1)S(1)}, bf16[256,2048]{1,0:T(8,128)(2,1)S(1)}) custom-call(bf16[1024,2048]{1,0:T(8,128)(2,1)S(1)} %get-tuple-element.79.in_ref, bf16[512,2048]{1,0:T(8,128)(2,1)S(1)} %get-tuple-element.80.down_ref, ...), custom_call_target="tpu_custom_call" | custom-call | flops 1610612736 | bytes 10485760 | tf_op jit(solution)/shard_map/forward/pallas_call | solution.py:157
  63.6 1.9 %forward.5 = (bf16[512,256]{1,0:T(8,128)(2,1)S(1)}, bf16[512,256]{1,0:T(8,128)(2,1)S(1)}, bf16[512,256]{1,0:T(8,128)(2,1)S(1)}, bf16[256,2048]{1,0:T(8,128)(2,1)S(1)}, bf16[256,2048]{1,0:T(8,128)(2,1)S(1)}) custom-call(bf16[1024,2048]{1,0:T(8,128)(2,1)S(1)} %get-tuple-element.79.in_ref, bf16[512,2048]{1,0:T(8,128)(2,1)S(1)} %get-tuple-element.80.down_ref, ...), custom_call_target="tpu_custom_call" | custom-call | flops 1610612736 | bytes 10485760 | tf_op jit(solution)/shard_map/forward/pallas_call | solution.py:157
  65.5 1.9 %forward.4 = (bf16[512,256]{1,0:T(8,128)(2,1)S(1)}, bf16[512,256]{1,0:T(8,128)(2,1)S(1)}, bf16[512,256]{1,0:T(8,128)(2,1)S(1)}, bf16[256,2048]{1,0:T(8,128)(2,1)S(1)}, bf16[256,2048]{1,0:T(8,128)(2,1)S(1)}) custom-call(bf16[1024,2048]{1,0:T(8,128)(2,1)S(1)} %get-tuple-element.79.in_ref, bf16[512,2048]{1,0:T(8,128)(2,1)S(1)} %get-tuple-element.80.down_ref, ...), custom_call_target="tpu_custom_call" | custom-call | flops 1610612736 | bytes 10485760 | tf_op jit(solution)/shard_map/forward/pallas_call | solution.py:157
  67.5 1.4 %collective-permute-done.20.refs_6_ = bf16[1,64,2048]{2,1,0:T(8,128)(2,1)S(1)} collective-permute-done((bf16[1,64,2048]{2,1,0:T(8,128)(2,1)S(1)}, bf16[1,64,2048]{2,1,0:T(8,128)(2,1)S(1)}, u32[]{:S(2)}, u32[]{:S(2)}) %collective-permute-start.20) | collective-permute-done | bytes 262176 | tf_op jit(solution)/shard_map/ppermute | solution.py:34
  68.9 1.9 %forward.7 = (bf16[512,256]{1,0:T(8,128)(2,1)S(1)}, bf16[512,256]{1,0:T(8,128)(2,1)S(1)}, bf16[512,256]{1,0:T(8,128)(2,1)S(1)}, bf16[256,2048]{1,0:T(8,128)(2,1)S(1)}, bf16[256,2048]{1,0:T(8,128)(2,1)S(1)}) custom-call(bf16[1024,2048]{1,0:T(8,128)(2,1)S(1)} %get-tuple-element.79.in_ref, bf16[512,2048]{1,0:T(8,128)(2,1)S(1)} %get-tuple-element.80.down_ref, ...), custom_call_target="tpu_custom_call" | custom-call | flops 1610612736 | bytes 10485760 | tf_op jit(solution)/shard_map/forward/pallas_call | solution.py:157
  70.8 2.3 %gradient.4 = (f32[128,2048]{1,0:T(8,128)S(1)}, f32[128,2048]{1,0:T(8,128)S(1)}, bf16[2,128,2048]{2,1,0:T(8,128)(2,1)S(1)}) custom-call(bf16[512,256]{1,0:T(8,128)(2,1)S(1)} %get-tuple-element.101.refs_0_, bf16[512,256]{1,0:T(8,128)(2,1)S(1)} %get-tuple-element.102.refs_1_, bf16[512,256]{1,0:T(8,128)(2,1)S(1)} %get-tuple-element.103.refs_2_, ...), custom_call_target="tpu_custom_call" | custom-call | flops 2147483648 | bytes 8388608 | tf_op jit(solution)/shard_map/gradient/pallas_call | solution.py:196
  73.2 5.1 %collective-permute-start.25 = (bf16[2,128,2048]{2,1,0:T(8,128)(2,1)S(1)}, bf16[2,128,2048]{2,1,0:T(8,128)(2,1)S(1)}, u32[]{:S(2)}, u32[]{:S(2)}) collective-permute-start(bf16[2,128,2048]{2,1,0:T(8,128)(2,1)S(1)} %get-tuple-element.106), channel_id=1, source_target_pairs={{0,1},{1,0},{2,3},{3,2},{4,5},{5,4},{6,7},{7,6},{8,9},{9,8},{10,11... | collective-permute-start | bytes 3145736 | tf_op jit(solution)/shard_map/ppermute | solution.py:34
  78.2 2.3 %gradient.3 = (f32[128,2048]{1,0:T(8,128)S(1)}, f32[128,2048]{1,0:T(8,128)S(1)}, bf16[2,128,2048]{2,1,0:T(8,128)(2,1)S(1)}) custom-call(bf16[512,256]{1,0:T(8,128)(2,1)S(1)} %get-tuple-element.81.refs_0_, bf16[512,256]{1,0:T(8,128)(2,1)S(1)} %get-tuple-element.86.refs_1_, bf16[512,256]{1,0:T(8,128)(2,1)S(1)} %get-tuple-element.88.refs_2_, ...), custom_call_target="tpu_custom_call" | custom-call | flops 2147483648 | bytes 8388608 | tf_op jit(solution)/shard_map/gradient/pallas_call | solution.py:196
  80.7 2.3 %gradient.5 = (f32[128,2048]{1,0:T(8,128)S(1)}, f32[128,2048]{1,0:T(8,128)S(1)}, bf16[2,128,2048]{2,1,0:T(8,128)(2,1)S(1)}) custom-call(bf16[512,256]{1,0:T(8,128)(2,1)S(1)} %get-tuple-element.121.refs_0_, bf16[512,256]{1,0:T(8,128)(2,1)S(1)} %get-tuple-element.122.refs_1_, bf16[512,256]{1,0:T(8,128)(2,1)S(1)} %get-tuple-element.123.refs_2_, ...), custom_call_target="tpu_custom_call" | custom-call | flops 2147483648 | bytes 8388608 | tf_op jit(solution)/shard_map/gradient/pallas_call | solution.py:196
  84.1 1.7 %collective-permute-start.27 = (bf16[64,2048]{1,0:T(8,128)(2,1)S(1)}, bf16[64,2048]{1,0:T(8,128)(2,1)S(1)}, u32[]{:S(2)}, u32[]{:S(2)}) collective-permute-start(bf16[64,2048]{1,0:T(8,128)(2,1)S(1)} %get-tuple-element.109), channel_id=1, source_target_pairs={{0,48},{1,49},{2,50},{3,51},{4,52},{5,53},{6,54},{7,55},{8,56},{9,... | collective-permute-start | bytes 786440 | tf_op jit(solution)/shard_map/ppermute | solution.py:34
  86.3 1.2 collective-permute-start.24
  88.0 3.7 %collective-permute-done.26.refs_2_ = bf16[64,2048]{1,0:T(8,128)(2,1)S(1)} collective-permute-done((bf16[64,2048]{1,0:T(8,128)(2,1)S(1)}, bf16[64,2048]{1,0:T(8,128)(2,1)S(1)}, u32[]{:S(2)}, u32[]{:S(2)}) %collective-permute-start.26) | collective-permute-done | bytes 262176 | tf_op jit(solution)/shard_map/ppermute | solution.py:34
  91.6 1.5 %collective-permute-start.32 = (bf16[64,2048]{1,0:T(8,128)(2,1)S(1)}, bf16[64,2048]{1,0:T(8,128)(2,1)S(1)}, u32[]{:S(2)}, u32[]{:S(2)}) collective-permute-start(bf16[64,2048]{1,0:T(8,128)(2,1)S(1)} %get-tuple-element.133), channel_id=1, source_target_pairs={{0,48},{1,49},{2,50},{3,51},{4,52},{5,53},{6,54},{7,55},{8,56},{9,... | collective-permute-start | bytes 786440 | tf_op jit(solution)/shard_map/ppermute | solution.py:34
  93.2 1.9 %inner_step.3 = (bf16[1,2,2048,128]{3,2,1,0:T(8,128)(2,1)}, bf16[1,2,2048,128]{3,2,1,0:T(8,128)(2,1)}, bf16[2048,128]{1,0:T(8,128)(2,1)S(1)}) custom-call(f32[128,2048]{1,0:T(8,128)S(1)} %get-tuple-element.105.refs_0_, bf16[2,128,2048]{2,1,0:T(8,128)(2,1)S(1)} %collective-permute-done.25.core_ref.refs_1_, ...), custom_call_target="tpu_custom_call" | custom-call | flops 5242880 | bytes 6815744 | tf_op jit(solution)/shard_map/inner_step/pallas_call | solution.py:276
  95.1 3.3 %collective-permute-start.29 = (bf16[2048,128]{1,0:T(8,128)(2,1)S(1)}, bf16[2048,128]{1,0:T(8,128)(2,1)S(1)}, u32[]{:S(2)}, u32[]{:S(2)}) collective-permute-start(bf16[2048,128]{1,0:T(8,128)(2,1)S(1)} %get-tuple-element.113.refs_0_), channel_id=1, source_target_pairs={{0,64},{64,0},{1,65},{65,1},{2,66},{66,2},{3,67},{67,3},{4,68},{68... | collective-permute-start | bytes 1572872 | tf_op jit(solution)/shard_map/ppermute | solution.py:68
  98.5 1.9 %inner_step.4 = (bf16[1,2,2048,128]{3,2,1,0:T(8,128)(2,1)}, bf16[1,2,2048,128]{3,2,1,0:T(8,128)(2,1)}, bf16[2048,128]{1,0:T(8,128)(2,1)S(1)}) custom-call(f32[128,2048]{1,0:T(8,128)S(1)} %get-tuple-element.96.refs_0_, bf16[2,128,2048]{2,1,0:T(8,128)(2,1)S(1)} %collective-permute-done.22.core_ref.refs_1_, ...), custom_call_target="tpu_custom_call", output_to_operand_aliasing={{0}: (8, {}), {1}: (9, {})} | custom-call | flops 5242880 | bytes 6815744 | tf_op jit(solution)/shard_map/inner_step/pallas_call | solution.py:276
  100.4 3.6 %collective-permute-start.28 = (bf16[2048,128]{1,0:T(8,128)(2,1)S(1)}, bf16[2048,128]{1,0:T(8,128)(2,1)S(1)}, u32[]{:S(2)}, u32[]{:S(2)}) collective-permute-start(bf16[2048,128]{1,0:T(8,128)(2,1)S(1)} %get-tuple-element.112.refs_0_), channel_id=1, source_target_pairs={{0,64},{64,0},{1,65},{65,1},{2,66},{66,2},{3,67},{67,3},{4,68},{68... | collective-permute-start | bytes 1572872 | tf_op jit(solution)/shard_map/ppermute | solution.py:68
  104.1 1.9 %inner_step.5 = (bf16[1,128,2048]{2,1,0:T(8,128)(2,1)}, bf16[1,128,2048]{2,1,0:T(8,128)(2,1)}, bf16[128,2048]{1,0:T(8,128)(2,1)S(1)}) custom-call(f32[128,2048]{1,0:T(8,128)S(1)} %get-tuple-element.129.refs_0_, bf16[2,128,2048]{2,1,0:T(8,128)(2,1)S(1)} %collective-permute-done.30.core_ref.refs_1_, bf16[64,2048]{1,0:T(8,128)(2,1)S(1)} %collective-permute-done.31.refs_2_, ...), custom_call_target="tpu_custom_call" | custom-call | flops 5242880 | bytes 6815744 | tf_op jit(solution)/shard_map/inner_step/pallas_call | solution.py:276
  106.0 3.6 %collective-permute-start.33 = (bf16[128,2048]{1,0:T(8,128)(2,1)S(1)}, bf16[128,2048]{1,0:T(8,128)(2,1)S(1)}, u32[]{:S(2)}, u32[]{:S(2)}) collective-permute-start(bf16[128,2048]{1,0:T(8,128)(2,1)S(1)} %get-tuple-element.134.refs_0_), channel_id=1, source_target_pairs={{0,64},{64,0},{1,65},{65,1},{2,66},{66,2},{3,67},{67,3},{4,68},{68... | collective-permute-start | bytes 1572872 | tf_op jit(solution)/shard_map/ppermute | solution.py:68
  109.6 1.4 %outer_step.3 = (f32[2,2048,128]{2,1,0:T(8,128)}, f32[2,2048,128]{2,1,0:T(8,128)}) custom-call(bf16[2048,128]{1,0:T(8,128)(2,1)S(1)} %get-tuple-element.113.refs_0_, bf16[2048,128]{1,0:T(8,128)(2,1)S(1)} %collective-permute-done.29.refs_1_, f32[2,2048,128]{2,1,0:T(8,128)S(1)} %copy-done, f32[2,2048,128]{2,1,0:T(8,128)S(1)} %copy-done.3), custom_call_target="tpu_custom_call" | custom-call | flops 2097152 | bytes 5242880 | tf_op jit(solution)/shard_map/outer_step/pallas_call | solution.py:315
  111.1 8.9 %collective-permute-done.28.refs_1_ = bf16[2048,128]{1,0:T(8,128)(2,1)S(1)} collective-permute-done((bf16[2048,128]{1,0:T(8,128)(2,1)S(1)}, bf16[2048,128]{1,0:T(8,128)(2,1)S(1)}, u32[]{:S(2)}, u32[]{:S(2)}) %collective-permute-start.28) | collective-permute-done | bytes 524320 | tf_op jit(solution)/shard_map/ppermute | solution.py:68
  120.0 1.4 %outer_step.4 = (f32[2,2048,128]{2,1,0:T(8,128)}, f32[2,2048,128]{2,1,0:T(8,128)}) custom-call(bf16[2048,128]{1,0:T(8,128)(2,1)S(1)} %get-tuple-element.112.refs_0_, bf16[2048,128]{1,0:T(8,128)(2,1)S(1)} %collective-permute-done.28.refs_1_, f32[2,2048,128]{2,1,0:T(8,128)S(1)} %copy-done, ...), custom_call_target="tpu_custom_call", output_to_operand_aliasing={{0}: (4, {}), {1}: (5, {})} | custom-call | flops 2097152 | bytes 5242880 | tf_op jit(solution)/shard_map/outer_step/pallas_call | solution.py:315
  121.4 9.8 %collective-permute-done.33.refs_1_ = bf16[128,2048]{1,0:T(8,128)(2,1)S(1)} collective-permute-done((bf16[128,2048]{1,0:T(8,128)(2,1)S(1)}, bf16[128,2048]{1,0:T(8,128)(2,1)S(1)}, u32[]{:S(2)}, u32[]{:S(2)}) %collective-permute-start.33) | collective-permute-done | bytes 524320 | tf_op jit(solution)/shard_map/ppermute | solution.py:68
  131.2 1.4 %outer_step.5 = (f32[128,2048]{1,0:T(8,128)}, f32[128,2048]{1,0:T(8,128)}) custom-call(bf16[128,2048]{1,0:T(8,128)(2,1)S(1)} %get-tuple-element.134.refs_0_, bf16[128,2048]{1,0:T(8,128)(2,1)S(1)} %collective-permute-done.33.refs_1_, f32[128,2048]{1,0:T(8,128)S(1)} %copy-done.6, f32[128,2048]{1,0:T(8,128)S(1)} %copy-done.9), custom_call_target="tpu_custom_call" | custom-call | flops 2097152 | bytes 5242880 | tf_op jit(solution)/shard_map/outer_step/pallas_call | solution.py:315
  (68 shorter events, 4.5 us)
Async XLA Ops:
  2.6 14.8 %collective-permute-start.2 = (bf16[2,64,2048]{2,1,0:T(8,128)(2,1)S(1)}, bf16[2,64,2048]{2,1,0:T(8,128)(2,1)S(1)}, u32[]{:S(2)}, u32[]{:S(2)}) collective-permute-start(bf16[2,64,2048]{2,1,0:T(8,128)(2,1)S(1)} %constant_dynamic-update-slice_fusion.refs_0_.refs_1_), channel_id=1, source_target_pairs={{0,32},{1,33},{2,34},{3,35},{4,36},{5,37},{6,38},{7,39},{8,40},{9,... | collective-permute-start | bytes 1572872 | tf_op jit(solution)/shard_map/ppermute | solution.py:34
  6.2 14.6 %collective-permute-start.12 = (bf16[2,64,2048]{2,1,0:T(8,128)(2,1)S(1)}, bf16[2,64,2048]{2,1,0:T(8,128)(2,1)S(1)}, u32[]{:S(2)}, u32[]{:S(2)}) collective-permute-start(bf16[2,64,2048]{2,1,0:T(8,128)(2,1)S(1)} %constant_dynamic-update-slice_fusion.refs_0_.refs_1_), channel_id=1, source_target_pairs={{0,8},{1,9},{2,10},{3,11},{4,12},{5,13},{6,14},{7,15},{8,0},{9,1},... | collective-permute-start | bytes 1572872 | tf_op jit(solution)/shard_map/ppermute | solution.py:34
  7.9 14.6 %collective-permute-start.8 = (bf16[2,64,2048]{2,1,0:T(8,128)(2,1)S(1)}, bf16[2,64,2048]{2,1,0:T(8,128)(2,1)S(1)}, u32[]{:S(2)}, u32[]{:S(2)}) collective-permute-start(bf16[2,64,2048]{2,1,0:T(8,128)(2,1)S(1)} %constant_dynamic-update-slice_fusion.refs_0_.refs_1_), channel_id=1, source_target_pairs={{0,6},{1,7},{2,0},{3,1},{4,2},{5,3},{6,4},{7,5},{8,14},{9,15},{10,... | collective-permute-start | bytes 1572872 | tf_op jit(solution)/shard_map/ppermute | solution.py:34
  10.6 14.6 %collective-permute-start.7 = (bf16[2,64,2048]{2,1,0:T(8,128)(2,1)S(1)}, bf16[2,64,2048]{2,1,0:T(8,128)(2,1)S(1)}, u32[]{:S(2)}, u32[]{:S(2)}) collective-permute-start(bf16[2,64,2048]{2,1,0:T(8,128)(2,1)S(1)} %constant_dynamic-update-slice_fusion.refs_0_.refs_1_), channel_id=1, source_target_pairs={{0,2},{1,3},{2,4},{3,5},{4,6},{5,7},{6,0},{7,1},{8,10},{9,11},{10,... | collective-permute-start | bytes 1572872 | tf_op jit(solution)/shard_map/ppermute | solution.py:34
  10.6 1.6 %copy-start.1 = (f32[1,2,2048,128]{3,2,1,0:T(8,128)S(1)}, f32[1,2,2048,128]{3,2,1,0:T(8,128)}, u32[]{:S(2)}) copy-start(f32[1,2,2048,128]{3,2,1,0:T(8,128)} %refs_4_.4) | copy-start | bytes 6291460
  12.2 1.2 copy-start.4
  17.4 20.0 %collective-permute-start.3 = (bf16[3,64,2048]{2,1,0:T(8,128)(2,1)S(1)}, bf16[3,64,2048]{2,1,0:T(8,128)(2,1)S(1)}, u32[]{:S(2)}, u32[]{:S(2)}) collective-permute-start(bf16[3,64,2048]{2,1,0:T(8,128)(2,1)S(1)} %get-tuple-element.77.refs_2_), channel_id=1, source_target_pairs={{0,16},{1,17},{2,18},{3,19},{4,20},{5,21},{6,22},{7,23},{8,24},{9,... | collective-permute-start | bytes 2359304 | tf_op jit(solution)/shard_map/ppermute | solution.py:34
  19.0 18.5 %collective-permute-start.4 = (bf16[3,64,2048]{2,1,0:T(8,128)(2,1)S(1)}, bf16[3,64,2048]{2,1,0:T(8,128)(2,1)S(1)}, u32[]{:S(2)}, u32[]{:S(2)}) collective-permute-start(bf16[3,64,2048]{2,1,0:T(8,128)(2,1)S(1)} %get-tuple-element.78.refs_3_), channel_id=1, source_target_pairs={{0,48},{1,49},{2,50},{3,51},{4,52},{5,53},{6,54},{7,55},{8,56},{9,... | collective-permute-start | bytes 2359304 | tf_op jit(solution)/shard_map/ppermute | solution.py:34
  20.8 11.7 %collective-permute-start.13 = (bf16[2,64,2048]{2,1,0:T(8,128)(2,1)S(1)}, bf16[2,64,2048]{2,1,0:T(8,128)(2,1)S(1)}, u32[]{:S(2)}, u32[]{:S(2)}) collective-permute-start(bf16[2,64,2048]{2,1,0:T(8,128)(2,1)S(1)} %collective-permute-done.2.refs_0_.refs_1_), channel_id=1, source_target_pairs={{0,8},{1,9},{2,10},{3,11},{4,12},{5,13},{6,14},{7,15},{8,0},{9,1},... | collective-permute-start | bytes 1572872 | tf_op jit(solution)/shard_map/ppermute | solution.py:34
  22.5 11.6 %collective-permute-start.11 = (bf16[2,64,2048]{2,1,0:T(8,128)(2,1)S(1)}, bf16[2,64,2048]{2,1,0:T(8,128)(2,1)S(1)}, u32[]{:S(2)}, u32[]{:S(2)}) collective-permute-start(bf16[2,64,2048]{2,1,0:T(8,128)(2,1)S(1)} %collective-permute-done.2.refs_0_.refs_1_), channel_id=1, source_target_pairs={{0,6},{1,7},{2,0},{3,1},{4,2},{5,3},{6,4},{7,5},{8,14},{9,15},{10,... | collective-permute-start | bytes 1572872 | tf_op jit(solution)/shard_map/ppermute | solution.py:34
  25.2 12.2 %collective-permute-start.9 = (bf16[2,64,2048]{2,1,0:T(8,128)(2,1)S(1)}, bf16[2,64,2048]{2,1,0:T(8,128)(2,1)S(1)}, u32[]{:S(2)}, u32[]{:S(2)}) collective-permute-start(bf16[2,64,2048]{2,1,0:T(8,128)(2,1)S(1)} %collective-permute-done.7.refs_2_.refs_3_), channel_id=1, source_target_pairs={{0,2},{1,3},{2,4},{3,5},{4,6},{5,7},{6,0},{7,1},{8,10},{9,11},{10,... | collective-permute-start | bytes 1572872 | tf_op jit(solution)/shard_map/ppermute | solution.py:34
  32.5 21.8 %collective-permute-start.15 = (bf16[4,64,2048]{2,1,0:T(8,128)(2,1)S(1)}, bf16[4,64,2048]{2,1,0:T(8,128)(2,1)S(1)}, u32[]{:S(2)}, u32[]{:S(2)}) collective-permute-start(bf16[4,64,2048]{2,1,0:T(8,128)(2,1)S(1)} %pad_maximum_fusion), channel_id=1, source_target_pairs={{0,8},{1,9},{2,10},{3,11},{4,12},{5,13},{6,14},{7,15},{8,0},{9,1},... | collective-permute-start | bytes 3145736 | tf_op jit(solution)/shard_map/ppermute | solution.py:34
  34.0 11.3 %collective-permute-start.17 = (bf16[2,64,2048]{2,1,0:T(8,128)(2,1)S(1)}, bf16[2,64,2048]{2,1,0:T(8,128)(2,1)S(1)}, u32[]{:S(2)}, u32[]{:S(2)}) collective-permute-start(bf16[2,64,2048]{2,1,0:T(8,128)(2,1)S(1)} %collective-permute-done.13.refs_2_.refs_3_), channel_id=1, source_target_pairs={{0,6},{1,7},{2,0},{3,1},{4,2},{5,3},{6,4},{7,5},{8,14},{9,15},{10,... | collective-permute-start | bytes 1572872 | tf_op jit(solution)/shard_map/ppermute | solution.py:34
  37.4 12.1 %collective-permute-start.14 = (bf16[2,64,2048]{2,1,0:T(8,128)(2,1)S(1)}, bf16[2,64,2048]{2,1,0:T(8,128)(2,1)S(1)}, u32[]{:S(2)}, u32[]{:S(2)}) collective-permute-start(bf16[2,64,2048]{2,1,0:T(8,128)(2,1)S(1)} %collective-permute-done.13.refs_2_.refs_3_), channel_id=1, source_target_pairs={{0,2},{1,3},{2,4},{3,5},{4,6},{5,7},{6,0},{7,1},{8,10},{9,11},{10,... | collective-permute-start | bytes 1572872 | tf_op jit(solution)/shard_map/ppermute | solution.py:34
  37.5 15.5 %collective-permute-start.10 = (bf16[2,64,2048]{2,1,0:T(8,128)(2,1)S(1)}, bf16[2,64,2048]{2,1,0:T(8,128)(2,1)S(1)}, u32[]{:S(2)}, u32[]{:S(2)}) collective-permute-start(bf16[2,64,2048]{2,1,0:T(8,128)(2,1)S(1)} %collective-permute-done.7.refs_2_.refs_3_), channel_id=1, source_target_pairs={{0,32},{1,33},{2,34},{3,35},{4,36},{5,37},{6,38},{7,39},{8,40},{9,... | collective-permute-start | bytes 1572872 | tf_op jit(solution)/shard_map/ppermute | solution.py:34
  38.7 16.9 %collective-permute-start = (bf16[3,64,2048]{2,1,0:T(8,128)(2,1)S(1)}, bf16[3,64,2048]{2,1,0:T(8,128)(2,1)S(1)}, u32[]{:S(2)}, u32[]{:S(2)}) collective-permute-start(bf16[3,64,2048]{2,1,0:T(8,128)(2,1)S(1)} %get-tuple-element.77.refs_2_), channel_id=1, source_target_pairs={{0,1},{1,0},{2,3},{3,2},{4,5},{5,4},{6,7},{7,6},{8,9},{9,8},{10,11... | collective-permute-start | bytes 2359304 | tf_op jit(solution)/shard_map/ppermute | solution.py:34
  45.3 13.0 %collective-permute-start.1 = (bf16[3,64,2048]{2,1,0:T(8,128)(2,1)S(1)}, bf16[3,64,2048]{2,1,0:T(8,128)(2,1)S(1)}, u32[]{:S(2)}, u32[]{:S(2)}) collective-permute-start(bf16[3,64,2048]{2,1,0:T(8,128)(2,1)S(1)} %get-tuple-element.78.refs_3_), channel_id=1, source_target_pairs={{0,1},{1,0},{2,3},{3,2},{4,5},{5,4},{6,7},{7,6},{8,9},{9,8},{10,11... | collective-permute-start | bytes 2359304 | tf_op jit(solution)/shard_map/ppermute | solution.py:34
  49.6 8.8 %collective-permute-start.5 = (bf16[3,64,2048]{2,1,0:T(8,128)(2,1)S(1)}, bf16[3,64,2048]{2,1,0:T(8,128)(2,1)S(1)}, u32[]{:S(2)}, u32[]{:S(2)}) collective-permute-start(bf16[3,64,2048]{2,1,0:T(8,128)(2,1)S(1)} %collective-permute-done.3.refs_4_), channel_id=1, source_target_pairs={{0,1},{1,0},{2,3},{3,2},{4,5},{5,4},{6,7},{7,6},{8,9},{9,8},{10,11... | collective-permute-start | bytes 2359304 | tf_op jit(solution)/shard_map/ppermute | solution.py:34
  53.0 5.4 %collective-permute-start.6 = (bf16[3,64,2048]{2,1,0:T(8,128)(2,1)S(1)}, bf16[3,64,2048]{2,1,0:T(8,128)(2,1)S(1)}, u32[]{:S(2)}, u32[]{:S(2)}) collective-permute-start(bf16[3,64,2048]{2,1,0:T(8,128)(2,1)S(1)} %collective-permute-done.4.refs_5_), channel_id=1, source_target_pairs={{0,1},{1,0},{2,3},{3,2},{4,5},{5,4},{6,7},{7,6},{8,9},{9,8},{10,11... | collective-permute-start | bytes 2359304 | tf_op jit(solution)/shard_map/ppermute | solution.py:34
  54.3 14.6 %collective-permute-start.16 = (bf16[2,64,2048]{2,1,0:T(8,128)(2,1)S(1)}, bf16[2,64,2048]{2,1,0:T(8,128)(2,1)S(1)}, u32[]{:S(2)}, u32[]{:S(2)}) collective-permute-start(bf16[2,64,2048]{2,1,0:T(8,128)(2,1)S(1)} %collective-permute-done.9.refs_6_.refs_7_), channel_id=1, source_target_pairs={{0,32},{1,33},{2,34},{3,35},{4,36},{5,37},{6,38},{7,39},{8,40},{9,... | collective-permute-start | bytes 1572872 | tf_op jit(solution)/shard_map/ppermute | solution.py:34
  55.5 11.9 %collective-permute-start.19 = (bf16[1,64,2048]{2,1,0:T(8,128)(2,1)S(1)}, bf16[1,64,2048]{2,1,0:T(8,128)(2,1)S(1)}, u32[]{:S(2)}, u32[]{:S(2)}) collective-permute-start(bf16[1,64,2048]{2,1,0:T(8,128)(2,1)S(1)} %slice.17), channel_id=1, source_target_pairs={{0,6},{1,7},{2,0},{3,1},{4,2},{5,3},{6,4},{7,5},{8,14},{9,15},{10,... | collective-permute-start | bytes 786440 | tf_op jit(solution)/shard_map/ppermute | solution.py:34
  58.3 9.1 %collective-permute-start.18 = (bf16[1,64,2048]{2,1,0:T(8,128)(2,1)S(1)}, bf16[1,64,2048]{2,1,0:T(8,128)(2,1)S(1)}, u32[]{:S(2)}, u32[]{:S(2)}) collective-permute-start(bf16[1,64,2048]{2,1,0:T(8,128)(2,1)S(1)} %slice.16), channel_id=1, source_target_pairs={{0,2},{1,3},{2,4},{3,5},{4,6},{5,7},{6,0},{7,1},{8,10},{9,11},{10,... | collective-permute-start | bytes 786440 | tf_op jit(solution)/shard_map/ppermute | solution.py:34
  58.3 10.6 %collective-permute-start.20 = (bf16[1,64,2048]{2,1,0:T(8,128)(2,1)S(1)}, bf16[1,64,2048]{2,1,0:T(8,128)(2,1)S(1)}, u32[]{:S(2)}, u32[]{:S(2)}) collective-permute-start(bf16[1,64,2048]{2,1,0:T(8,128)(2,1)S(1)} %get-tuple-element.143), channel_id=1, source_target_pairs={{0,2},{1,3},{2,4},{3,5},{4,6},{5,7},{6,0},{7,1},{8,10},{9,11},{10,... | collective-permute-start | bytes 786440 | tf_op jit(solution)/shard_map/ppermute | solution.py:34
  58.4 10.5 %collective-permute-start.21 = (bf16[1,64,2048]{2,1,0:T(8,128)(2,1)S(1)}, bf16[1,64,2048]{2,1,0:T(8,128)(2,1)S(1)}, u32[]{:S(2)}, u32[]{:S(2)}) collective-permute-start(bf16[1,64,2048]{2,1,0:T(8,128)(2,1)S(1)} %get-tuple-element.142), channel_id=1, source_target_pairs={{0,6},{1,7},{2,0},{3,1},{4,2},{5,3},{6,4},{7,5},{8,14},{9,15},{10,... | collective-permute-start | bytes 786440 | tf_op jit(solution)/shard_map/ppermute | solution.py:34
  73.2 7.5 %collective-permute-start.25 = (bf16[2,128,2048]{2,1,0:T(8,128)(2,1)S(1)}, bf16[2,128,2048]{2,1,0:T(8,128)(2,1)S(1)}, u32[]{:S(2)}, u32[]{:S(2)}) collective-permute-start(bf16[2,128,2048]{2,1,0:T(8,128)(2,1)S(1)} %get-tuple-element.106), channel_id=1, source_target_pairs={{0,1},{1,0},{2,3},{3,2},{4,5},{5,4},{6,7},{7,6},{8,9},{9,8},{10,11... | collective-permute-start | bytes 3145736 | tf_op jit(solution)/shard_map/ppermute | solution.py:34
  80.6 5.2 %collective-permute-start.22 = (bf16[2,128,2048]{2,1,0:T(8,128)(2,1)S(1)}, bf16[2,128,2048]{2,1,0:T(8,128)(2,1)S(1)}, u32[]{:S(2)}, u32[]{:S(2)}) collective-permute-start(bf16[2,128,2048]{2,1,0:T(8,128)(2,1)S(1)} %get-tuple-element.97), channel_id=1, source_target_pairs={{0,1},{1,0},{2,3},{3,2},{4,5},{5,4},{6,7},{7,6},{8,9},{9,8},{10,11... | collective-permute-start | bytes 3145736 | tf_op jit(solution)/shard_map/ppermute | solution.py:34
  83.0 4.5 %collective-permute-start.30 = (bf16[2,128,2048]{2,1,0:T(8,128)(2,1)S(1)}, bf16[2,128,2048]{2,1,0:T(8,128)(2,1)S(1)}, u32[]{:S(2)}, u32[]{:S(2)}) collective-permute-start(bf16[2,128,2048]{2,1,0:T(8,128)(2,1)S(1)} %get-tuple-element.130), channel_id=1, source_target_pairs={{0,1},{1,0},{2,3},{3,2},{4,5},{5,4},{6,7},{7,6},{8,9},{9,8},{10,11... | collective-permute-start | bytes 3145736 | tf_op jit(solution)/shard_map/ppermute | solution.py:34
  83.6 9.6 %copy-start.7 = (bf16[1,2,2048,128]{3,2,1,0:T(8,128)(2,1)S(1)}, bf16[1,2,2048,128]{3,2,1,0:T(8,128)(2,1)}, u32[]{:S(2)}) copy-start(bf16[1,2,2048,128]{3,2,1,0:T(8,128)(2,1)} %refs_5_.4) | copy-start | bytes 3145732
  83.6 9.6 %copy-start.8 = (bf16[1,2,2048,128]{3,2,1,0:T(8,128)(2,1)S(1)}, bf16[1,2,2048,128]{3,2,1,0:T(8,128)(2,1)}, u32[]{:S(2)}) copy-start(bf16[1,2,2048,128]{3,2,1,0:T(8,128)(2,1)} %refs_6_.4) | copy-start | bytes 3145732
  83.7 8.0 %collective-permute-start.26 = (bf16[64,2048]{1,0:T(8,128)(2,1)S(1)}, bf16[64,2048]{1,0:T(8,128)(2,1)S(1)}, u32[]{:S(2)}, u32[]{:S(2)}) collective-permute-start(bf16[64,2048]{1,0:T(8,128)(2,1)S(1)} %get-tuple-element.108), channel_id=1, source_target_pairs={{0,16},{1,17},{2,18},{3,19},{4,20},{5,21},{6,22},{7,23},{8,24},{9,... | collective-permute-start | bytes 786440 | tf_op jit(solution)/shard_map/ppermute | solution.py:34
  84.1 9.1 %collective-permute-start.27 = (bf16[64,2048]{1,0:T(8,128)(2,1)S(1)}, bf16[64,2048]{1,0:T(8,128)(2,1)S(1)}, u32[]{:S(2)}, u32[]{:S(2)}) collective-permute-start(bf16[64,2048]{1,0:T(8,128)(2,1)S(1)} %get-tuple-element.109), channel_id=1, source_target_pairs={{0,48},{1,49},{2,50},{3,51},{4,52},{5,53},{6,54},{7,55},{8,56},{9,... | collective-permute-start | bytes 786440 | tf_op jit(solution)/shard_map/ppermute | solution.py:34
  85.8 7.4 %copy-start = (f32[2,2048,128]{2,1,0:T(8,128)S(1)}, f32[2,2048,128]{2,1,0:T(8,128)}, u32[]{:S(2)}) copy-start(f32[2,2048,128]{2,1,0:T(8,128)} %refs_2_.4) | copy-start | bytes 6291460
  85.8 7.4 %copy-start.2 = (f32[1,2,2048,128]{3,2,1,0:T(8,128)S(1)}, f32[1,2,2048,128]{3,2,1,0:T(8,128)}, u32[]{:S(2)}) copy-start(f32[1,2,2048,128]{3,2,1,0:T(8,128)} %refs_4_.4) | copy-start | bytes 6291460
  85.9 12.5 %collective-permute-start.23 = (bf16[64,2048]{1,0:T(8,128)(2,1)S(1)}, bf16[64,2048]{1,0:T(8,128)(2,1)S(1)}, u32[]{:S(2)}, u32[]{:S(2)}) collective-permute-start(bf16[64,2048]{1,0:T(8,128)(2,1)S(1)} %get-tuple-element.99), channel_id=1, source_target_pairs={{0,16},{1,17},{2,18},{3,19},{4,20},{5,21},{6,22},{7,23},{8,24},{9,... | collective-permute-start | bytes 786440 | tf_op jit(solution)/shard_map/ppermute | solution.py:34
  86.3 12.2 %collective-permute-start.24 = (bf16[64,2048]{1,0:T(8,128)(2,1)S(1)}, bf16[64,2048]{1,0:T(8,128)(2,1)S(1)}, u32[]{:S(2)}, u32[]{:S(2)}) collective-permute-start(bf16[64,2048]{1,0:T(8,128)(2,1)S(1)} %get-tuple-element.100), channel_id=1, source_target_pairs={{0,48},{1,49},{2,50},{3,51},{4,52},{5,53},{6,54},{7,55},{8,56},{9,... | collective-permute-start | bytes 786440 | tf_op jit(solution)/shard_map/ppermute | solution.py:34
  87.6 16.5 %collective-permute-start.31 = (bf16[64,2048]{1,0:T(8,128)(2,1)S(1)}, bf16[64,2048]{1,0:T(8,128)(2,1)S(1)}, u32[]{:S(2)}, u32[]{:S(2)}) collective-permute-start(bf16[64,2048]{1,0:T(8,128)(2,1)S(1)} %get-tuple-element.132), channel_id=1, source_target_pairs={{0,16},{1,17},{2,18},{3,19},{4,20},{5,21},{6,22},{7,23},{8,24},{9,... | collective-permute-start | bytes 786440 | tf_op jit(solution)/shard_map/ppermute | solution.py:34
  91.6 12.4 %collective-permute-start.32 = (bf16[64,2048]{1,0:T(8,128)(2,1)S(1)}, bf16[64,2048]{1,0:T(8,128)(2,1)S(1)}, u32[]{:S(2)}, u32[]{:S(2)}) collective-permute-start(bf16[64,2048]{1,0:T(8,128)(2,1)S(1)} %get-tuple-element.133), channel_id=1, source_target_pairs={{0,48},{1,49},{2,50},{3,51},{4,52},{5,53},{6,54},{7,55},{8,56},{9,... | collective-permute-start | bytes 786440 | tf_op jit(solution)/shard_map/ppermute | solution.py:34
  95.1 14.5 %collective-permute-start.29 = (bf16[2048,128]{1,0:T(8,128)(2,1)S(1)}, bf16[2048,128]{1,0:T(8,128)(2,1)S(1)}, u32[]{:S(2)}, u32[]{:S(2)}) collective-permute-start(bf16[2048,128]{1,0:T(8,128)(2,1)S(1)} %get-tuple-element.113.refs_0_), channel_id=1, source_target_pairs={{0,64},{64,0},{1,65},{65,1},{2,66},{66,2},{3,67},{67,3},{4,68},{68... | collective-permute-start | bytes 1572872 | tf_op jit(solution)/shard_map/ppermute | solution.py:68
  98.5 5.6 %copy-start.5 = (f32[1,128,2048]{2,1,0:T(8,128)S(1)}, f32[1,128,2048]{2,1,0:T(8,128)}, u32[]{:S(2)}) copy-start(f32[1,128,2048]{2,1,0:T(8,128)} %refs_4_.5) | copy-start | bytes 3145732
  98.5 5.6 %copy-start.6 = (f32[128,2048]{1,0:T(8,128)S(1)}, f32[128,2048]{1,0:T(8,128)}, u32[]{:S(2)}) copy-start(f32[128,2048]{1,0:T(8,128)} %refs_2_.5) | copy-start | bytes 3145732
  98.5 5.6 %copy-start.10 = (bf16[1,128,2048]{2,1,0:T(8,128)(2,1)S(1)}, bf16[1,128,2048]{2,1,0:T(8,128)(2,1)}, u32[]{:S(2)}) copy-start(bf16[1,128,2048]{2,1,0:T(8,128)(2,1)} %refs_5_.5) | copy-start | bytes 1572868
  98.5 5.6 %copy-start.11 = (bf16[1,128,2048]{2,1,0:T(8,128)(2,1)S(1)}, bf16[1,128,2048]{2,1,0:T(8,128)(2,1)}, u32[]{:S(2)}) copy-start(bf16[1,128,2048]{2,1,0:T(8,128)(2,1)} %refs_6_.5) | copy-start | bytes 1572868
  100.4 19.6 %collective-permute-start.28 = (bf16[2048,128]{1,0:T(8,128)(2,1)S(1)}, bf16[2048,128]{1,0:T(8,128)(2,1)S(1)}, u32[]{:S(2)}, u32[]{:S(2)}) collective-permute-start(bf16[2048,128]{1,0:T(8,128)(2,1)S(1)} %get-tuple-element.112.refs_0_), channel_id=1, source_target_pairs={{0,64},{64,0},{1,65},{65,1},{2,66},{66,2},{3,67},{67,3},{4,68},{68... | collective-permute-start | bytes 1572872 | tf_op jit(solution)/shard_map/ppermute | solution.py:68
  104.1 5.5 %copy-start.3 = (f32[2,2048,128]{2,1,0:T(8,128)S(1)}, f32[2,2048,128]{2,1,0:T(8,128)}, u32[]{:S(2)}) copy-start(f32[2,2048,128]{2,1,0:T(8,128)} %refs_3_.4) | copy-start | bytes 6291460
  106.0 25.2 %collective-permute-start.33 = (bf16[128,2048]{1,0:T(8,128)(2,1)S(1)}, bf16[128,2048]{1,0:T(8,128)(2,1)S(1)}, u32[]{:S(2)}, u32[]{:S(2)}) collective-permute-start(bf16[128,2048]{1,0:T(8,128)(2,1)S(1)} %get-tuple-element.134.refs_0_), channel_id=1, source_target_pairs={{0,64},{64,0},{1,65},{65,1},{2,66},{66,2},{3,67},{67,3},{4,68},{68... | collective-permute-start | bytes 1572872 | tf_op jit(solution)/shard_map/ppermute | solution.py:68
  120.0 11.2 %copy-start.9 = (f32[128,2048]{1,0:T(8,128)S(1)}, f32[128,2048]{1,0:T(8,128)}, u32[]{:S(2)}) copy-start(f32[128,2048]{1,0:T(8,128)} %refs_3_.5) | copy-start | bytes 3145732

commit v5 on v4

--- a/solution.py
+++ b/solution.py
@@ -70,6 +70,31 @@
 
 def struct(shape, dtype):
     return jax.ShapeDtypeStruct(shape, dtype)
+
+
+def own_rows_kernel(in_ref, cot_ref, out_ref, sems):
+    copies = [
+        pltpu.make_async_copy(ref, out_ref.at[k : k + 1], sems.at[k])
+        for k, ref in enumerate((in_ref, cot_ref))
+    ]
+    for copy in copies:
+        copy.start()
+    for copy in copies:
+        copy.wait()
+
+
+def own_rows(inputs, cotangent):
+    rows, depth = inputs.shape[1:]
+    return pl.pallas_call(
+        own_rows_kernel,
+        in_specs=[pl.BlockSpec(memory_space=pl.ANY)] * 2,
+        out_specs=VMEM,
+        out_shape=struct((2, rows, depth), BF16),
+        scratch_shapes=[pltpu.SemaphoreType.DMA((2,))],
+        cost_estimate=pl.CostEstimate(flops=0, bytes_accessed=rows * depth * 8, transcendentals=0),
+        compiler_params=pltpu.CompilerParams(vmem_limit_bytes=56 * 1024 * 1024),
+        name="own_rows",
+    )(inputs, cotangent)
 
 
 def weights_kernel(in_ref, down_ref, all_ref, *outs):
@@ -345,7 +370,7 @@
     outer_in,
     outer_down,
 ):
-    own = jnp.concatenate([inputs, cotangent])
+    own = own_rows(inputs, cotangent)
     low, high = up_y(own), down_y(own)
     by_x, by_z = far_x(own), swap_z(own)
     mine, *halves = own_weights(params_in, params_down)

time: 134 us -> 134 us (level)
  local copies, waits for them, and re-layouts: 4.86 us -> 2.94 us
  Pallas kernels: 26.9 us -> 28.7 us
    pallas_call x0 -> x1, Pallas kernels: none -> 1.84 us  [own_rows(): pl.pallas_call(own_rows_kernel, in_specs=[pl.BlockSpec(memory_space=pl.AN...]
    unnamed x25 -> x26, local copies, waits for them, and re-layouts: 3.82 us -> 2.86 us
where the time goes in v5:
time: 134 us; the launch traced here: 133 us
  starting transfers between devices  61.9 us (46%)
  waiting for transfers between devices  38.3 us (29%)
  Pallas kernels  28.7 us (21%)
  local copies, waits for them, and re-layouts  2.94 us (2%)
    ppermute x31, starting transfers between devices, move(): return lax.ppermute(value, 'fsdp', pairs)  51.4 us
    ppermute x31, waiting for transfers between devices, move(): return lax.ppermute(value, 'fsdp', pairs)  19.5 us
    ppermute x3, waiting for transfers between devices, swap_replica(): return lax.ppermute(value, 'replica', [(0, 1), (1, 0)])  18.7 us
    ppermute x3, starting transfers between devices, swap_replica(): return lax.ppermute(value, 'replica', [(0, 1), (1, 0)])  10.5 us
    pallas_call x4, Pallas kernels, forward(): pl.pallas_call(functools.partial(forward_kernel, [(p[1], p[3]) for p in p...  7.68 us
    pallas_call x3, Pallas kernels, gradient(): pl.pallas_call(functools.partial(gradient_kernel, len(left), start), in_s...  7.01 us
    pallas_call x3, Pallas kernels, inner_step(): pl.pallas_call(functools.partial(inner_kernel, which, start), grid=(size...  5.77 us
    pallas_call x3, Pallas kernels, outer_step(): pl.pallas_call(functools.partial(outer_kernel, which, start), grid=(size...  4.28 us
  transfers between devices with their start and end apart: 34, of which 11 were waited for; matrix products, arithmetic and copies ran while one was open for 0% of the time, Pallas kernels for 16%

profile of v5, /device:TPU:1, one launch (start us, length us, event | category | flops | bytes accessed | tf_op | source)
XLA Modules:
  0.0 132.8 jit_solution(2905816672404917974)
XLA Ops:
  0.6 1.8 %own_rows.1.refs_0_.refs_1_ = bf16[2,64,2048]{2,1,0:T(8,128)(2,1)} custom-call(bf16[1,64,2048]{2,1,0:T(8,128)(2,1)} %in_ref.3, bf16[1,64,2048]{2,1,0:T(8,128)(2,1)} %cot_ref.1), custom_call_target="tpu_custom_call" | custom-call | bytes 1048576 | tf_op jit(solution)/shard_map/own_rows/pallas_call | solution.py:88
  2.5 3.7 %collective-permute-start.2 = (bf16[2,64,2048]{2,1,0:T(8,128)(2,1)}, bf16[2,64,2048]{2,1,0:T(8,128)(2,1)S(1)}, u32[]{:S(2)}, u32[]{:S(2)}) collective-permute-start(bf16[2,64,2048]{2,1,0:T(8,128)(2,1)} %own_rows.1.refs_0_.refs_1_), channel_id=1, source_target_pairs={{0,32},{1,33},{2,34},{3,35},{4,36},{5,37},{6,38},{7,39},{8,40},{9,... | collective-permute-start | bytes 1572872 | tf_op jit(solution)/shard_map/ppermute | solution.py:34
  6.1 1.6 %collective-permute-start.12 = (bf16[2,64,2048]{2,1,0:T(8,128)(2,1)}, bf16[2,64,2048]{2,1,0:T(8,128)(2,1)S(1)}, u32[]{:S(2)}, u32[]{:S(2)}) collective-permute-start(bf16[2,64,2048]{2,1,0:T(8,128)(2,1)} %own_rows.1.refs_0_.refs_1_), channel_id=1, source_target_pairs={{0,8},{1,9},{2,10},{3,11},{4,12},{5,13},{6,14},{7,15},{8,0},{9,1},... | collective-permute-start | bytes 1572872 | tf_op jit(solution)/shard_map/ppermute | solution.py:34
  7.8 2.7 %collective-permute-start.8 = (bf16[2,64,2048]{2,1,0:T(8,128)(2,1)}, bf16[2,64,2048]{2,1,0:T(8,128)(2,1)S(1)}, u32[]{:S(2)}, u32[]{:S(2)}) collective-permute-start(bf16[2,64,2048]{2,1,0:T(8,128)(2,1)} %own_rows.1.refs_0_.refs_1_), channel_id=1, source_target_pairs={{0,6},{1,7},{2,0},{3,1},{4,2},{5,3},{6,4},{7,5},{8,14},{9,15},{10,... | collective-permute-start | bytes 1572872 | tf_op jit(solution)/shard_map/ppermute | solution.py:34
  10.5 1.6 %copy-done.1 = f32[1,2,2048,128]{3,2,1,0:T(8,128)S(1)} copy-done((f32[1,2,2048,128]{3,2,1,0:T(8,128)S(1)}, f32[1,2,2048,128]{3,2,1,0:T(8,128)}, u32[]{:S(2)}) %copy-start.1) | copy-done | bytes 2097176
  12.1 1.2 copy-done.5
  13.3 1.5 %own_weights.1 = (bf16[2,3,64,2048]{3,2,1,0:T(8,128)(2,1)}, bf16[3,64,2048]{2,1,0:T(8,128)(2,1)S(1)}, bf16[3,64,2048]{2,1,0:T(8,128)(2,1)S(1)}) custom-call(f32[1,2,2048,128]{3,2,1,0:T(8,128)S(1)} %copy-done.1, f32[1,128,2048]{2,1,0:T(8,128)S(1)} %copy-done.5), custom_call_target="tpu_custom_call" | custom-call | flops 786432 | bytes 4718592 | tf_op jit(solution)/shard_map/own_weights/pallas_call | solution.py:113
  14.8 2.7 %collective-permute-done.2.refs_0_.refs_1_ = bf16[2,64,2048]{2,1,0:T(8,128)(2,1)S(1)} collective-permute-done((bf16[2,64,2048]{2,1,0:T(8,128)(2,1)}, bf16[2,64,2048]{2,1,0:T(8,128)(2,1)S(1)}, u32[]{:S(2)}, u32[]{:S(2)}) %collective-permute-start.2) | collective-permute-done | bytes 524320 | tf_op jit(solution)/shard_map/ppermute | solution.py:34
  17.5 1.6 %collective-permute-start.3 = (bf16[3,64,2048]{2,1,0:T(8,128)(2,1)S(1)}, bf16[3,64,2048]{2,1,0:T(8,128)(2,1)S(1)}, u32[]{:S(2)}, u32[]{:S(2)}) collective-permute-start(bf16[3,64,2048]{2,1,0:T(8,128)(2,1)S(1)} %get-tuple-element.77.refs_2_), channel_id=1, source_target_pairs={{0,16},{1,17},{2,18},{3,19},{4,20},{5,21},{6,22},{7,23},{8,24},{9,... | collective-permute-start | bytes 2359304 | tf_op jit(solution)/shard_map/ppermute | solution.py:34
  19.1 1.8 %collective-permute-start.4 = (bf16[3,64,2048]{2,1,0:T(8,128)(2,1)S(1)}, bf16[3,64,2048]{2,1,0:T(8,128)(2,1)S(1)}, u32[]{:S(2)}, u32[]{:S(2)}) collective-permute-start(bf16[3,64,2048]{2,1,0:T(8,128)(2,1)S(1)} %get-tuple-element.78.refs_3_), channel_id=1, source_target_pairs={{0,48},{1,49},{2,50},{3,51},{4,52},{5,53},{6,54},{7,55},{8,56},{9,... | collective-permute-start | bytes 2359304 | tf_op jit(solution)/shard_map/ppermute | solution.py:34
  20.9 1.6 %collective-permute-start.13 = (bf16[2,64,2048]{2,1,0:T(8,128)(2,1)S(1)}, bf16[2,64,2048]{2,1,0:T(8,128)(2,1)S(1)}, u32[]{:S(2)}, u32[]{:S(2)}) collective-permute-start(bf16[2,64,2048]{2,1,0:T(8,128)(2,1)S(1)} %collective-permute-done.2.refs_0_.refs_1_), channel_id=1, source_target_pairs={{0,8},{1,9},{2,10},{3,11},{4,12},{5,13},{6,14},{7,15},{8,0},{9,1},... | collective-permute-start | bytes 1572872 | tf_op jit(solution)/shard_map/ppermute | solution.py:34
  22.6 2.7 %collective-permute-start.11 = (bf16[2,64,2048]{2,1,0:T(8,128)(2,1)S(1)}, bf16[2,64,2048]{2,1,0:T(8,128)(2,1)S(1)}, u32[]{:S(2)}, u32[]{:S(2)}) collective-permute-start(bf16[2,64,2048]{2,1,0:T(8,128)(2,1)S(1)} %collective-permute-done.2.refs_0_.refs_1_), channel_id=1, source_target_pairs={{0,6},{1,7},{2,0},{3,1},{4,2},{5,3},{6,4},{7,5},{8,14},{9,15},{10,... | collective-permute-start | bytes 1572872 | tf_op jit(solution)/shard_map/ppermute | solution.py:34
  25.4 7.2 %collective-permute-done.13.refs_2_.refs_3_ = bf16[2,64,2048]{2,1,0:T(8,128)(2,1)S(1)} collective-permute-done((bf16[2,64,2048]{2,1,0:T(8,128)(2,1)S(1)}, bf16[2,64,2048]{2,1,0:T(8,128)(2,1)S(1)}, u32[]{:S(2)}, u32[]{:S(2)}) %collective-permute-start.13) | collective-permute-done | bytes 524320 | tf_op jit(solution)/shard_map/ppermute | solution.py:34
  32.6 1.3 collective-permute-start.15
  34.1 3.4 %collective-permute-start.17 = (bf16[2,64,2048]{2,1,0:T(8,128)(2,1)S(1)}, bf16[2,64,2048]{2,1,0:T(8,128)(2,1)S(1)}, u32[]{:S(2)}, u32[]{:S(2)}) collective-permute-start(bf16[2,64,2048]{2,1,0:T(8,128)(2,1)S(1)} %collective-permute-done.13.refs_2_.refs_3_), channel_id=1, source_target_pairs={{0,6},{1,7},{2,0},{3,1},{4,2},{5,3},{6,4},{7,5},{8,14},{9,15},{10,... | collective-permute-start | bytes 1572872 | tf_op jit(solution)/shard_map/ppermute | solution.py:34
  37.6 1.2 collective-permute-start.10
  38.8 3.4 %collective-permute-start = (bf16[3,64,2048]{2,1,0:T(8,128)(2,1)S(1)}, bf16[3,64,2048]{2,1,0:T(8,128)(2,1)S(1)}, u32[]{:S(2)}, u32[]{:S(2)}) collective-permute-start(bf16[3,64,2048]{2,1,0:T(8,128)(2,1)S(1)} %get-tuple-element.77.refs_2_), channel_id=1, source_target_pairs={{0,1},{1,0},{2,3},{3,2},{4,5},{5,4},{6,7},{7,6},{8,9},{9,8},{10,11... | collective-permute-start | bytes 2359304 | tf_op jit(solution)/shard_map/ppermute | solution.py:34
  42.2 3.3 %collective-permute-done.17.refs_2_.refs_3_ = bf16[2,64,2048]{2,1,0:T(8,128)(2,1)S(1)} collective-permute-done((bf16[2,64,2048]{2,1,0:T(8,128)(2,1)S(1)}, bf16[2,64,2048]{2,1,0:T(8,128)(2,1)S(1)}, u32[]{:S(2)}, u32[]{:S(2)}) %collective-permute-start.17) | collective-permute-done | bytes 524320 | tf_op jit(solution)/shard_map/ppermute | solution.py:34
  45.5 4.2 %collective-permute-start.1 = (bf16[3,64,2048]{2,1,0:T(8,128)(2,1)S(1)}, bf16[3,64,2048]{2,1,0:T(8,128)(2,1)S(1)}, u32[]{:S(2)}, u32[]{:S(2)}) collective-permute-start(bf16[3,64,2048]{2,1,0:T(8,128)(2,1)S(1)} %get-tuple-element.78.refs_3_), channel_id=1, source_target_pairs={{0,1},{1,0},{2,3},{3,2},{4,5},{5,4},{6,7},{7,6},{8,9},{9,8},{10,11... | collective-permute-start | bytes 2359304 | tf_op jit(solution)/shard_map/ppermute | solution.py:34
  49.7 3.4 %collective-permute-start.5 = (bf16[3,64,2048]{2,1,0:T(8,128)(2,1)S(1)}, bf16[3,64,2048]{2,1,0:T(8,128)(2,1)S(1)}, u32[]{:S(2)}, u32[]{:S(2)}) collective-permute-start(bf16[3,64,2048]{2,1,0:T(8,128)(2,1)S(1)} %collective-permute-done.3.refs_4_), channel_id=1, source_target_pairs={{0,1},{1,0},{2,3},{3,2},{4,5},{5,4},{6,7},{7,6},{8,9},{9,8},{10,11... | collective-permute-start | bytes 2359304 | tf_op jit(solution)/shard_map/ppermute | solution.py:34
  53.5 0.8 collective-permute-done.15.refs_4_.refs_5_.refs_6_.refs_7_
  54.4 1.2 collective-permute-start.16
  55.6 2.8 %collective-permute-start.19 = (bf16[1,64,2048]{2,1,0:T(8,128)(2,1)S(1)}, bf16[1,64,2048]{2,1,0:T(8,128)(2,1)S(1)}, u32[]{:S(2)}, u32[]{:S(2)}) collective-permute-start(bf16[1,64,2048]{2,1,0:T(8,128)(2,1)S(1)} %slice.17), channel_id=1, source_target_pairs={{0,6},{1,7},{2,0},{3,1},{4,2},{5,3},{6,4},{7,5},{8,14},{9,15},{10,... | collective-permute-start | bytes 786440 | tf_op jit(solution)/shard_map/ppermute | solution.py:34
  58.6 2.8 %collective-permute-start.21 = (bf16[1,64,2048]{2,1,0:T(8,128)(2,1)S(1)}, bf16[1,64,2048]{2,1,0:T(8,128)(2,1)S(1)}, u32[]{:S(2)}, u32[]{:S(2)}) collective-permute-start(bf16[1,64,2048]{2,1,0:T(8,128)(2,1)S(1)} %get-tuple-element.142), channel_id=1, source_target_pairs={{0,6},{1,7},{2,0},{3,1},{4,2},{5,3},{6,4},{7,5},{8,14},{9,15},{10,... | collective-permute-start | bytes 786440 | tf_op jit(solution)/shard_map/ppermute | solution.py:34
  61.8 1.9 %forward.6 = (bf16[512,256]{1,0:T(8,128)(2,1)S(1)}, bf16[512,256]{1,0:T(8,128)(2,1)S(1)}, bf16[512,256]{1,0:T(8,128)(2,1)S(1)}, bf16[256,2048]{1,0:T(8,128)(2,1)S(1)}, bf16[256,2048]{1,0:T(8,128)(2,1)S(1)}) custom-call(bf16[1024,2048]{1,0:T(8,128)(2,1)S(1)} %get-tuple-element.79.in_ref, bf16[512,2048]{1,0:T(8,128)(2,1)S(1)} %get-tuple-element.80.down_ref, ...), custom_call_target="tpu_custom_call" | custom-call | flops 1610612736 | bytes 10485760 | tf_op jit(solution)/shard_map/forward/pallas_call | solution.py:182
  63.7 1.9 %forward.5 = (bf16[512,256]{1,0:T(8,128)(2,1)S(1)}, bf16[512,256]{1,0:T(8,128)(2,1)S(1)}, bf16[512,256]{1,0:T(8,128)(2,1)S(1)}, bf16[256,2048]{1,0:T(8,128)(2,1)S(1)}, bf16[256,2048]{1,0:T(8,128)(2,1)S(1)}) custom-call(bf16[1024,2048]{1,0:T(8,128)(2,1)S(1)} %get-tuple-element.79.in_ref, bf16[512,2048]{1,0:T(8,128)(2,1)S(1)} %get-tuple-element.80.down_ref, ...), custom_call_target="tpu_custom_call" | custom-call | flops 1610612736 | bytes 10485760 | tf_op jit(solution)/shard_map/forward/pallas_call | solution.py:182
  65.7 1.9 %forward.4 = (bf16[512,256]{1,0:T(8,128)(2,1)S(1)}, bf16[512,256]{1,0:T(8,128)(2,1)S(1)}, bf16[512,256]{1,0:T(8,128)(2,1)S(1)}, bf16[256,2048]{1,0:T(8,128)(2,1)S(1)}, bf16[256,2048]{1,0:T(8,128)(2,1)S(1)}) custom-call(bf16[1024,2048]{1,0:T(8,128)(2,1)S(1)} %get-tuple-element.79.in_ref, bf16[512,2048]{1,0:T(8,128)(2,1)S(1)} %get-tuple-element.80.down_ref, ...), custom_call_target="tpu_custom_call" | custom-call | flops 1610612736 | bytes 10485760 | tf_op jit(solution)/shard_map/forward/pallas_call | solution.py:182
  67.6 1.4 %collective-permute-done.20.refs_6_ = bf16[1,64,2048]{2,1,0:T(8,128)(2,1)S(1)} collective-permute-done((bf16[1,64,2048]{2,1,0:T(8,128)(2,1)S(1)}, bf16[1,64,2048]{2,1,0:T(8,128)(2,1)S(1)}, u32[]{:S(2)}, u32[]{:S(2)}) %collective-permute-start.20) | collective-permute-done | bytes 262176 | tf_op jit(solution)/shard_map/ppermute | solution.py:34
  69.0 1.9 %forward.7 = (bf16[512,256]{1,0:T(8,128)(2,1)S(1)}, bf16[512,256]{1,0:T(8,128)(2,1)S(1)}, bf16[512,256]{1,0:T(8,128)(2,1)S(1)}, bf16[256,2048]{1,0:T(8,128)(2,1)S(1)}, bf16[256,2048]{1,0:T(8,128)(2,1)S(1)}) custom-call(bf16[1024,2048]{1,0:T(8,128)(2,1)S(1)} %get-tuple-element.79.in_ref, bf16[512,2048]{1,0:T(8,128)(2,1)S(1)} %get-tuple-element.80.down_ref, ...), custom_call_target="tpu_custom_call" | custom-call | flops 1610612736 | bytes 10485760 | tf_op jit(solution)/shard_map/forward/pallas_call | solution.py:182
  71.0 2.3 %gradient.4 = (f32[128,2048]{1,0:T(8,128)S(1)}, f32[128,2048]{1,0:T(8,128)S(1)}, bf16[2,128,2048]{2,1,0:T(8,128)(2,1)S(1)}) custom-call(bf16[512,256]{1,0:T(8,128)(2,1)S(1)} %get-tuple-element.101.refs_0_, bf16[512,256]{1,0:T(8,128)(2,1)S(1)} %get-tuple-element.102.refs_1_, bf16[512,256]{1,0:T(8,128)(2,1)S(1)} %get-tuple-element.103.refs_2_, ...), custom_call_target="tpu_custom_call" | custom-call | flops 2147483648 | bytes 8388608 | tf_op jit(solution)/shard_map/gradient/pallas_call | solution.py:221
  73.3 5.0 %collective-permute-start.25 = (bf16[2,128,2048]{2,1,0:T(8,128)(2,1)S(1)}, bf16[2,128,2048]{2,1,0:T(8,128)(2,1)S(1)}, u32[]{:S(2)}, u32[]{:S(2)}) collective-permute-start(bf16[2,128,2048]{2,1,0:T(8,128)(2,1)S(1)} %get-tuple-element.106), channel_id=1, source_target_pairs={{0,1},{1,0},{2,3},{3,2},{4,5},{5,4},{6,7},{7,6},{8,9},{9,8},{10,11... | collective-permute-start | bytes 3145736 | tf_op jit(solution)/shard_map/ppermute | solution.py:34
  78.4 2.3 %gradient.3 = (f32[128,2048]{1,0:T(8,128)S(1)}, f32[128,2048]{1,0:T(8,128)S(1)}, bf16[2,128,2048]{2,1,0:T(8,128)(2,1)S(1)}) custom-call(bf16[512,256]{1,0:T(8,128)(2,1)S(1)} %get-tuple-element.81.refs_0_, bf16[512,256]{1,0:T(8,128)(2,1)S(1)} %get-tuple-element.86.refs_1_, bf16[512,256]{1,0:T(8,128)(2,1)S(1)} %get-tuple-element.88.refs_2_, ...), custom_call_target="tpu_custom_call" | custom-call | flops 2147483648 | bytes 8388608 | tf_op jit(solution)/shard_map/gradient/pallas_call | solution.py:221
  80.8 2.3 %gradient.5 = (f32[128,2048]{1,0:T(8,128)S(1)}, f32[128,2048]{1,0:T(8,128)S(1)}, bf16[2,128,2048]{2,1,0:T(8,128)(2,1)S(1)}) custom-call(bf16[512,256]{1,0:T(8,128)(2,1)S(1)} %get-tuple-element.121.refs_0_, bf16[512,256]{1,0:T(8,128)(2,1)S(1)} %get-tuple-element.122.refs_1_, bf16[512,256]{1,0:T(8,128)(2,1)S(1)} %get-tuple-element.123.refs_2_, ...), custom_call_target="tpu_custom_call" | custom-call | flops 2147483648 | bytes 8388608 | tf_op jit(solution)/shard_map/gradient/pallas_call | solution.py:221
  84.2 1.7 %collective-permute-start.27 = (bf16[64,2048]{1,0:T(8,128)(2,1)S(1)}, bf16[64,2048]{1,0:T(8,128)(2,1)S(1)}, u32[]{:S(2)}, u32[]{:S(2)}) collective-permute-start(bf16[64,2048]{1,0:T(8,128)(2,1)S(1)} %get-tuple-element.109), channel_id=1, source_target_pairs={{0,48},{1,49},{2,50},{3,51},{4,52},{5,53},{6,54},{7,55},{8,56},{9,... | collective-permute-start | bytes 786440 | tf_op jit(solution)/shard_map/ppermute | solution.py:34
  86.4 1.2 collective-permute-start.24
  88.1 3.7 %collective-permute-done.26.refs_2_ = bf16[64,2048]{1,0:T(8,128)(2,1)S(1)} collective-permute-done((bf16[64,2048]{1,0:T(8,128)(2,1)S(1)}, bf16[64,2048]{1,0:T(8,128)(2,1)S(1)}, u32[]{:S(2)}, u32[]{:S(2)}) %collective-permute-start.26) | collective-permute-done | bytes 262176 | tf_op jit(solution)/shard_map/ppermute | solution.py:34
  91.8 1.5 %collective-permute-start.32 = (bf16[64,2048]{1,0:T(8,128)(2,1)S(1)}, bf16[64,2048]{1,0:T(8,128)(2,1)S(1)}, u32[]{:S(2)}, u32[]{:S(2)}) collective-permute-start(bf16[64,2048]{1,0:T(8,128)(2,1)S(1)} %get-tuple-element.133), channel_id=1, source_target_pairs={{0,48},{1,49},{2,50},{3,51},{4,52},{5,53},{6,54},{7,55},{8,56},{9,... | collective-permute-start | bytes 786440 | tf_op jit(solution)/shard_map/ppermute | solution.py:34
  93.3 1.9 %inner_step.3 = (bf16[1,2,2048,128]{3,2,1,0:T(8,128)(2,1)}, bf16[1,2,2048,128]{3,2,1,0:T(8,128)(2,1)}, bf16[2048,128]{1,0:T(8,128)(2,1)S(1)}) custom-call(f32[128,2048]{1,0:T(8,128)S(1)} %get-tuple-element.105.refs_0_, bf16[2,128,2048]{2,1,0:T(8,128)(2,1)S(1)} %collective-permute-done.25.core_ref.refs_1_, ...), custom_call_target="tpu_custom_call" | custom-call | flops 5242880 | bytes 6815744 | tf_op jit(solution)/shard_map/inner_step/pallas_call | solution.py:301
  95.3 3.3 %collective-permute-start.29 = (bf16[2048,128]{1,0:T(8,128)(2,1)S(1)}, bf16[2048,128]{1,0:T(8,128)(2,1)S(1)}, u32[]{:S(2)}, u32[]{:S(2)}) collective-permute-start(bf16[2048,128]{1,0:T(8,128)(2,1)S(1)} %get-tuple-element.113.refs_0_), channel_id=1, source_target_pairs={{0,64},{64,0},{1,65},{65,1},{2,66},{66,2},{3,67},{67,3},{4,68},{68... | collective-permute-start | bytes 1572872 | tf_op jit(solution)/shard_map/ppermute | solution.py:68
  98.6 1.9 %inner_step.4 = (bf16[1,2,2048,128]{3,2,1,0:T(8,128)(2,1)}, bf16[1,2,2048,128]{3,2,1,0:T(8,128)(2,1)}, bf16[2048,128]{1,0:T(8,128)(2,1)S(1)}) custom-call(f32[128,2048]{1,0:T(8,128)S(1)} %get-tuple-element.96.refs_0_, bf16[2,128,2048]{2,1,0:T(8,128)(2,1)S(1)} %collective-permute-done.22.core_ref.refs_1_, ...), custom_call_target="tpu_custom_call", output_to_operand_aliasing={{0}: (8, {}), {1}: (9, {})} | custom-call | flops 5242880 | bytes 6815744 | tf_op jit(solution)/shard_map/inner_step/pallas_call | solution.py:301
  100.6 3.6 %collective-permute-start.28 = (bf16[2048,128]{1,0:T(8,128)(2,1)S(1)}, bf16[2048,128]{1,0:T(8,128)(2,1)S(1)}, u32[]{:S(2)}, u32[]{:S(2)}) collective-permute-start(bf16[2048,128]{1,0:T(8,128)(2,1)S(1)} %get-tuple-element.112.refs_0_), channel_id=1, source_target_pairs={{0,64},{64,0},{1,65},{65,1},{2,66},{66,2},{3,67},{67,3},{4,68},{68... | collective-permute-start | bytes 1572872 | tf_op jit(solution)/shard_map/ppermute | solution.py:68
  104.3 1.9 %inner_step.5 = (bf16[1,128,2048]{2,1,0:T(8,128)(2,1)}, bf16[1,128,2048]{2,1,0:T(8,128)(2,1)}, bf16[128,2048]{1,0:T(8,128)(2,1)S(1)}) custom-call(f32[128,2048]{1,0:T(8,128)S(1)} %get-tuple-element.129.refs_0_, bf16[2,128,2048]{2,1,0:T(8,128)(2,1)S(1)} %collective-permute-done.30.core_ref.refs_1_, bf16[64,2048]{1,0:T(8,128)(2,1)S(1)} %collective-permute-done.31.refs_2_, ...), custom_call_target="tpu_custom_call" | custom-call | flops 5242880 | bytes 6815744 | tf_op jit(solution)/shard_map/inner_step/pallas_call | solution.py:301
  106.2 3.6 %collective-permute-start.33 = (bf16[128,2048]{1,0:T(8,128)(2,1)S(1)}, bf16[128,2048]{1,0:T(8,128)(2,1)S(1)}, u32[]{:S(2)}, u32[]{:S(2)}) collective-permute-start(bf16[128,2048]{1,0:T(8,128)(2,1)S(1)} %get-tuple-element.134.refs_0_), channel_id=1, source_target_pairs={{0,64},{64,0},{1,65},{65,1},{2,66},{66,2},{3,67},{67,3},{4,68},{68... | collective-permute-start | bytes 1572872 | tf_op jit(solution)/shard_map/ppermute | solution.py:68
  109.8 1.4 %outer_step.3 = (f32[2,2048,128]{2,1,0:T(8,128)}, f32[2,2048,128]{2,1,0:T(8,128)}) custom-call(bf16[2048,128]{1,0:T(8,128)(2,1)S(1)} %get-tuple-element.113.refs_0_, bf16[2048,128]{1,0:T(8,128)(2,1)S(1)} %collective-permute-done.29.refs_1_, f32[2,2048,128]{2,1,0:T(8,128)S(1)} %copy-done, f32[2,2048,128]{2,1,0:T(8,128)S(1)} %copy-done.3), custom_call_target="tpu_custom_call" | custom-call | flops 2097152 | bytes 5242880 | tf_op jit(solution)/shard_map/outer_step/pallas_call | solution.py:340
  111.2 8.9 %collective-permute-done.28.refs_1_ = bf16[2048,128]{1,0:T(8,128)(2,1)S(1)} collective-permute-done((bf16[2048,128]{1,0:T(8,128)(2,1)S(1)}, bf16[2048,128]{1,0:T(8,128)(2,1)S(1)}, u32[]{:S(2)}, u32[]{:S(2)}) %collective-permute-start.28) | collective-permute-done | bytes 524320 | tf_op jit(solution)/shard_map/ppermute | solution.py:68
  120.1 1.4 %outer_step.4 = (f32[2,2048,128]{2,1,0:T(8,128)}, f32[2,2048,128]{2,1,0:T(8,128)}) custom-call(bf16[2048,128]{1,0:T(8,128)(2,1)S(1)} %get-tuple-element.112.refs_0_, bf16[2048,128]{1,0:T(8,128)(2,1)S(1)} %collective-permute-done.28.refs_1_, f32[2,2048,128]{2,1,0:T(8,128)S(1)} %copy-done, ...), custom_call_target="tpu_custom_call", output_to_operand_aliasing={{0}: (4, {}), {1}: (5, {})} | custom-call | flops 2097152 | bytes 5242880 | tf_op jit(solution)/shard_map/outer_step/pallas_call | solution.py:340
  121.5 9.8 %collective-permute-done.33.refs_1_ = bf16[128,2048]{1,0:T(8,128)(2,1)S(1)} collective-permute-done((bf16[128,2048]{1,0:T(8,128)(2,1)S(1)}, bf16[128,2048]{1,0:T(8,128)(2,1)S(1)}, u32[]{:S(2)}, u32[]{:S(2)}) %collective-permute-start.33) | collective-permute-done | bytes 524320 | tf_op jit(solution)/shard_map/ppermute | solution.py:68
  131.4 1.4 %outer_step.5 = (f32[128,2048]{1,0:T(8,128)}, f32[128,2048]{1,0:T(8,128)}) custom-call(bf16[128,2048]{1,0:T(8,128)(2,1)S(1)} %get-tuple-element.134.refs_0_, bf16[128,2048]{1,0:T(8,128)(2,1)S(1)} %collective-permute-done.33.refs_1_, f32[128,2048]{1,0:T(8,128)S(1)} %copy-done.7, f32[128,2048]{1,0:T(8,128)S(1)} %copy-done.10), custom_call_target="tpu_custom_call" | custom-call | flops 2097152 | bytes 5242880 | tf_op jit(solution)/shard_map/outer_step/pallas_call | solution.py:340
  (69 shorter events, 3.7 us)
Async XLA Ops:
  2.5 15.0 %collective-permute-start.2 = (bf16[2,64,2048]{2,1,0:T(8,128)(2,1)}, bf16[2,64,2048]{2,1,0:T(8,128)(2,1)S(1)}, u32[]{:S(2)}, u32[]{:S(2)}) collective-permute-start(bf16[2,64,2048]{2,1,0:T(8,128)(2,1)} %own_rows.1.refs_0_.refs_1_), channel_id=1, source_target_pairs={{0,32},{1,33},{2,34},{3,35},{4,36},{5,37},{6,38},{7,39},{8,40},{9,... | collective-permute-start | bytes 1572872 | tf_op jit(solution)/shard_map/ppermute | solution.py:34
  6.1 14.8 %collective-permute-start.12 = (bf16[2,64,2048]{2,1,0:T(8,128)(2,1)}, bf16[2,64,2048]{2,1,0:T(8,128)(2,1)S(1)}, u32[]{:S(2)}, u32[]{:S(2)}) collective-permute-start(bf16[2,64,2048]{2,1,0:T(8,128)(2,1)} %own_rows.1.refs_0_.refs_1_), channel_id=1, source_target_pairs={{0,8},{1,9},{2,10},{3,11},{4,12},{5,13},{6,14},{7,15},{8,0},{9,1},... | collective-permute-start | bytes 1572872 | tf_op jit(solution)/shard_map/ppermute | solution.py:34
  7.8 14.8 %collective-permute-start.8 = (bf16[2,64,2048]{2,1,0:T(8,128)(2,1)}, bf16[2,64,2048]{2,1,0:T(8,128)(2,1)S(1)}, u32[]{:S(2)}, u32[]{:S(2)}) collective-permute-start(bf16[2,64,2048]{2,1,0:T(8,128)(2,1)} %own_rows.1.refs_0_.refs_1_), channel_id=1, source_target_pairs={{0,6},{1,7},{2,0},{3,1},{4,2},{5,3},{6,4},{7,5},{8,14},{9,15},{10,... | collective-permute-start | bytes 1572872 | tf_op jit(solution)/shard_map/ppermute | solution.py:34
  10.5 14.8 %collective-permute-start.7 = (bf16[2,64,2048]{2,1,0:T(8,128)(2,1)}, bf16[2,64,2048]{2,1,0:T(8,128)(2,1)S(1)}, u32[]{:S(2)}, u32[]{:S(2)}) collective-permute-start(bf16[2,64,2048]{2,1,0:T(8,128)(2,1)} %own_rows.1.refs_0_.refs_1_), channel_id=1, source_target_pairs={{0,2},{1,3},{2,4},{3,5},{4,6},{5,7},{6,0},{7,1},{8,10},{9,11},{10,... | collective-permute-start | bytes 1572872 | tf_op jit(solution)/shard_map/ppermute | solution.py:34
  10.5 1.6 %copy-start.1 = (f32[1,2,2048,128]{3,2,1,0:T(8,128)S(1)}, f32[1,2,2048,128]{3,2,1,0:T(8,128)}, u32[]{:S(2)}) copy-start(f32[1,2,2048,128]{3,2,1,0:T(8,128)} %refs_4_.4) | copy-start | bytes 6291460
  12.1 1.2 copy-start.5
  17.5 20.0 %collective-permute-start.3 = (bf16[3,64,2048]{2,1,0:T(8,128)(2,1)S(1)}, bf16[3,64,2048]{2,1,0:T(8,128)(2,1)S(1)}, u32[]{:S(2)}, u32[]{:S(2)}) collective-permute-start(bf16[3,64,2048]{2,1,0:T(8,128)(2,1)S(1)} %get-tuple-element.77.refs_2_), channel_id=1, source_target_pairs={{0,16},{1,17},{2,18},{3,19},{4,20},{5,21},{6,22},{7,23},{8,24},{9,... | collective-permute-start | bytes 2359304 | tf_op jit(solution)/shard_map/ppermute | solution.py:34
  19.1 18.5 %collective-permute-start.4 = (bf16[3,64,2048]{2,1,0:T(8,128)(2,1)S(1)}, bf16[3,64,2048]{2,1,0:T(8,128)(2,1)S(1)}, u32[]{:S(2)}, u32[]{:S(2)}) collective-permute-start(bf16[3,64,2048]{2,1,0:T(8,128)(2,1)S(1)} %get-tuple-element.78.refs_3_), channel_id=1, source_target_pairs={{0,48},{1,49},{2,50},{3,51},{4,52},{5,53},{6,54},{7,55},{8,56},{9,... | collective-permute-start | bytes 2359304 | tf_op jit(solution)/shard_map/ppermute | solution.py:34
  20.9 11.7 %collective-permute-start.13 = (bf16[2,64,2048]{2,1,0:T(8,128)(2,1)S(1)}, bf16[2,64,2048]{2,1,0:T(8,128)(2,1)S(1)}, u32[]{:S(2)}, u32[]{:S(2)}) collective-permute-start(bf16[2,64,2048]{2,1,0:T(8,128)(2,1)S(1)} %collective-permute-done.2.refs_0_.refs_1_), channel_id=1, source_target_pairs={{0,8},{1,9},{2,10},{3,11},{4,12},{5,13},{6,14},{7,15},{8,0},{9,1},... | collective-permute-start | bytes 1572872 | tf_op jit(solution)/shard_map/ppermute | solution.py:34
  22.6 11.6 %collective-permute-start.11 = (bf16[2,64,2048]{2,1,0:T(8,128)(2,1)S(1)}, bf16[2,64,2048]{2,1,0:T(8,128)(2,1)S(1)}, u32[]{:S(2)}, u32[]{:S(2)}) collective-permute-start(bf16[2,64,2048]{2,1,0:T(8,128)(2,1)S(1)} %collective-permute-done.2.refs_0_.refs_1_), channel_id=1, source_target_pairs={{0,6},{1,7},{2,0},{3,1},{4,2},{5,3},{6,4},{7,5},{8,14},{9,15},{10,... | collective-permute-start | bytes 1572872 | tf_op jit(solution)/shard_map/ppermute | solution.py:34
  25.3 12.2 %collective-permute-start.9 = (bf16[2,64,2048]{2,1,0:T(8,128)(2,1)S(1)}, bf16[2,64,2048]{2,1,0:T(8,128)(2,1)S(1)}, u32[]{:S(2)}, u32[]{:S(2)}) collective-permute-start(bf16[2,64,2048]{2,1,0:T(8,128)(2,1)S(1)} %collective-permute-done.7.refs_2_.refs_3_), channel_id=1, source_target_pairs={{0,2},{1,3},{2,4},{3,5},{4,6},{5,7},{6,0},{7,1},{8,10},{9,11},{10,... | collective-permute-start | bytes 1572872 | tf_op jit(solution)/shard_map/ppermute | solution.py:34
  32.6 21.8 %collective-permute-start.15 = (bf16[4,64,2048]{2,1,0:T(8,128)(2,1)S(1)}, bf16[4,64,2048]{2,1,0:T(8,128)(2,1)S(1)}, u32[]{:S(2)}, u32[]{:S(2)}) collective-permute-start(bf16[4,64,2048]{2,1,0:T(8,128)(2,1)S(1)} %pad_maximum_fusion), channel_id=1, source_target_pairs={{0,8},{1,9},{2,10},{3,11},{4,12},{5,13},{6,14},{7,15},{8,0},{9,1},... | collective-permute-start | bytes 3145736 | tf_op jit(solution)/shard_map/ppermute | solution.py:34
  34.1 11.3 %collective-permute-start.17 = (bf16[2,64,2048]{2,1,0:T(8,128)(2,1)S(1)}, bf16[2,64,2048]{2,1,0:T(8,128)(2,1)S(1)}, u32[]{:S(2)}, u32[]{:S(2)}) collective-permute-start(bf16[2,64,2048]{2,1,0:T(8,128)(2,1)S(1)} %collective-permute-done.13.refs_2_.refs_3_), channel_id=1, source_target_pairs={{0,6},{1,7},{2,0},{3,1},{4,2},{5,3},{6,4},{7,5},{8,14},{9,15},{10,... | collective-permute-start | bytes 1572872 | tf_op jit(solution)/shard_map/ppermute | solution.py:34
  37.5 12.1 %collective-permute-start.14 = (bf16[2,64,2048]{2,1,0:T(8,128)(2,1)S(1)}, bf16[2,64,2048]{2,1,0:T(8,128)(2,1)S(1)}, u32[]{:S(2)}, u32[]{:S(2)}) collective-permute-start(bf16[2,64,2048]{2,1,0:T(8,128)(2,1)S(1)} %collective-permute-done.13.refs_2_.refs_3_), channel_id=1, source_target_pairs={{0,2},{1,3},{2,4},{3,5},{4,6},{5,7},{6,0},{7,1},{8,10},{9,11},{10,... | collective-permute-start | bytes 1572872 | tf_op jit(solution)/shard_map/ppermute | solution.py:34
  37.6 15.5 %collective-permute-start.10 = (bf16[2,64,2048]{2,1,0:T(8,128)(2,1)S(1)}, bf16[2,64,2048]{2,1,0:T(8,128)(2,1)S(1)}, u32[]{:S(2)}, u32[]{:S(2)}) collective-permute-start(bf16[2,64,2048]{2,1,0:T(8,128)(2,1)S(1)} %collective-permute-done.7.refs_2_.refs_3_), channel_id=1, source_target_pairs={{0,32},{1,33},{2,34},{3,35},{4,36},{5,37},{6,38},{7,39},{8,40},{9,... | collective-permute-start | bytes 1572872 | tf_op jit(solution)/shard_map/ppermute | solution.py:34
  38.8 16.9 %collective-permute-start = (bf16[3,64,2048]{2,1,0:T(8,128)(2,1)S(1)}, bf16[3,64,2048]{2,1,0:T(8,128)(2,1)S(1)}, u32[]{:S(2)}, u32[]{:S(2)}) collective-permute-start(bf16[3,64,2048]{2,1,0:T(8,128)(2,1)S(1)} %get-tuple-element.77.refs_2_), channel_id=1, source_target_pairs={{0,1},{1,0},{2,3},{3,2},{4,5},{5,4},{6,7},{7,6},{8,9},{9,8},{10,11... | collective-permute-start | bytes 2359304 | tf_op jit(solution)/shard_map/ppermute | solution.py:34
  45.5 13.0 %collective-permute-start.1 = (bf16[3,64,2048]{2,1,0:T(8,128)(2,1)S(1)}, bf16[3,64,2048]{2,1,0:T(8,128)(2,1)S(1)}, u32[]{:S(2)}, u32[]{:S(2)}) collective-permute-start(bf16[3,64,2048]{2,1,0:T(8,128)(2,1)S(1)} %get-tuple-element.78.refs_3_), channel_id=1, source_target_pairs={{0,1},{1,0},{2,3},{3,2},{4,5},{5,4},{6,7},{7,6},{8,9},{9,8},{10,11... | collective-permute-start | bytes 2359304 | tf_op jit(solution)/shard_map/ppermute | solution.py:34
  49.7 8.8 %collective-permute-start.5 = (bf16[3,64,2048]{2,1,0:T(8,128)(2,1)S(1)}, bf16[3,64,2048]{2,1,0:T(8,128)(2,1)S(1)}, u32[]{:S(2)}, u32[]{:S(2)}) collective-permute-start(bf16[3,64,2048]{2,1,0:T(8,128)(2,1)S(1)} %collective-permute-done.3.refs_4_), channel_id=1, source_target_pairs={{0,1},{1,0},{2,3},{3,2},{4,5},{5,4},{6,7},{7,6},{8,9},{9,8},{10,11... | collective-permute-start | bytes 2359304 | tf_op jit(solution)/shard_map/ppermute | solution.py:34
  53.1 5.4 %collective-permute-start.6 = (bf16[3,64,2048]{2,1,0:T(8,128)(2,1)S(1)}, bf16[3,64,2048]{2,1,0:T(8,128)(2,1)S(1)}, u32[]{:S(2)}, u32[]{:S(2)}) collective-permute-start(bf16[3,64,2048]{2,1,0:T(8,128)(2,1)S(1)} %collective-permute-done.4.refs_5_), channel_id=1, source_target_pairs={{0,1},{1,0},{2,3},{3,2},{4,5},{5,4},{6,7},{7,6},{8,9},{9,8},{10,11... | collective-permute-start | bytes 2359304 | tf_op jit(solution)/shard_map/ppermute | solution.py:34
  54.4 14.7 %collective-permute-start.16 = (bf16[2,64,2048]{2,1,0:T(8,128)(2,1)S(1)}, bf16[2,64,2048]{2,1,0:T(8,128)(2,1)S(1)}, u32[]{:S(2)}, u32[]{:S(2)}) collective-permute-start(bf16[2,64,2048]{2,1,0:T(8,128)(2,1)S(1)} %collective-permute-done.9.refs_6_.refs_7_), channel_id=1, source_target_pairs={{0,32},{1,33},{2,34},{3,35},{4,36},{5,37},{6,38},{7,39},{8,40},{9,... | collective-permute-start | bytes 1572872 | tf_op jit(solution)/shard_map/ppermute | solution.py:34
  55.6 12.0 %collective-permute-start.19 = (bf16[1,64,2048]{2,1,0:T(8,128)(2,1)S(1)}, bf16[1,64,2048]{2,1,0:T(8,128)(2,1)S(1)}, u32[]{:S(2)}, u32[]{:S(2)}) collective-permute-start(bf16[1,64,2048]{2,1,0:T(8,128)(2,1)S(1)} %slice.17), channel_id=1, source_target_pairs={{0,6},{1,7},{2,0},{3,1},{4,2},{5,3},{6,4},{7,5},{8,14},{9,15},{10,... | collective-permute-start | bytes 786440 | tf_op jit(solution)/shard_map/ppermute | solution.py:34
  58.5 9.2 %collective-permute-start.18 = (bf16[1,64,2048]{2,1,0:T(8,128)(2,1)S(1)}, bf16[1,64,2048]{2,1,0:T(8,128)(2,1)S(1)}, u32[]{:S(2)}, u32[]{:S(2)}) collective-permute-start(bf16[1,64,2048]{2,1,0:T(8,128)(2,1)S(1)} %slice.16), channel_id=1, source_target_pairs={{0,2},{1,3},{2,4},{3,5},{4,6},{5,7},{6,0},{7,1},{8,10},{9,11},{10,... | collective-permute-start | bytes 786440 | tf_op jit(solution)/shard_map/ppermute | solution.py:34
  58.5 10.6 %collective-permute-start.20 = (bf16[1,64,2048]{2,1,0:T(8,128)(2,1)S(1)}, bf16[1,64,2048]{2,1,0:T(8,128)(2,1)S(1)}, u32[]{:S(2)}, u32[]{:S(2)}) collective-permute-start(bf16[1,64,2048]{2,1,0:T(8,128)(2,1)S(1)} %get-tuple-element.143), channel_id=1, source_target_pairs={{0,2},{1,3},{2,4},{3,5},{4,6},{5,7},{6,0},{7,1},{8,10},{9,11},{10,... | collective-permute-start | bytes 786440 | tf_op jit(solution)/shard_map/ppermute | solution.py:34
  58.6 10.5 %collective-permute-start.21 = (bf16[1,64,2048]{2,1,0:T(8,128)(2,1)S(1)}, bf16[1,64,2048]{2,1,0:T(8,128)(2,1)S(1)}, u32[]{:S(2)}, u32[]{:S(2)}) collective-permute-start(bf16[1,64,2048]{2,1,0:T(8,128)(2,1)S(1)} %get-tuple-element.142), channel_id=1, source_target_pairs={{0,6},{1,7},{2,0},{3,1},{4,2},{5,3},{6,4},{7,5},{8,14},{9,15},{10,... | collective-permute-start | bytes 786440 | tf_op jit(solution)/shard_map/ppermute | solution.py:34
  63.7 1.9 %copy-start.4 = (bf16[2,64,2048]{2,1,0:T(8,128)(2,1)S(1)}, bf16[2,64,2048]{2,1,0:T(8,128)(2,1)}, u32[]{:S(2)}) copy-start(bf16[2,64,2048]{2,1,0:T(8,128)(2,1)} %own_rows.1.refs_0_.refs_1_) | copy-start | bytes 1572868
  73.3 7.5 %collective-permute-start.25 = (bf16[2,128,2048]{2,1,0:T(8,128)(2,1)S(1)}, bf16[2,128,2048]{2,1,0:T(8,128)(2,1)S(1)}, u32[]{:S(2)}, u32[]{:S(2)}) collective-permute-start(bf16[2,128,2048]{2,1,0:T(8,128)(2,1)S(1)} %get-tuple-element.106), channel_id=1, source_target_pairs={{0,1},{1,0},{2,3},{3,2},{4,5},{5,4},{6,7},{7,6},{8,9},{9,8},{10,11... | collective-permute-start | bytes 3145736 | tf_op jit(solution)/shard_map/ppermute | solution.py:34
  80.7 5.2 %collective-permute-start.22 = (bf16[2,128,2048]{2,1,0:T(8,128)(2,1)S(1)}, bf16[2,128,2048]{2,1,0:T(8,128)(2,1)S(1)}, u32[]{:S(2)}, u32[]{:S(2)}) collective-permute-start(bf16[2,128,2048]{2,1,0:T(8,128)(2,1)S(1)} %get-tuple-element.97), channel_id=1, source_target_pairs={{0,1},{1,0},{2,3},{3,2},{4,5},{5,4},{6,7},{7,6},{8,9},{9,8},{10,11... | collective-permute-start | bytes 3145736 | tf_op jit(solution)/shard_map/ppermute | solution.py:34
  83.1 4.5 %collective-permute-start.30 = (bf16[2,128,2048]{2,1,0:T(8,128)(2,1)S(1)}, bf16[2,128,2048]{2,1,0:T(8,128)(2,1)S(1)}, u32[]{:S(2)}, u32[]{:S(2)}) collective-permute-start(bf16[2,128,2048]{2,1,0:T(8,128)(2,1)S(1)} %get-tuple-element.130), channel_id=1, source_target_pairs={{0,1},{1,0},{2,3},{3,2},{4,5},{5,4},{6,7},{7,6},{8,9},{9,8},{10,11... | collective-permute-start | bytes 3145736 | tf_op jit(solution)/shard_map/ppermute | solution.py:34
  83.7 9.6 %copy-start.8 = (bf16[1,2,2048,128]{3,2,1,0:T(8,128)(2,1)S(1)}, bf16[1,2,2048,128]{3,2,1,0:T(8,128)(2,1)}, u32[]{:S(2)}) copy-start(bf16[1,2,2048,128]{3,2,1,0:T(8,128)(2,1)} %refs_5_.4) | copy-start | bytes 3145732
  83.7 9.6 %copy-start.9 = (bf16[1,2,2048,128]{3,2,1,0:T(8,128)(2,1)S(1)}, bf16[1,2,2048,128]{3,2,1,0:T(8,128)(2,1)}, u32[]{:S(2)}) copy-start(bf16[1,2,2048,128]{3,2,1,0:T(8,128)(2,1)} %refs_6_.4) | copy-start | bytes 3145732
  83.8 8.0 %collective-permute-start.26 = (bf16[64,2048]{1,0:T(8,128)(2,1)S(1)}, bf16[64,2048]{1,0:T(8,128)(2,1)S(1)}, u32[]{:S(2)}, u32[]{:S(2)}) collective-permute-start(bf16[64,2048]{1,0:T(8,128)(2,1)S(1)} %get-tuple-element.108), channel_id=1, source_target_pairs={{0,16},{1,17},{2,18},{3,19},{4,20},{5,21},{6,22},{7,23},{8,24},{9,... | collective-permute-start | bytes 786440 | tf_op jit(solution)/shard_map/ppermute | solution.py:34
  84.2 9.1 %collective-permute-start.27 = (bf16[64,2048]{1,0:T(8,128)(2,1)S(1)}, bf16[64,2048]{1,0:T(8,128)(2,1)S(1)}, u32[]{:S(2)}, u32[]{:S(2)}) collective-permute-start(bf16[64,2048]{1,0:T(8,128)(2,1)S(1)} %get-tuple-element.109), channel_id=1, source_target_pairs={{0,48},{1,49},{2,50},{3,51},{4,52},{5,53},{6,54},{7,55},{8,56},{9,... | collective-permute-start | bytes 786440 | tf_op jit(solution)/shard_map/ppermute | solution.py:34
  85.9 7.4 %copy-start = (f32[2,2048,128]{2,1,0:T(8,128)S(1)}, f32[2,2048,128]{2,1,0:T(8,128)}, u32[]{:S(2)}) copy-start(f32[2,2048,128]{2,1,0:T(8,128)} %refs_2_.4) | copy-start | bytes 6291460
  85.9 7.4 %copy-start.2 = (f32[1,2,2048,128]{3,2,1,0:T(8,128)S(1)}, f32[1,2,2048,128]{3,2,1,0:T(8,128)}, u32[]{:S(2)}) copy-start(f32[1,2,2048,128]{3,2,1,0:T(8,128)} %refs_4_.4) | copy-start | bytes 6291460
  86.0 12.5 %collective-permute-start.23 = (bf16[64,2048]{1,0:T(8,128)(2,1)S(1)}, bf16[64,2048]{1,0:T(8,128)(2,1)S(1)}, u32[]{:S(2)}, u32[]{:S(2)}) collective-permute-start(bf16[64,2048]{1,0:T(8,128)(2,1)S(1)} %get-tuple-element.99), channel_id=1, source_target_pairs={{0,16},{1,17},{2,18},{3,19},{4,20},{5,21},{6,22},{7,23},{8,24},{9,... | collective-permute-start | bytes 786440 | tf_op jit(solution)/shard_map/ppermute | solution.py:34
  86.4 12.2 %collective-permute-start.24 = (bf16[64,2048]{1,0:T(8,128)(2,1)S(1)}, bf16[64,2048]{1,0:T(8,128)(2,1)S(1)}, u32[]{:S(2)}, u32[]{:S(2)}) collective-permute-start(bf16[64,2048]{1,0:T(8,128)(2,1)S(1)} %get-tuple-element.100), channel_id=1, source_target_pairs={{0,48},{1,49},{2,50},{3,51},{4,52},{5,53},{6,54},{7,55},{8,56},{9,... | collective-permute-start | bytes 786440 | tf_op jit(solution)/shard_map/ppermute | solution.py:34
  87.7 16.5 %collective-permute-start.31 = (bf16[64,2048]{1,0:T(8,128)(2,1)S(1)}, bf16[64,2048]{1,0:T(8,128)(2,1)S(1)}, u32[]{:S(2)}, u32[]{:S(2)}) collective-permute-start(bf16[64,2048]{1,0:T(8,128)(2,1)S(1)} %get-tuple-element.132), channel_id=1, source_target_pairs={{0,16},{1,17},{2,18},{3,19},{4,20},{5,21},{6,22},{7,23},{8,24},{9,... | collective-permute-start | bytes 786440 | tf_op jit(solution)/shard_map/ppermute | solution.py:34
  91.8 12.4 %collective-permute-start.32 = (bf16[64,2048]{1,0:T(8,128)(2,1)S(1)}, bf16[64,2048]{1,0:T(8,128)(2,1)S(1)}, u32[]{:S(2)}, u32[]{:S(2)}) collective-permute-start(bf16[64,2048]{1,0:T(8,128)(2,1)S(1)} %get-tuple-element.133), channel_id=1, source_target_pairs={{0,48},{1,49},{2,50},{3,51},{4,52},{5,53},{6,54},{7,55},{8,56},{9,... | collective-permute-start | bytes 786440 | tf_op jit(solution)/shard_map/ppermute | solution.py:34
  95.3 14.5 %collective-permute-start.29 = (bf16[2048,128]{1,0:T(8,128)(2,1)S(1)}, bf16[2048,128]{1,0:T(8,128)(2,1)S(1)}, u32[]{:S(2)}, u32[]{:S(2)}) collective-permute-start(bf16[2048,128]{1,0:T(8,128)(2,1)S(1)} %get-tuple-element.113.refs_0_), channel_id=1, source_target_pairs={{0,64},{64,0},{1,65},{65,1},{2,66},{66,2},{3,67},{67,3},{4,68},{68... | collective-permute-start | bytes 1572872 | tf_op jit(solution)/shard_map/ppermute | solution.py:68
  98.6 5.6 %copy-start.6 = (f32[1,128,2048]{2,1,0:T(8,128)S(1)}, f32[1,128,2048]{2,1,0:T(8,128)}, u32[]{:S(2)}) copy-start(f32[1,128,2048]{2,1,0:T(8,128)} %refs_4_.5) | copy-start | bytes 3145732
  98.6 5.6 %copy-start.7 = (f32[128,2048]{1,0:T(8,128)S(1)}, f32[128,2048]{1,0:T(8,128)}, u32[]{:S(2)}) copy-start(f32[128,2048]{1,0:T(8,128)} %refs_2_.5) | copy-start | bytes 3145732
  98.6 5.6 %copy-start.11 = (bf16[1,128,2048]{2,1,0:T(8,128)(2,1)S(1)}, bf16[1,128,2048]{2,1,0:T(8,128)(2,1)}, u32[]{:S(2)}) copy-start(bf16[1,128,2048]{2,1,0:T(8,128)(2,1)} %refs_5_.5) | copy-start | bytes 1572868
  98.6 5.6 %copy-start.12 = (bf16[1,128,2048]{2,1,0:T(8,128)(2,1)S(1)}, bf16[1,128,2048]{2,1,0:T(8,128)(2,1)}, u32[]{:S(2)}) copy-start(bf16[1,128,2048]{2,1,0:T(8,128)(2,1)} %refs_6_.5) | copy-start | bytes 1572868
  100.6 19.6 %collective-permute-start.28 = (bf16[2048,128]{1,0:T(8,128)(2,1)S(1)}, bf16[2048,128]{1,0:T(8,128)(2,1)S(1)}, u32[]{:S(2)}, u32[]{:S(2)}) collective-permute-start(bf16[2048,128]{1,0:T(8,128)(2,1)S(1)} %get-tuple-element.112.refs_0_), channel_id=1, source_target_pairs={{0,64},{64,0},{1,65},{65,1},{2,66},{66,2},{3,67},{67,3},{4,68},{68... | collective-permute-start | bytes 1572872 | tf_op jit(solution)/shard_map/ppermute | solution.py:68
  104.2 5.5 %copy-start.3 = (f32[2,2048,128]{2,1,0:T(8,128)S(1)}, f32[2,2048,128]{2,1,0:T(8,128)}, u32[]{:S(2)}) copy-start(f32[2,2048,128]{2,1,0:T(8,128)} %refs_3_.4) | copy-start | bytes 6291460
  106.2 25.2 %collective-permute-start.33 = (bf16[128,2048]{1,0:T(8,128)(2,1)S(1)}, bf16[128,2048]{1,0:T(8,128)(2,1)S(1)}, u32[]{:S(2)}, u32[]{:S(2)}) collective-permute-start(bf16[128,2048]{1,0:T(8,128)(2,1)S(1)} %get-tuple-element.134.refs_0_), channel_id=1, source_target_pairs={{0,64},{64,0},{1,65},{65,1},{2,66},{66,2},{3,67},{67,3},{4,68},{68... | collective-permute-start | bytes 1572872 | tf_op jit(solution)/shard_map/ppermute | solution.py:68
  120.1 11.2 %copy-start.10 = (f32[128,2048]{1,0:T(8,128)S(1)}, f32[128,2048]{1,0:T(8,128)}, u32[]{:S(2)}) copy-start(f32[128,2048]{1,0:T(8,128)} %refs_3_.5) | copy-start | bytes 3145732
